TPU v7x, 32 devices: a whole 2x2x4 slice. The times are simulated.
32 devices in a mesh: section: 4 (over z), expert: 8 (over y, x, core).
Axes of the slice: x: 2, y: 2, z: 4, core: 2. Of those that a mesh axis runs over, the one named last changes fastest.
Arguments:
- tokens_in: bfloat16 [4, 128, 4096], P('section', 'expert'), may hold values from -6 to 6
- out_grad: bfloat16 [4, 128, 4096], P('section', 'expert'), may hold values from -6 to 6
- expert_ids: int32 [4, 128, 2], P('section', 'expert'), may hold values from 0 to 7, all different within a row; in each aligned block of 16 rows (0 to 15, 16 to 31, ..., all dimensions but the last counted through in order) at most 8 rows name the same one
- gate_weights: bfloat16 [4, 128, 2], P('section', 'expert'), may hold values from 0.099609375 to 1
- w_gate: bfloat16 [4, 6144, 4096], P('section', 'expert'), may hold values from -0.09375 to 0.09375
- w_up: bfloat16 [4, 6144, 4096], P('section', 'expert'), may hold values from -0.09375 to 0.09375
- w_down: bfloat16 [4, 6144, 4096], P('section', 'expert'), may hold values from -0.09375 to 0.09375
Outputs:
- passed_grad: bfloat16 [4, 128, 4096], P('section', 'expert')
- route_grad: float32 [4, 128, 2], P('section', 'expert')
Inputs may be any that keep to these rules, and one draw needn't show every extreme that they name: `expert_ids`: the 2 experts of a token differ. Among the 16 tokens of one device no expert is named by more than 8 tokens, and in some device's rows some expert is named by exactly 8.
All inputs are finite; a program needn't handle non-finite values.
Results may differ from a plain program's by a relative error of at most 0.0057.
Values may be sent and summed in bfloat16 or wider, within the bound.
No kernel may reach another device: no remote copies, remote signals or barrier semaphores. Data moves between devices by JAX's collectives and lax.ppermute only.
A program may use at most 64 MiB of HBM per device.

v0:
```python
import jax
import jax.numpy as jnp
from jax import lax
from jax.sharding import PartitionSpec as P

EXPERTS = 8


def shifted(array, axis, by):
    peers = lax.axis_size(axis)
    return lax.ppermute(array, axis, [(i, (i + by) % peers) for i in range(peers)])


def expert_terms(rows_x, rows_dy, rows_g, gate_mat, up_mat, down_mat):
    dims = (((1,), (1,)), ((), ()))
    gate_pre = lax.dot_general(rows_x, gate_mat, dims, preferred_element_type=jnp.float32)
    up_pre = lax.dot_general(rows_x, up_mat, dims, preferred_element_type=jnp.float32)
    hidden_grad = lax.dot_general(rows_dy, down_mat, dims, preferred_element_type=jnp.float32)
    sigmoid_val = jax.nn.sigmoid(gate_pre)
    activated = gate_pre * sigmoid_val
    slope = sigmoid_val * (1.0 + gate_pre * (1.0 - sigmoid_val))
    scores = jnp.sum(activated * up_pre * hidden_grad, axis=1)
    scaled = hidden_grad * rows_g[:, None]
    grad_gate = (scaled * up_pre * slope).astype(jnp.bfloat16)
    grad_up = (scaled * activated).astype(jnp.bfloat16)
    partial_value = jnp.dot(grad_gate, gate_mat, preferred_element_type=jnp.float32)
    partial_value = partial_value + jnp.dot(grad_up, up_mat, preferred_element_type=jnp.float32)
    return (partial_value.astype(jnp.bfloat16), scores)


def on_device(tokens_in, out_grad, expert_ids, gate_weights, w_gate, w_up, w_down):
    inputs = tokens_in[0]
    upstream = out_grad[0]
    routes = expert_ids[0]
    gate_vals = gate_weights[0]
    gate_mat = w_gate[0]
    up_mat = w_up[0]
    down_mat = w_down[0]
    tok_rows = inputs.shape[0]
    devices = lax.axis_size("expert")
    group_size = devices // EXPERTS
    route_hit = (routes[:, :, None] == jnp.arange(EXPERTS, dtype=jnp.int32)[None, None, :]).astype(
        jnp.float32
    )
    table = jnp.sum(gate_vals.astype(jnp.float32)[:, :, None] * route_hit, axis=1).astype(
        jnp.bfloat16
    )
    slot_count = tok_rows // 2
    routed = jnp.sum(route_hit, axis=1)
    earlier = (jnp.arange(tok_rows)[:, None] > jnp.arange(tok_rows)[None, :]).astype(jnp.float32)
    slot_of = jnp.dot(earlier, routed, preferred_element_type=jnp.float32)
    slot_hit = (
        slot_of[:, :, None] == jnp.arange(slot_count, dtype=jnp.float32)[None, None, :]
    ).astype(jnp.float32)
    placer = routed[:, :, None] * slot_hit
    placer_b = placer.astype(jnp.bfloat16)
    send_x = jnp.einsum("tes,td->esd", placer_b, inputs, preferred_element_type=jnp.float32).astype(
        jnp.bfloat16
    )
    send_dy = jnp.einsum(
        "tes,td->esd", placer_b, upstream, preferred_element_type=jnp.float32
    ).astype(jnp.bfloat16)
    send_g = jnp.einsum("tes,te->es", placer_b, table, preferred_element_type=jnp.float32).astype(
        jnp.bfloat16
    )
    send_x = jnp.repeat(send_x, group_size, axis=0)
    send_dy = jnp.repeat(send_dy, group_size, axis=0)
    send_g = jnp.repeat(send_g, group_size, axis=0)
    recv_x = lax.all_to_all(send_x, "expert", split_axis=0, concat_axis=0, tiled=True)
    recv_dy = lax.all_to_all(send_dy, "expert", split_axis=0, concat_axis=0, tiled=True)
    recv_g = lax.all_to_all(send_g, "expert", split_axis=0, concat_axis=0, tiled=True)
    sources = recv_x.shape[0]
    slots_here = recv_x.shape[1]
    partial_value, scores = expert_terms(
        recv_x.reshape(sources * slots_here, recv_x.shape[2]),
        recv_dy.reshape(sources * slots_here, recv_dy.shape[2]),
        recv_g.reshape(sources * slots_here).astype(jnp.float32),
        gate_mat,
        up_mat,
        down_mat,
    )
    rows_back = lax.all_to_all(
        partial_value.reshape(sources, slots_here, partial_value.shape[1]),
        "expert",
        split_axis=0,
        concat_axis=0,
        tiled=True,
    )
    scores_back = lax.all_to_all(
        scores.reshape(sources, slots_here), "expert", split_axis=0, concat_axis=0, tiled=True
    )
    rows_back, scores_back = (rows_back, scores_back)
    placer_rep = jnp.repeat(jnp.transpose(placer_b, (1, 2, 0)), group_size, axis=0)
    input_grad = jnp.einsum(
        "jst,jsd->td", placer_rep, rows_back, preferred_element_type=jnp.float32
    )
    slice_sums = jnp.sum(scores_back.reshape(EXPERTS, group_size, slot_count), axis=1)
    score_table = jnp.einsum("tes,es->te", placer, slice_sums, precision=lax.Precision.HIGHEST)
    grads_route = jnp.sum(route_hit * score_table[:, None, :], axis=2)
    passed = shifted(input_grad.astype(jnp.bfloat16), "section", -1)
    return (passed[None], grads_route[None])


def solution(mesh):
    return jax.shard_map(
        on_device,
        mesh=mesh,
        in_specs=(
            P("section", "expert", None),
            P("section", "expert", None),
            P("section", "expert", None),
            P("section", "expert", None),
            P("section", "expert", None),
            P("section", "expert", None),
            P("section", "expert", None),
        ),
        out_specs=(P("section", "expert", None), P("section", "expert", None)),
        check_vma=False,
    )
```

profile of v0, /device:TPU:0, one launch (start us, length us, event | category | flops | bytes accessed | tf_op | source)
XLA Modules:
  0.0 77.0 jit_solution(15320089262282385496)
XLA Ops:
  0.6 0.0 copy-start
  0.6 0.7 convert_reduce_fusion
  1.4 0.1 fusion.48
  1.5 0.1 copy-done
  1.6 1.1 %convolution_convert_fusion = bf16[8,8,4096]{2,1,0:T(8,128)(2,1)} fusion(bf16[1,16,4096]{2,1,0:T(8,128)(2,1)S(1)} %copy-done, f32[16,8]{0,1:T(8,128)S(1)} %convert_reduce_fusion, f32[16,8]{0,1:T(8,128)S(1)} %fusion.48), kind=kOutput, calls=%fused_computation.11 | convolution fusion | flops 8652800 | bytes 656384 | tf_op jit(solution)/shard_map/tes,td->esd/dot_general | solution.py:57
  2.6 5.2 %all-to-all-start.2 = ((bf16[8,8,4096]{2,1,0:T(8,128)(2,1)}), bf16[8,8,4096]{2,1,0:T(8,128)(2,1)S(1)}, u32[]{:S(2)}, u32[]{:S(2)}) async-start(bf16[8,8,4096]{2,1,0:T(8,128)(2,1)} %convolution_convert_fusion), calls=%async_computation.2 | async-start | bytes 1048576 | tf_op jit(solution)/shard_map/all_to_all | solution.py:69
  7.8 2.0 %convolution_convert_fusion.1 = bf16[8,8,4096]{2,1,0:T(8,128)(2,1)} fusion(bf16[1,16,4096]{2,1,0:T(8,128)(2,1)} %param.8, f32[16,8]{0,1:T(8,128)S(1)} %convert_reduce_fusion, f32[16,8]{0,1:T(8,128)S(1)} %fusion.48), kind=kOutput, calls=%fused_computation.12 | convolution fusion | flops 8652800 | bytes 656384 | tf_op jit(solution)/shard_map/tes,td->esd/dot_general | solution.py:60
  9.8 7.8 %all-to-all-done.2 = bf16[8,8,4096]{2,1,0:T(8,128)(2,1)S(1)} async-done(((bf16[8,8,4096]{2,1,0:T(8,128)(2,1)}), bf16[8,8,4096]{2,1,0:T(8,128)(2,1)S(1)}, u32[]{:S(2)}, u32[]{:S(2)}) %all-to-all-start.2) | async-done | bytes 524320 | tf_op jit(solution)/shard_map/all_to_all | solution.py:69
  17.5 3.5 %all-to-all-start = ((bf16[8,8,4096]{2,1,0:T(8,128)(2,1)}), bf16[8,8,4096]{2,1,0:T(8,128)(2,1)S(1)}, u32[]{:S(2)}, u32[]{:S(2)}) async-start(bf16[8,8,4096]{2,1,0:T(8,128)(2,1)} %convolution_convert_fusion.1), calls=%async_computation | async-start | bytes 1048576 | tf_op jit(solution)/shard_map/all_to_all | solution.py:70
  21.0 0.0 copy-start.1
  21.1 5.0 %fusion.2 = f32[64,768]{1,0:T(8,128)S(1)} fusion(bf16[1,768,4096]{2,1,0:T(8,128)(2,1)} %param.11, bf16[8,8,4096]{2,1,0:T(8,128)(2,1)S(1)} %all-to-all-done.2), kind=kOutput, calls=%fused_computation.2 | convolution fusion | flops 402653184 | bytes 7012352 | tf_op jit(solution)/shard_map/dot_general | solution.py:16
  26.0 0.0 copy-start.3
  26.0 0.0 copy-start.2
  26.0 2.0 %fusion.6 = f32[64,768]{1,0:T(8,128)S(1)} fusion(bf16[1,768,4096]{2,1,0:T(8,128)(2,1)S(1)} %copy-done.1, bf16[8,8,4096]{2,1,0:T(8,128)(2,1)S(1)} %all-to-all-done.2), kind=kOutput, calls=%fused_computation.6 | convolution fusion | flops 402653184 | bytes 7012352 | tf_op jit(solution)/shard_map/dot_general | solution.py:17
  28.1 0.0 slice-start
  28.1 2.6 %all-to-all-done = bf16[8,8,4096]{2,1,0:T(8,128)(2,1)S(1)} async-done(((bf16[8,8,4096]{2,1,0:T(8,128)(2,1)}), bf16[8,8,4096]{2,1,0:T(8,128)(2,1)S(1)}, u32[]{:S(2)}, u32[]{:S(2)}) %all-to-all-start) | async-done | bytes 524320 | tf_op jit(solution)/shard_map/all_to_all | solution.py:70
  30.7 4.9 %multiply_reduce_fusion = (f32[64]{0:T(128)S(1)}, f32[64,768]{1,0:T(8,128)S(1)}) fusion(f32[64,768]{1,0:T(8,128)S(1)} %fusion.6, f32[64,768]{1,0:T(8,128)S(1)} %fusion.2, bf16[1,768,4096]{2,1,0:T(8,128)(2,1)} %param.13, bf16[8,8,4096]{2,1,0:T(8,128)(2,1)S(1)} %all-to-all-done), kind=kOutput, calls=%fused_computation.20 | convolution fusion | flops 402997184 | bytes 7405824 | tf_op jit(solution)/shard_map/dot_general | solution.py:18
  35.6 0.7 all_to_all.26
  36.3 3.3 %all-to-all-start.4 = ((f32[8,1,8]{2,1,0:T(1,128)}), f32[8,1,8]{2,1,0:T(1,128)S(1)}, u32[]{:S(2)}, u32[]{:S(2)}) async-start(f32[8,1,8]{2,1,0:T(1,128)} %bitcast.20), calls=%async_computation.4 | async-start | bytes 8192 | tf_op jit(solution)/shard_map/all_to_all | solution.py:89
  39.7 4.5 %all-to-all-done.4 = f32[8,1,8]{2,1,0:T(1,128)S(1)} async-done(((f32[8,1,8]{2,1,0:T(1,128)}), f32[8,1,8]{2,1,0:T(1,128)S(1)}, u32[]{:S(2)}, u32[]{:S(2)}) %all-to-all-start.4) | async-done | bytes 288 | tf_op jit(solution)/shard_map/all_to_all | solution.py:89
  44.2 0.2 fusion.29
  44.4 0.6 select_reduce_fusion
  44.9 0.1 fusion.32
  45.1 7.0 %all_to_all.33 = bf16[8,1,8]{2,1,0:T(2,128)(2,1)S(1)} all-to-all(bf16[8,1,8]{2,1,0:T(2,128)(2,1)S(1)} %copy.15), channel_id=1, replica_groups=mesh['section'=4,'expert'=8] {'expert'}, dimensions={0} | all-to-all | bytes 256 | tf_op jit(solution)/shard_map/all_to_all | solution.py:71
  52.1 0.1 reshape.47
  52.2 4.2 %fusion = f32[64,4096]{1,0:T(8,128)S(1)} fusion(bf16[1,768,4096]{2,1,0:T(8,128)(2,1)} %param.11, f32[64,768]{1,0:T(8,128)S(1)} %fusion.2, f32[64,768]{1,0:T(8,128)S(1)} %fusion.6, f32[64,768]{1,0:T(8,128)S(1)} %get-tuple-element.5, f32[64]{0:T(128)S(1)} %reshape.47), kind=kOutput, calls=%fused_computation | convolution fusion | flops 403193856 | bytes 7930112 | tf_op jit(solution)/shard_map/dot_general | solution.py:26
  56.4 1.3 %fusion.16 = bf16[8,8,4096]{2,1,0:T(8,128)(2,1)S(1)} fusion(f32[64,4096]{1,0:T(8,128)S(1)} %fusion, bf16[1,768,4096]{2,1,0:T(8,128)(2,1)S(1)} %bitcast.74, f32[64,768]{1,0:T(8,128)S(1)} %get-tuple-element.5, f32[64]{0:T(128)S(1)} %reshape.47, f32[64,768]{1,0:T(8,128)S(1)} %fusion.2), kind=kOutput, calls=%fused_computation.14 | convolution fusion | flops 403521536 | bytes 8257792 | tf_op jit(solution)/shard_map/dot_general | solution.py:27
  57.7 12.2 %all_to_all.34 = bf16[8,8,4096]{2,1,0:T(8,128)(2,1)S(1)} all-to-all(bf16[8,8,4096]{2,1,0:T(8,128)(2,1)S(1)} %fusion.16), channel_id=1, replica_groups=mesh['section'=4,'expert'=8] {'expert'}, dimensions={0} | all-to-all | bytes 1048576 | tf_op jit(solution)/shard_map/all_to_all | solution.py:82
  69.9 0.2 fusion.19
  70.1 3.7 %collective-permute-start = (bf16[16,4096]{1,0:T(8,128)(2,1)S(1)}, bf16[16,4096]{1,0:T(8,128)(2,1)S(1)}, u32[]{:S(2)}, u32[]{:S(2)}) collective-permute-start(bf16[16,4096]{1,0:T(8,128)(2,1)S(1)} %fusion.19), channel_id=1, source_target_pairs={{0,24},{8,0},{16,8},{24,16},{1,25},{9,1},{17,9},{25,17},{2,26},{10... | collective-permute-start | bytes 393224 | tf_op jit(solution)/shard_map/ppermute | solution.py:11
  73.8 2.5 %collective-permute-done = bf16[16,4096]{1,0:T(8,128)(2,1)S(1)} collective-permute-done((bf16[16,4096]{1,0:T(8,128)(2,1)S(1)}, bf16[16,4096]{1,0:T(8,128)(2,1)S(1)}, u32[]{:S(2)}, u32[]{:S(2)}) %collective-permute-start) | collective-permute-done | bytes 131104 | tf_op jit(solution)/shard_map/ppermute | solution.py:11
  76.3 0.7 copy.24
  (11 shorter events, 0.0 us)
Async XLA Ops:
  0.6 0.9 %copy-start = (bf16[1,16,4096]{2,1,0:T(8,128)(2,1)S(1)}, bf16[1,16,4096]{2,1,0:T(8,128)(2,1)}, u32[]{:S(2)}) copy-start(bf16[1,16,4096]{2,1,0:T(8,128)(2,1)} %param.7) | copy-start | bytes 393220
  2.6 14.9 %all-to-all-start.2 = ((bf16[8,8,4096]{2,1,0:T(8,128)(2,1)}), bf16[8,8,4096]{2,1,0:T(8,128)(2,1)S(1)}, u32[]{:S(2)}, u32[]{:S(2)}) async-start(bf16[8,8,4096]{2,1,0:T(8,128)(2,1)} %convolution_convert_fusion), calls=%async_computation.2 | async-start | bytes 1048576 | tf_op jit(solution)/shard_map/all_to_all | solution.py:69
  17.5 13.2 %all-to-all-start = ((bf16[8,8,4096]{2,1,0:T(8,128)(2,1)}), bf16[8,8,4096]{2,1,0:T(8,128)(2,1)S(1)}, u32[]{:S(2)}, u32[]{:S(2)}) async-start(bf16[8,8,4096]{2,1,0:T(8,128)(2,1)} %convolution_convert_fusion.1), calls=%async_computation | async-start | bytes 1048576 | tf_op jit(solution)/shard_map/all_to_all | solution.py:70
  21.0 5.0 %copy-start.1 = (bf16[1,768,4096]{2,1,0:T(8,128)(2,1)S(1)}, bf16[1,768,4096]{2,1,0:T(8,128)(2,1)}, u32[]{:S(2)}) copy-start(bf16[1,768,4096]{2,1,0:T(8,128)(2,1)} %param.12) | copy-start | bytes 18874372
  26.0 13.6 %copy-start.3 = (bf16[1,16,2]{1,2,0:T(2,128)(2,1)S(1)}, bf16[1,16,2]{1,2,0:T(2,128)(2,1)}, u32[]{:S(2)}) copy-start(bf16[1,16,2]{1,2,0:T(2,128)(2,1)} %param.10) | copy-start | bytes 196
  26.0 18.3 %copy-start.2 = (s32[1,16,2]{1,2,0:T(2,128)S(1)}, s32[1,16,2]{1,2,0:T(2,128)}, u32[]{:S(2)}) copy-start(s32[1,16,2]{1,2,0:T(2,128)} %param.9) | copy-start | bytes 388
  28.1 28.3 %slice-start = ((s8[6291456]{0:T(1024)(128)(4,1)}), s8[2097152]{0:T(1024)(128)(4,1)S(1)}, s32[]{:S(2)}) async-start(s8[6291456]{0:T(1024)(128)(4,1)} %bitcast.73), calls=%async_computation.5 | async-start | bytes 4194304
  36.3 7.8 %all-to-all-start.4 = ((f32[8,1,8]{2,1,0:T(1,128)}), f32[8,1,8]{2,1,0:T(1,128)S(1)}, u32[]{:S(2)}, u32[]{:S(2)}) async-start(f32[8,1,8]{2,1,0:T(1,128)} %bitcast.20), calls=%async_computation.4 | async-start | bytes 8192 | tf_op jit(solution)/shard_map/all_to_all | solution.py:89
  52.2 4.2 %slice-start.1 = ((s8[6291456]{0:T(1024)(128)(4,1)}), s8[4194304]{0:T(1024)(128)(4,1)S(1)}, s32[]{:S(2)}) async-start(s8[6291456]{0:T(1024)(128)(4,1)} %bitcast.73), calls=%async_computation.6 | async-start | bytes 8388608
  70.1 6.2 %collective-permute-start = (bf16[16,4096]{1,0:T(8,128)(2,1)S(1)}, bf16[16,4096]{1,0:T(8,128)(2,1)S(1)}, u32[]{:S(2)}, u32[]{:S(2)}) collective-permute-start(bf16[16,4096]{1,0:T(8,128)(2,1)S(1)} %fusion.19), channel_id=1, source_target_pairs={{0,24},{8,0},{16,8},{24,16},{1,25},{9,1},{17,9},{25,17},{2,26},{10... | collective-permute-start | bytes 393224 | tf_op jit(solution)/shard_map/ppermute | solution.py:11
where the time goes:
time: 77.5 us; the launch traced here: 77 us
  matrix products  21.1 us (27%)
  blocking collectives  19.2 us (25%)
  waiting for transfers between devices  17.4 us (22%)
  starting transfers between devices  15.6 us (20%)
  local copies, waits for them, and re-layouts  1.53 us (2%)
  other arithmetic  1.33 us (2%)
  between operations  0.79 us (1%)
    all_to_all x1, blocking collectives, on_device(): lax.all_to_all(partial_value.reshape(sources, slots_here, partial_value.s...  12.2 us
    all_to_all x1, waiting for transfers between devices, on_device(): lax.all_to_all(send_x, 'expert', split_axis=0, concat_axis=0, tiled=True)  7.77 us
    all_to_all x1, blocking collectives, on_device(): lax.all_to_all(send_g, 'expert', split_axis=0, concat_axis=0, tiled=True)  7.02 us
    all_to_all x1, starting transfers between devices, on_device(): lax.all_to_all(send_x, 'expert', split_axis=0, concat_axis=0, tiled=True)  5.17 us
    dot_general x1, matrix products, expert_terms(): lax.dot_general(rows_x, gate_mat, dims, preferred_element_type=jnp.float32)  4.96 us
    dot_general x1, matrix products, expert_terms(): lax.dot_general(rows_dy, down_mat, dims, preferred_element_type=jnp.float32)  4.92 us
    all_to_all x1, waiting for transfers between devices, on_device(): lax.all_to_all(scores.reshape(sources, slots_here), 'expert', split_axis=...  4.49 us
    dot_general x1, matrix products, expert_terms(): jnp.dot(grad_gate, gate_mat, preferred_element_type=jnp.float32)  4.2 us
  transfers between devices with their start and end apart: 4, of which 4 were waited for; matrix products, arithmetic and copies ran while one was open for 12% of the time, Pallas kernels for 0%

commit v1 on v0

v1 whole, which is shorter than its diff:
```python
import functools

import jax
import jax.numpy as jnp
from jax import lax
from jax.experimental import pallas as pl
from jax.experimental.pallas import tpu as pltpu
from jax.sharding import PartitionSpec as P

EXPERTS = 8
LANES = 128
CHUNKS = 2
NT = (((1,), (1,)), ((), ()))
TN = (((0,), (0,)), ((), ()))
VMEM = pl.BlockSpec(memory_space=pltpu.VMEM)
HBM = pl.BlockSpec(memory_space=pltpu.HBM)


def shifted(array, axis, by):
    peers = lax.axis_size(axis)
    return lax.ppermute(array, axis, [(i, (i + by) % peers) for i in range(peers)])


def swapped(array, bits):
    peers = lax.axis_size("expert")
    return lax.ppermute(array, "expert", [(i, i ^ bits) for i in range(peers)])


def resident(array):
    return pltpu.with_memory_space_constraint(array, pltpu.VMEM)


def streamed(array):
    return pltpu.with_memory_space_constraint(array, pltpu.HBM)


def rows_of(near_ref, far_ref, columns):
    return jnp.concatenate([near_ref[:, columns], far_ref[:, columns]], axis=0)


def products(mat_ref, near_ref, far_ref, width):
    total = None
    step = 1024
    for start in range(0, width, step):
        columns = pl.ds(start, min(step, width - start))
        term = lax.dot_general(
            mat_ref[:, columns],
            rows_of(near_ref, far_ref, columns),
            NT,
            preferred_element_type=jnp.float32,
        )
        total = term if total is None else total + term
    return total


def load_kernel(gate_ref, upstream_ref, table_ref, gate_out, packed_out, sems):
    width = upstream_ref.shape[1]
    rows = pltpu.make_async_copy(upstream_ref, packed_out.at[:, pl.ds(0, width)], sems.at[0])
    gate = pltpu.make_async_copy(gate_ref, gate_out, sems.at[1])
    rows.start()
    gate.start()
    packed_out[:, width:] = table_ref[...]
    rows.wait()
    gate.wait()


def first_kernel(
    near_ref, far_ref, gate_ref, up_hbm, down_hbm, gate_pre_ref, up_pre_ref, up_out, down_out, sems
):
    width = gate_ref.shape[1]
    up_copy = pltpu.make_async_copy(up_hbm, up_out, sems.at[0])
    down_copy = pltpu.make_async_copy(down_hbm, down_out, sems.at[1])
    up_copy.start()
    down_copy.start()
    gate_pre_ref[...] = products(gate_ref, near_ref, far_ref, width)
    up_copy.wait()
    up_pre_ref[...] = products(up_out, near_ref, far_ref, width)
    down_copy.wait()


def second_kernel(
    group_size, near_ref, far_ref, down_ref, gate_pre_ref, up_pre_ref, grad_gate_ref, grad_up_ref, score_ref
):
    me = lax.axis_index("expert")
    width = down_ref.shape[1]
    hidden_grad = products(down_ref, near_ref, far_ref, width)
    table = rows_of(near_ref, far_ref, pl.ds(width, LANES))
    lane = lax.broadcasted_iota(jnp.int32, (8, LANES), 1)
    pick = jnp.where(lane == me // group_size, 1.0, 0.0).astype(jnp.bfloat16)
    weight = lax.dot_general(pick, table, NT, preferred_element_type=jnp.float32)[0:1, :]
    gate_pre = gate_pre_ref[...]
    up_pre = up_pre_ref[...]
    sigmoid_val = 1.0 / (1.0 + jnp.exp(-gate_pre))
    activated = gate_pre * sigmoid_val
    slope = sigmoid_val * (1.0 + gate_pre * (1.0 - sigmoid_val))
    scores = jnp.sum(activated * up_pre * hidden_grad, axis=0, keepdims=True)
    scaled = hidden_grad * weight
    grad_gate_ref[...] = (scaled * up_pre * slope).astype(jnp.bfloat16)
    grad_up_ref[...] = (scaled * activated).astype(jnp.bfloat16)
    scores = jnp.where(weight != 0.0, scores, 0.0)
    tokens = scores.shape[1]
    by_token = jnp.transpose(jnp.broadcast_to(scores, (LANES, tokens)))
    high = by_token.astype(jnp.bfloat16).astype(jnp.float32)
    low = by_token - high
    column = lax.broadcasted_iota(jnp.int32, (tokens, LANES), 1)
    half = LANES // 2
    score_ref[...] = jnp.where(
        column == me, high, jnp.where(column == me + half, low, 0.0)
    ).astype(jnp.bfloat16)


def third_kernel(first, span, grad_gate_ref, grad_up_ref, gate_ref, up_ref, score_ref, near_ref, far_ref):
    columns = pl.ds(first, span)
    partial_value = lax.dot_general(
        grad_gate_ref[...], gate_ref[:, columns], TN, preferred_element_type=jnp.float32
    )
    partial_value = partial_value + lax.dot_general(
        grad_up_ref[...], up_ref[:, columns], TN, preferred_element_type=jnp.float32
    )
    partial_value = partial_value.astype(jnp.bfloat16)
    half = near_ref.shape[0]
    near_ref[:, :span] = partial_value[:half]
    far_ref[:, :span] = partial_value[half:]
    if near_ref.shape[1] > span:
        near_ref[:, span:] = score_ref[:half, :]
        far_ref[:, span:] = score_ref[half:, :]


def params(megabytes):
    return pltpu.CompilerParams(vmem_limit_bytes=megabytes * 1024 * 1024)


def on_device(tokens_in, out_grad, expert_ids, gate_weights, w_gate, w_up, w_down):
    inputs = tokens_in[0]
    upstream = out_grad[0]
    routes = expert_ids[0]
    gate_vals = gate_weights[0]
    tok_rows, width = inputs.shape
    hidden = w_gate.shape[1]
    devices = lax.axis_size("expert")
    group_size = devices // EXPERTS
    half = tok_rows * devices // 2
    others = sorted(range(2, devices, 2), reverse=True)

    def gathered(block):
        parts = {0: block}
        for bits in others:
            parts[bits] = swapped(block, bits)
        near = jnp.concatenate([parts[bits] for bits in range(0, devices, 2)], axis=0)
        return near, swapped(near, 1)

    lanes = jnp.arange(LANES, dtype=jnp.int32)
    route_hit = routes[:, :, None] == lanes[None, None, :]
    table = jnp.sum(jnp.where(route_hit, gate_vals[:, :, None].astype(jnp.float32), 0.0), axis=1)
    near_x, far_x = gathered(inputs)
    matrix = jax.ShapeDtypeStruct((hidden, width), jnp.bfloat16)
    gate_mat, packed = pl.pallas_call(
        load_kernel,
        out_shape=(matrix, jax.ShapeDtypeStruct((tok_rows, width + LANES), jnp.bfloat16)),
        in_specs=[HBM, HBM, VMEM],
        out_specs=(VMEM, VMEM),
        scratch_shapes=[pltpu.SemaphoreType.DMA((2,))],
        compiler_params=params(8),
        cost_estimate=pl.CostEstimate(
            flops=0, bytes_accessed=4 * hidden * width, transcendentals=0
        ),
    )(streamed(w_gate[0]), streamed(upstream), table.astype(jnp.bfloat16))
    gate_mat = resident(gate_mat)
    near_dy, far_dy = gathered(packed)
    pre = jax.ShapeDtypeStruct((hidden, 2 * half), jnp.float32)
    gate_pre, up_pre, up_mat, down_mat = pl.pallas_call(
        first_kernel,
        out_shape=(pre, pre, matrix, matrix),
        in_specs=[VMEM, VMEM, VMEM, HBM, HBM],
        out_specs=(VMEM,) * 4,
        scratch_shapes=[pltpu.SemaphoreType.DMA((2,))],
        compiler_params=params(8),
        cost_estimate=pl.CostEstimate(
            flops=8 * half * hidden * width, bytes_accessed=8 * hidden * width, transcendentals=0
        ),
    )(resident(near_x), resident(far_x), gate_mat, streamed(w_up[0]), streamed(w_down[0]))
    up_mat = resident(up_mat)
    down_mat = resident(down_mat)
    grads = jax.ShapeDtypeStruct((hidden, 2 * half), jnp.bfloat16)
    grad_gate, grad_up, score_lanes = pl.pallas_call(
        functools.partial(second_kernel, group_size),
        out_shape=(grads, grads, jax.ShapeDtypeStruct((2 * half, LANES), jnp.bfloat16)),
        in_specs=[VMEM] * 5,
        out_specs=(VMEM, VMEM, VMEM),
        compiler_params=params(8),
    )(resident(near_dy), resident(far_dy), down_mat, resident(gate_pre), resident(up_pre))
    passed = []
    score_sum = None
    span = width // CHUNKS
    for chunk in range(CHUNKS):
        extra = LANES if chunk == 0 else 0
        out = jax.ShapeDtypeStruct((half, span + extra), jnp.bfloat16)
        near, far = pl.pallas_call(
            functools.partial(third_kernel, chunk * span, span),
            out_shape=(out, out),
            in_specs=[VMEM] * 5,
            out_specs=(VMEM, VMEM),
            compiler_params=params(8),
        )(resident(grad_gate), resident(grad_up), gate_mat, up_mat, resident(score_lanes))
        merged = near.astype(jnp.float32) + swapped(far, 1).astype(jnp.float32)
        merged = merged.astype(jnp.bfloat16)
        blocks = merged.reshape(devices // 2, tok_rows, span + extra)
        total = blocks[0].astype(jnp.float32)
        for bits in others:
            total = total + swapped(blocks[bits // 2], bits).astype(jnp.float32)
        if extra:
            score_sum = total[:, span:]
        passed.append(shifted(total[:, :span].astype(jnp.bfloat16), "section", -1))
    score_sum = score_sum[:, : LANES // 2] + score_sum[:, LANES // 2 :]
    owner = jnp.arange(LANES // 2, dtype=jnp.int32) // group_size
    mine = routes[:, :, None] == owner[None, None, :]
    grads_route = jnp.sum(jnp.where(mine, score_sum[:, None, :], 0.0), axis=2)
    return (jnp.concatenate(passed, axis=1)[None], grads_route[None])


def solution(mesh):
    return jax.shard_map(
        on_device,
        mesh=mesh,
        in_specs=(P("section", "expert", None),) * 7,
        out_specs=(P("section", "expert", None), P("section", "expert", None)),
        check_vma=False,
    )
```

time: 77.5 us -> 48.8 us (0.63)
  matrix products: 21.1 us -> 0 us
  blocking collectives: 19.2 us -> 0 us
  Pallas kernels: 0 us -> 13.7 us
  waiting for transfers between devices: 17.4 us -> 8.41 us
  starting transfers between devices: 15.6 us -> 22.4 us
  other arithmetic: 1.33 us -> 3.11 us
  local copies, waits for them, and re-layouts: 1.53 us -> 0.11 us
    dot_general x11 -> x0, matrix products: 21.1 us -> none  [the longest x1 4.96 us: expert_terms(): lax.dot_general(rows_x, gate_mat, dims, preferred_element_type=jnp.float32)]
    all_to_all x2 -> x0, blocking collectives: 19.2 us -> none  [the longest x1 12.2 us: on_device(): lax.all_to_all(partial_value.reshape(sources, slots_here, partial_value.s...]
    ppermute x0 -> x16, starting transfers between devices: none -> 15.2 us  [swapped(): return lax.ppermute(array, 'expert', [(i, i ^ bits) for i in range(peers)])]
    all_to_all x3 -> x0, waiting for transfers between devices: 14.9 us -> none  [the longest x1 7.77 us: on_device(): lax.all_to_all(send_x, 'expert', split_axis=0, concat_axis=0, tiled=True)]
    pallas_call x0 -> x5, Pallas kernels: none -> 13.7 us  [the longest x1 6.79 us: on_device(): pl.pallas_call(first_kernel, out_shape=(pre, pre, matrix, matrix), in_spe...]
    all_to_all x3 -> x0, starting transfers between devices: 12 us -> none  [the longest x1 5.17 us: on_device(): lax.all_to_all(send_x, 'expert', split_axis=0, concat_axis=0, tiled=True)]
    ppermute x0 -> x16, waiting for transfers between devices: none -> 7.23 us  [swapped(): return lax.ppermute(array, 'expert', [(i, i ^ bits) for i in range(peers)])]
    ppermute x1 -> x2, starting transfers between devices: 3.66 us -> 7.26 us  [shifted(): lax.ppermute(array, axis, [(i, (i + by) % peers) for i in range(peers)])]
  transfers between devices with their start and end apart: 4 -> 18, of which waited for: 4 -> 6; matrix products, arithmetic and copies ran while one was open for 12% -> 5% of each run, Pallas kernels for 0% -> 22%
where the time goes in v1:
time: 48.8 us; the launch traced here: 48.6 us
  starting transfers between devices  22.4 us (46%)
  Pallas kernels  13.7 us (28%)
  waiting for transfers between devices  8.41 us (17%)
  other arithmetic  3.11 us (6%)
  between operations  0.82 us (2%)
    ppermute x16, starting transfers between devices, swapped(): return lax.ppermute(array, 'expert', [(i, i ^ bits) for i in range(peers)])  15.2 us
    ppermute x2, starting transfers between devices, shifted(): lax.ppermute(array, axis, [(i, (i + by) % peers) for i in range(peers)])  7.26 us
    ppermute x16, waiting for transfers between devices, swapped(): return lax.ppermute(array, 'expert', [(i, i ^ bits) for i in range(peers)])  7.23 us
    pallas_call x1, Pallas kernels, on_device(): pl.pallas_call(first_kernel, out_shape=(pre, pre, matrix, matrix), in_spe...  6.79 us
    pallas_call x1, Pallas kernels, on_device(): pl.pallas_call(load_kernel, out_shape=(matrix, jax.ShapeDtypeStruct((tok_...  2.89 us
    pallas_call x1, Pallas kernels, on_device(): pl.pallas_call(functools.partial(second_kernel, group_size), out_shape=(g...  2.03 us
    pallas_call x2, Pallas kernels, on_device(): pl.pallas_call(functools.partial(third_kernel, chunk * span, span), out_s...  2.01 us
    ppermute x2, waiting for transfers between devices, shifted(): lax.ppermute(array, axis, [(i, (i + by) % peers) for i in range(peers)])  1.18 us
  transfers between devices with their start and end apart: 18, of which 6 were waited for; matrix products, arithmetic and copies ran while one was open for 5% of the time, Pallas kernels for 22%

profile of v1, /device:TPU:0, one launch (start us, length us, event | category | flops | bytes accessed | tf_op | source)
XLA Modules:
  0.0 48.6 jit_solution(3891141167021833587)
XLA Ops:
  0.6 3.0 %collective-permute-start.4 = (bf16[16,4096]{1,0:T(8,128)(2,1)}, bf16[16,4096]{1,0:T(8,128)(2,1)S(1)}, u32[]{:S(2)}, u32[]{:S(2)}) collective-permute-start(bf16[16,4096]{1,0:T(8,128)(2,1)} %bitcast.16), channel_id=1, source_target_pairs={{0,2},{1,3},{2,0},{3,1},{4,6},{5,7},{6,4},{7,5},{8,10},{9,11},{10,... | collective-permute-start | bytes 393224 | tf_op jit(solution)/shard_map/ppermute | solution.py:26
  3.6 1.5 %collective-permute-start.5 = (bf16[16,4096]{1,0:T(8,128)(2,1)}, bf16[16,4096]{1,0:T(8,128)(2,1)S(1)}, u32[]{:S(2)}, u32[]{:S(2)}) collective-permute-start(bf16[16,4096]{1,0:T(8,128)(2,1)} %bitcast.17), channel_id=1, source_target_pairs={{0,4},{1,5},{2,6},{3,7},{4,0},{5,1},{6,2},{7,3},{8,12},{9,13},{10,... | collective-permute-start | bytes 393224 | tf_op jit(solution)/shard_map/ppermute | solution.py:26
  5.2 0.7 %bitcast_convert_fusion = f32[16,2]{0,1:T(2,128)S(1)} fusion(bf16[1,16,2]{1,2,0:T(2,128)(2,1)} %param.10), kind=kLoop, calls=%fused_computation.16 | loop fusion | flops 32 | bytes 192 | tf_op jit(solution)/shard_map/convert_element_type | solution.py:154
  5.8 0.8 %select_reduce_fusion.1.table_ref = bf16[16,128]{1,0:T(8,128)(2,1)S(1)} fusion(f32[16,2]{0,1:T(2,128)S(1)} %bitcast_convert_fusion, s32[16,2]{0,1:T(2,128)} %bitcast.20), kind=kLoop, calls=%fused_computation.9 | loop fusion | flops 10240 | bytes 4352 | tf_op jit(solution)/shard_map/reduce_sum | solution.py:154
  6.6 2.9 %shard_map.86 = (bf16[768,4096]{1,0:T(8,128)(2,1)S(1)}, bf16[16,4224]{1,0:T(8,128)(2,1)S(1)}) custom-call(bf16[768,4096]{1,0:T(8,128)(2,1)} %bitcast.14, bf16[16,4096]{1,0:T(8,128)(2,1)} %bitcast.15, bf16[16,128]{1,0:T(8,128)(2,1)S(1)} %select_reduce_fusion.1.table_ref), custom_call_target="tpu_custom_call" | custom-call | bytes 12582912 | tf_op jit(solution)/shard_map/pallas_call | solution.py:157
  9.5 2.0 %collective-permute-start = (bf16[16,4224]{1,0:T(8,128)(2,1)S(1)}, bf16[16,4224]{1,0:T(8,128)(2,1)S(1)}, u32[]{:S(2)}, u32[]{:S(2)}) collective-permute-start(bf16[16,4224]{1,0:T(8,128)(2,1)S(1)} %get-tuple-element.15), channel_id=1, source_target_pairs={{0,2},{1,3},{2,0},{3,1},{4,6},{5,7},{6,4},{7,5},{8,10},{9,11},{10,... | collective-permute-start | bytes 405512 | tf_op jit(solution)/shard_map/ppermute | solution.py:26
  11.5 1.5 %collective-permute-start.1 = (bf16[16,4224]{1,0:T(8,128)(2,1)S(1)}, bf16[16,4224]{1,0:T(8,128)(2,1)S(1)}, u32[]{:S(2)}, u32[]{:S(2)}) collective-permute-start(bf16[16,4224]{1,0:T(8,128)(2,1)S(1)} %get-tuple-element.15), channel_id=1, source_target_pairs={{0,4},{1,5},{2,6},{3,7},{4,0},{5,1},{6,2},{7,3},{8,12},{9,13},{10,... | collective-permute-start | bytes 405512 | tf_op jit(solution)/shard_map/ppermute | solution.py:26
  13.0 0.1 collective-permute-start.2
  13.2 0.1 collective-permute-start.7
  13.3 1.8 %collective-permute-done = bf16[16,4224]{1,0:T(8,128)(2,1)S(1)} collective-permute-done((bf16[16,4224]{1,0:T(8,128)(2,1)S(1)}, bf16[16,4224]{1,0:T(8,128)(2,1)S(1)}, u32[]{:S(2)}, u32[]{:S(2)}) %collective-permute-start) | collective-permute-done | bytes 135200 | tf_op jit(solution)/shard_map/ppermute | solution.py:26
  15.1 4.3 %collective-permute-done.1 = bf16[16,4224]{1,0:T(8,128)(2,1)S(1)} collective-permute-done((bf16[16,4224]{1,0:T(8,128)(2,1)S(1)}, bf16[16,4224]{1,0:T(8,128)(2,1)S(1)}, u32[]{:S(2)}, u32[]{:S(2)}) %collective-permute-start.1) | collective-permute-done | bytes 135200 | tf_op jit(solution)/shard_map/ppermute | solution.py:26
  19.4 0.1 collective-permute-start.3
  19.5 6.8 %shard_map.87 = (f32[768,128]{1,0:T(8,128)S(1)}, f32[768,128]{1,0:T(8,128)S(1)}, bf16[768,4096]{1,0:T(8,128)(2,1)S(1)}, bf16[768,4096]{1,0:T(8,128)(2,1)S(1)}) custom-call(bf16[64,4096]{1,0:T(8,128)(2,1)S(1)} %pad_maximum_fusion.near_ref, bf16[64,4096]{1,0:T(8,128)(2,1)S(1)} %collective-permute-done.7.far_ref, ...), custom_call_target="tpu_custom_call" | custom-call | flops 1610612736 | bytes 25165824 | tf_op jit(solution)/shard_map/pallas_call | solution.py:171
  26.3 2.0 %shard_map.88 = (bf16[768,128]{1,0:T(8,128)(2,1)S(1)}, bf16[768,128]{1,0:T(8,128)(2,1)S(1)}, bf16[128,128]{1,0:T(8,128)(2,1)S(1)}) custom-call(bf16[64,4224]{1,0:T(8,128)(2,1)S(1)} %constant_dynamic-update-slice_fusion.near_ref, bf16[64,4224]{1,0:T(8,128)(2,1)S(1)} %collective-permute-done.3.far_ref, bf16[768,4096]{1,0:T(8,128)(2,1)S(1)} %get-tuple-element.17.down_ref, ...), custom_call_target="tpu_custom_call" | custom-call | tf_op jit(solution)/shard_map/pallas_call | solution.py:185
  28.4 1.0 %shard_map.90 = (bf16[64,2048]{1,0:T(8,128)(2,1)S(1)}, bf16[64,2048]{1,0:T(8,128)(2,1)S(1)}) custom-call(bf16[768,128]{1,0:T(8,128)(2,1)S(1)} %get-tuple-element.20.grad_gate_ref, bf16[768,128]{1,0:T(8,128)(2,1)S(1)} %get-tuple-element.21.grad_up_ref, bf16[768,4096]{1,0:T(8,128)(2,1)S(1)} %get-tuple-element.16.gate_ref, ...), custom_call_target="tpu_custom_call" | custom-call | tf_op jit(solution)/shard_map/pallas_call | solution.py:198
  29.4 0.6 %collective-permute-start.13 = (bf16[64,2048]{1,0:T(8,128)(2,1)S(1)}, bf16[64,2048]{1,0:T(8,128)(2,1)S(1)}, u32[]{:S(2)}, u32[]{:S(2)}) collective-permute-start(bf16[64,2048]{1,0:T(8,128)(2,1)S(1)} %get-tuple-element.27), channel_id=1, source_target_pairs={{0,1},{1,0},{2,3},{3,2},{4,5},{5,4},{6,7},{7,6},{8,9},{9,8},{10,11... | collective-permute-start | bytes 786440 | tf_op jit(solution)/shard_map/ppermute | solution.py:26
  29.9 1.0 %shard_map.89 = (bf16[64,2176]{1,0:T(8,128)(2,1)S(1)}, bf16[64,2176]{1,0:T(8,128)(2,1)S(1)}) custom-call(bf16[768,128]{1,0:T(8,128)(2,1)S(1)} %get-tuple-element.20.grad_gate_ref, bf16[768,128]{1,0:T(8,128)(2,1)S(1)} %get-tuple-element.21.grad_up_ref, bf16[768,4096]{1,0:T(8,128)(2,1)S(1)} %get-tuple-element.16.gate_ref, ...), custom_call_target="tpu_custom_call" | custom-call | tf_op jit(solution)/shard_map/pallas_call | solution.py:198
  31.0 0.1 collective-permute-start.8
  31.2 0.8 %collective-permute-start.14 = (bf16[16,2048]{1,0:T(8,128)(2,1)S(1)}, bf16[16,2048]{1,0:T(8,128)(2,1)S(1)}, u32[]{:S(2)}, u32[]{:S(2)}) collective-permute-start(bf16[16,2048]{1,0:T(8,128)(2,1)S(1)} %get-tuple-element.31), channel_id=1, source_target_pairs={{0,6},{1,7},{2,4},{3,5},{4,2},{5,3},{6,0},{7,1},{8,14},{9,15},{10,... | collective-permute-start | bytes 196616 | tf_op jit(solution)/shard_map/ppermute | solution.py:26
  32.0 1.3 %collective-permute-start.15 = (bf16[16,2048]{1,0:T(8,128)(2,1)S(1)}, bf16[16,2048]{1,0:T(8,128)(2,1)S(1)}, u32[]{:S(2)}, u32[]{:S(2)}) collective-permute-start(bf16[16,2048]{1,0:T(8,128)(2,1)S(1)} %get-tuple-element.33), channel_id=1, source_target_pairs={{0,4},{1,5},{2,6},{3,7},{4,0},{5,1},{6,2},{7,3},{8,12},{9,13},{10,... | collective-permute-start | bytes 196616 | tf_op jit(solution)/shard_map/ppermute | solution.py:26
  33.2 1.5 %collective-permute-start.16 = (bf16[16,2048]{1,0:T(8,128)(2,1)S(1)}, bf16[16,2048]{1,0:T(8,128)(2,1)S(1)}, u32[]{:S(2)}, u32[]{:S(2)}) collective-permute-start(bf16[16,2048]{1,0:T(8,128)(2,1)S(1)} %get-tuple-element.32), channel_id=1, source_target_pairs={{0,2},{1,3},{2,0},{3,1},{4,6},{5,7},{6,4},{7,5},{8,10},{9,11},{10,... | collective-permute-start | bytes 196616 | tf_op jit(solution)/shard_map/ppermute | solution.py:26
  34.9 1.1 %collective-permute-start.10 = (bf16[16,2176]{1,0:T(8,128)(2,1)S(1)}, bf16[16,2176]{1,0:T(8,128)(2,1)S(1)}, u32[]{:S(2)}, u32[]{:S(2)}) collective-permute-start(bf16[16,2176]{1,0:T(8,128)(2,1)S(1)} %get-tuple-element.30), channel_id=1, source_target_pairs={{0,4},{1,5},{2,6},{3,7},{4,0},{5,1},{6,2},{7,3},{8,12},{9,13},{10,... | collective-permute-start | bytes 208904 | tf_op jit(solution)/shard_map/ppermute | solution.py:26
  35.9 0.3 collective-permute-start.11
  36.2 0.9 %collective-permute-done.14 = bf16[16,2048]{1,0:T(8,128)(2,1)S(1)} collective-permute-done((bf16[16,2048]{1,0:T(8,128)(2,1)S(1)}, bf16[16,2048]{1,0:T(8,128)(2,1)S(1)}, u32[]{:S(2)}, u32[]{:S(2)}) %collective-permute-start.14) | collective-permute-done | bytes 65568 | tf_op jit(solution)/shard_map/ppermute | solution.py:26
  37.1 1.3 %collective-permute-start.9 = (bf16[16,2176]{1,0:T(8,128)(2,1)S(1)}, bf16[16,2176]{1,0:T(8,128)(2,1)S(1)}, u32[]{:S(2)}, u32[]{:S(2)}) collective-permute-start(bf16[16,2176]{1,0:T(8,128)(2,1)S(1)} %get-tuple-element.28), channel_id=1, source_target_pairs={{0,6},{1,7},{2,4},{3,5},{4,2},{5,3},{6,0},{7,1},{8,14},{9,15},{10,... | collective-permute-start | bytes 208904 | tf_op jit(solution)/shard_map/ppermute | solution.py:26
  38.5 3.7 %collective-permute-start.17 = (bf16[16,2048]{1,0:T(8,128)(2,1)S(1)}, bf16[16,2048]{1,0:T(8,128)(2,1)S(1)}, u32[]{:S(2)}, u32[]{:S(2)}) collective-permute-start(bf16[16,2048]{1,0:T(8,128)(2,1)S(1)} %add_convert_fusion.2), channel_id=1, source_target_pairs={{0,24},{8,0},{16,8},{24,16},{1,25},{9,1},{17,9},{25,17},{2,26},{10... | collective-permute-start | bytes 196616 | tf_op jit(solution)/shard_map/ppermute | solution.py:21
  42.1 0.2 collective-permute-done.9
  42.4 0.1 slice_add_fusion
  42.4 3.6 %collective-permute-start.12 = (bf16[16,2048]{1,0:T(8,128)(2,1)S(1)}, bf16[16,2048]{1,0:T(8,128)(2,1)S(1)}, u32[]{:S(2)}, u32[]{:S(2)}) collective-permute-start(bf16[16,2048]{1,0:T(8,128)(2,1)S(1)} %slice.72), channel_id=1, source_target_pairs={{0,24},{8,0},{16,8},{24,16},{1,25},{9,1},{17,9},{25,17},{2,26},{10... | collective-permute-start | bytes 196616 | tf_op jit(solution)/shard_map/ppermute | solution.py:21
  46.0 0.7 %select_reduce_fusion = f32[16,2]{0,1:T(2,128)} fusion(f32[16,64]{1,0:T(8,128)S(1)} %slice_add_fusion, s32[16,2]{0,1:T(2,128)S(1)} %bitcast.21), kind=kLoop, calls=%fused_computation.7 | loop fusion | flops 6112 | bytes 4352 | tf_op jit(solution)/shard_map/reduce_sum | solution.py:217
  46.8 1.2 %collective-permute-done.12 = bf16[16,2048]{1,0:T(8,128)(2,1)S(1)} collective-permute-done((bf16[16,2048]{1,0:T(8,128)(2,1)S(1)}, bf16[16,2048]{1,0:T(8,128)(2,1)S(1)}, u32[]{:S(2)}, u32[]{:S(2)}) %collective-permute-start.12) | collective-permute-done | bytes 65568 | tf_op jit(solution)/shard_map/ppermute | solution.py:21
  47.9 0.7 %maximum_bitcast_fusion = bf16[1,16,4096]{2,1,0:T(8,128)(2,1)} fusion(bf16[16,2048]{1,0:T(8,128)(2,1)S(1)} %collective-permute-done.17, bf16[16,2048]{1,0:T(8,128)(2,1)S(1)} %collective-permute-done.12), kind=kLoop, calls=%fused_computation.5 | loop fusion | flops 262144 | bytes 262144 | tf_op jit(solution)/shard_map/broadcast_in_dim | solution.py:218
  (30 shorter events, 0.5 us)
Async XLA Ops:
  0.6 12.5 %copy-start = (bf16[1,16,4096]{2,1,0:T(8,128)(2,1)S(1)}, bf16[1,16,4096]{2,1,0:T(8,128)(2,1)}, u32[]{:S(2)}) copy-start(bf16[1,16,4096]{2,1,0:T(8,128)(2,1)} %param.7) | copy-start | bytes 393220
  0.6 12.4 %collective-permute-start.4 = (bf16[16,4096]{1,0:T(8,128)(2,1)}, bf16[16,4096]{1,0:T(8,128)(2,1)S(1)}, u32[]{:S(2)}, u32[]{:S(2)}) collective-permute-start(bf16[16,4096]{1,0:T(8,128)(2,1)} %bitcast.16), channel_id=1, source_target_pairs={{0,2},{1,3},{2,0},{3,1},{4,6},{5,7},{6,4},{7,5},{8,10},{9,11},{10,... | collective-permute-start | bytes 393224 | tf_op jit(solution)/shard_map/ppermute | solution.py:26
  3.6 9.5 %collective-permute-start.5 = (bf16[16,4096]{1,0:T(8,128)(2,1)}, bf16[16,4096]{1,0:T(8,128)(2,1)S(1)}, u32[]{:S(2)}, u32[]{:S(2)}) collective-permute-start(bf16[16,4096]{1,0:T(8,128)(2,1)} %bitcast.17), channel_id=1, source_target_pairs={{0,4},{1,5},{2,6},{3,7},{4,0},{5,1},{6,2},{7,3},{8,12},{9,13},{10,... | collective-permute-start | bytes 393224 | tf_op jit(solution)/shard_map/ppermute | solution.py:26
  5.2 8.0 %collective-permute-start.6 = (bf16[16,4096]{1,0:T(8,128)(2,1)}, bf16[16,4096]{1,0:T(8,128)(2,1)S(1)}, u32[]{:S(2)}, u32[]{:S(2)}) collective-permute-start(bf16[16,4096]{1,0:T(8,128)(2,1)} %bitcast.18), channel_id=1, source_target_pairs={{0,6},{1,7},{2,4},{3,5},{4,2},{5,3},{6,0},{7,1},{8,14},{9,15},{10,... | collective-permute-start | bytes 393224 | tf_op jit(solution)/shard_map/ppermute | solution.py:26
  9.5 5.6 %collective-permute-start = (bf16[16,4224]{1,0:T(8,128)(2,1)S(1)}, bf16[16,4224]{1,0:T(8,128)(2,1)S(1)}, u32[]{:S(2)}, u32[]{:S(2)}) collective-permute-start(bf16[16,4224]{1,0:T(8,128)(2,1)S(1)} %get-tuple-element.15), channel_id=1, source_target_pairs={{0,2},{1,3},{2,0},{3,1},{4,6},{5,7},{6,4},{7,5},{8,10},{9,11},{10,... | collective-permute-start | bytes 405512 | tf_op jit(solution)/shard_map/ppermute | solution.py:26
  11.5 7.9 %collective-permute-start.1 = (bf16[16,4224]{1,0:T(8,128)(2,1)S(1)}, bf16[16,4224]{1,0:T(8,128)(2,1)S(1)}, u32[]{:S(2)}, u32[]{:S(2)}) collective-permute-start(bf16[16,4224]{1,0:T(8,128)(2,1)S(1)} %get-tuple-element.15), channel_id=1, source_target_pairs={{0,4},{1,5},{2,6},{3,7},{4,0},{5,1},{6,2},{7,3},{8,12},{9,13},{10,... | collective-permute-start | bytes 405512 | tf_op jit(solution)/shard_map/ppermute | solution.py:26
  13.0 6.4 %collective-permute-start.2 = (bf16[16,4224]{1,0:T(8,128)(2,1)S(1)}, bf16[16,4224]{1,0:T(8,128)(2,1)S(1)}, u32[]{:S(2)}, u32[]{:S(2)}) collective-permute-start(bf16[16,4224]{1,0:T(8,128)(2,1)S(1)} %get-tuple-element.15), channel_id=1, source_target_pairs={{0,6},{1,7},{2,4},{3,5},{4,2},{5,3},{6,0},{7,1},{8,14},{9,15},{10,... | collective-permute-start | bytes 405512 | tf_op jit(solution)/shard_map/ppermute | solution.py:26
  13.2 6.3 %collective-permute-start.7 = (bf16[64,4096]{1,0:T(8,128)(2,1)S(1)}, bf16[64,4096]{1,0:T(8,128)(2,1)S(1)}, u32[]{:S(2)}, u32[]{:S(2)}) collective-permute-start(bf16[64,4096]{1,0:T(8,128)(2,1)S(1)} %pad_maximum_fusion.near_ref), channel_id=1, source_target_pairs={{0,1},{1,0},{2,3},{3,2},{4,5},{5,4},{6,7},{7,6},{8,9},{9,8},{10,11... | collective-permute-start | bytes 1572872 | tf_op jit(solution)/shard_map/ppermute | solution.py:26
  19.4 6.9 %collective-permute-start.3 = (bf16[64,4224]{1,0:T(8,128)(2,1)S(1)}, bf16[64,4224]{1,0:T(8,128)(2,1)S(1)}, u32[]{:S(2)}, u32[]{:S(2)}) collective-permute-start(bf16[64,4224]{1,0:T(8,128)(2,1)S(1)} %constant_dynamic-update-slice_fusion.near_ref), channel_id=1, source_target_pairs={{0,1},{1,0},{2,3},{3,2},{4,5},{5,4},{6,7},{7,6},{8,9},{9,8},{10,11... | collective-permute-start | bytes 1622024 | tf_op jit(solution)/shard_map/ppermute | solution.py:26
  29.4 16.7 %copy-start.1 = (s32[1,16,2]{1,2,0:T(2,128)S(1)}, s32[1,16,2]{1,2,0:T(2,128)}, u32[]{:S(2)}) copy-start(s32[1,16,2]{1,2,0:T(2,128)} %param.9) | copy-start | bytes 388
  29.4 1.7 %collective-permute-start.13 = (bf16[64,2048]{1,0:T(8,128)(2,1)S(1)}, bf16[64,2048]{1,0:T(8,128)(2,1)S(1)}, u32[]{:S(2)}, u32[]{:S(2)}) collective-permute-start(bf16[64,2048]{1,0:T(8,128)(2,1)S(1)} %get-tuple-element.27), channel_id=1, source_target_pairs={{0,1},{1,0},{2,3},{3,2},{4,5},{5,4},{6,7},{7,6},{8,9},{9,8},{10,11... | collective-permute-start | bytes 786440 | tf_op jit(solution)/shard_map/ppermute | solution.py:26
  31.0 3.8 %collective-permute-start.8 = (bf16[64,2176]{1,0:T(8,128)(2,1)S(1)}, bf16[64,2176]{1,0:T(8,128)(2,1)S(1)}, u32[]{:S(2)}, u32[]{:S(2)}) collective-permute-start(bf16[64,2176]{1,0:T(8,128)(2,1)S(1)} %get-tuple-element.25), channel_id=1, source_target_pairs={{0,1},{1,0},{2,3},{3,2},{4,5},{5,4},{6,7},{7,6},{8,9},{9,8},{10,11... | collective-permute-start | bytes 835592 | tf_op jit(solution)/shard_map/ppermute | solution.py:26
  31.2 5.9 %collective-permute-start.14 = (bf16[16,2048]{1,0:T(8,128)(2,1)S(1)}, bf16[16,2048]{1,0:T(8,128)(2,1)S(1)}, u32[]{:S(2)}, u32[]{:S(2)}) collective-permute-start(bf16[16,2048]{1,0:T(8,128)(2,1)S(1)} %get-tuple-element.31), channel_id=1, source_target_pairs={{0,6},{1,7},{2,4},{3,5},{4,2},{5,3},{6,0},{7,1},{8,14},{9,15},{10,... | collective-permute-start | bytes 196616 | tf_op jit(solution)/shard_map/ppermute | solution.py:26
  32.0 6.4 %collective-permute-start.15 = (bf16[16,2048]{1,0:T(8,128)(2,1)S(1)}, bf16[16,2048]{1,0:T(8,128)(2,1)S(1)}, u32[]{:S(2)}, u32[]{:S(2)}) collective-permute-start(bf16[16,2048]{1,0:T(8,128)(2,1)S(1)} %get-tuple-element.33), channel_id=1, source_target_pairs={{0,4},{1,5},{2,6},{3,7},{4,0},{5,1},{6,2},{7,3},{8,12},{9,13},{10,... | collective-permute-start | bytes 196616 | tf_op jit(solution)/shard_map/ppermute | solution.py:26
  33.2 5.2 %collective-permute-start.16 = (bf16[16,2048]{1,0:T(8,128)(2,1)S(1)}, bf16[16,2048]{1,0:T(8,128)(2,1)S(1)}, u32[]{:S(2)}, u32[]{:S(2)}) collective-permute-start(bf16[16,2048]{1,0:T(8,128)(2,1)S(1)} %get-tuple-element.32), channel_id=1, source_target_pairs={{0,2},{1,3},{2,0},{3,1},{4,6},{5,7},{6,4},{7,5},{8,10},{9,11},{10,... | collective-permute-start | bytes 196616 | tf_op jit(solution)/shard_map/ppermute | solution.py:26
  34.9 7.3 %collective-permute-start.10 = (bf16[16,2176]{1,0:T(8,128)(2,1)S(1)}, bf16[16,2176]{1,0:T(8,128)(2,1)S(1)}, u32[]{:S(2)}, u32[]{:S(2)}) collective-permute-start(bf16[16,2176]{1,0:T(8,128)(2,1)S(1)} %get-tuple-element.30), channel_id=1, source_target_pairs={{0,4},{1,5},{2,6},{3,7},{4,0},{5,1},{6,2},{7,3},{8,12},{9,13},{10,... | collective-permute-start | bytes 208904 | tf_op jit(solution)/shard_map/ppermute | solution.py:26
  35.9 6.2 %collective-permute-start.11 = (bf16[16,2176]{1,0:T(8,128)(2,1)S(1)}, bf16[16,2176]{1,0:T(8,128)(2,1)S(1)}, u32[]{:S(2)}, u32[]{:S(2)}) collective-permute-start(bf16[16,2176]{1,0:T(8,128)(2,1)S(1)} %get-tuple-element.29), channel_id=1, source_target_pairs={{0,2},{1,3},{2,0},{3,1},{4,6},{5,7},{6,4},{7,5},{8,10},{9,11},{10,... | collective-permute-start | bytes 208904 | tf_op jit(solution)/shard_map/ppermute | solution.py:26
  37.1 5.2 %collective-permute-start.9 = (bf16[16,2176]{1,0:T(8,128)(2,1)S(1)}, bf16[16,2176]{1,0:T(8,128)(2,1)S(1)}, u32[]{:S(2)}, u32[]{:S(2)}) collective-permute-start(bf16[16,2176]{1,0:T(8,128)(2,1)S(1)} %get-tuple-element.28), channel_id=1, source_target_pairs={{0,6},{1,7},{2,4},{3,5},{4,2},{5,3},{6,0},{7,1},{8,14},{9,15},{10,... | collective-permute-start | bytes 208904 | tf_op jit(solution)/shard_map/ppermute | solution.py:26
  38.5 8.3 %collective-permute-start.17 = (bf16[16,2048]{1,0:T(8,128)(2,1)S(1)}, bf16[16,2048]{1,0:T(8,128)(2,1)S(1)}, u32[]{:S(2)}, u32[]{:S(2)}) collective-permute-start(bf16[16,2048]{1,0:T(8,128)(2,1)S(1)} %add_convert_fusion.2), channel_id=1, source_target_pairs={{0,24},{8,0},{16,8},{24,16},{1,25},{9,1},{17,9},{25,17},{2,26},{10... | collective-permute-start | bytes 196616 | tf_op jit(solution)/shard_map/ppermute | solution.py:21
  42.4 5.5 %collective-permute-start.12 = (bf16[16,2048]{1,0:T(8,128)(2,1)S(1)}, bf16[16,2048]{1,0:T(8,128)(2,1)S(1)}, u32[]{:S(2)}, u32[]{:S(2)}) collective-permute-start(bf16[16,2048]{1,0:T(8,128)(2,1)S(1)} %slice.72), channel_id=1, source_target_pairs={{0,24},{8,0},{16,8},{24,16},{1,25},{9,1},{17,9},{25,17},{2,26},{10... | collective-permute-start | bytes 196616 | tf_op jit(solution)/shard_map/ppermute | solution.py:21

commit v2 on v1

v2 whole, which is shorter than its diff:
```python
import functools

import jax
import jax.numpy as jnp
from jax import lax
from jax.experimental import pallas as pl
from jax.experimental.pallas import tpu as pltpu
from jax.sharding import PartitionSpec as P

EXPERTS = 8
LANES = 128
CHUNKS = 2
VMEM = pl.BlockSpec(memory_space=pltpu.VMEM)
HBM = pl.BlockSpec(memory_space=pltpu.HBM)


def shifted(array, axis, by):
    peers = lax.axis_size(axis)
    return lax.ppermute(array, axis, [(i, (i + by) % peers) for i in range(peers)])


def swapped(array, bits):
    peers = lax.axis_size("expert")
    return lax.ppermute(array, "expert", [(i, i ^ bits) for i in range(peers)])


def resident(array):
    return pltpu.with_memory_space_constraint(array, pltpu.VMEM)


def streamed(array):
    return pltpu.with_memory_space_constraint(array, pltpu.HBM)


def rows_of(near_ref, far_ref, columns):
    return jnp.concatenate([near_ref[:, columns], far_ref[:, columns]], axis=0)


def flip_kernel(after_ref, mat_ref, out_ref):
    step = 512
    width = mat_ref.shape[1]
    for start in range(0, width, step):
        columns = pl.ds(start, min(step, width - start))
        out_ref[columns, :] = mat_ref[:, columns].T


def products(near_ref, far_ref, flipped_ref):
    rows = rows_of(near_ref, far_ref, pl.ds(0, flipped_ref.shape[0]))
    return jnp.dot(rows, flipped_ref[...], preferred_element_type=jnp.float32)


def pack_kernel(upstream_hbm, routes_hbm, vals_hbm, a_hbm, b_hbm, c_hbm, packed_ref, routes_ref, vals_ref, sems):
    tok_rows, width = upstream_hbm.shape
    copies = [
        pltpu.make_async_copy(routes_hbm, routes_ref, sems.at[0]),
        pltpu.make_async_copy(vals_hbm, vals_ref, sems.at[1]),
        pltpu.make_async_copy(upstream_hbm, packed_ref.at[:, pl.ds(0, width)], sems.at[2]),
    ]
    for copy in copies:
        copy.start()
    for copy in copies[:2]:
        copy.wait()
    expert = lax.broadcasted_iota(jnp.int32, (LANES, tok_rows), 0)
    table = jnp.zeros((LANES, tok_rows), jnp.float32)
    for route in range(routes_ref.shape[0]):
        chosen = routes_ref[route : route + 1, :] == expert
        value = vals_ref[route : route + 1, :].astype(jnp.float32)
        table = table + jnp.where(chosen, value, 0.0)
    packed_ref[:, width:] = jnp.transpose(table).astype(jnp.bfloat16)
    copies[2].wait()


def first_kernel(near_ref, far_ref, gate_ref, up_ref, gate_pre_ref, up_pre_ref):
    gate_pre_ref[...] = products(near_ref, far_ref, gate_ref)
    up_pre_ref[...] = products(near_ref, far_ref, up_ref)


def second_kernel(
    group_size, near_ref, far_ref, down_ref, gate_pre_ref, up_pre_ref, grad_gate_ref, grad_up_ref, score_ref
):
    me = lax.axis_index("expert")
    hidden_grad = products(near_ref, far_ref, down_ref)
    table = rows_of(near_ref, far_ref, pl.ds(down_ref.shape[0], LANES)).astype(jnp.float32)
    column = lax.broadcasted_iota(jnp.int32, table.shape, 1)
    weight = jnp.sum(jnp.where(column == me // group_size, table, 0.0), axis=1, keepdims=True)
    gate_pre = gate_pre_ref[...]
    up_pre = up_pre_ref[...]
    sigmoid_val = 1.0 / (1.0 + jnp.exp(-gate_pre))
    activated = gate_pre * sigmoid_val
    slope = sigmoid_val * (1.0 + gate_pre * (1.0 - sigmoid_val))
    scores = jnp.sum(activated * up_pre * hidden_grad, axis=1, keepdims=True)
    scaled = hidden_grad * weight
    grad_gate_ref[...] = (scaled * up_pre * slope).astype(jnp.bfloat16)
    grad_up_ref[...] = (scaled * activated).astype(jnp.bfloat16)
    scores = jnp.where(weight != 0.0, scores, 0.0)
    high = scores.astype(jnp.bfloat16).astype(jnp.float32)
    low = scores - high
    half = LANES // 2
    score_ref[...] = jnp.where(
        column == me, high, jnp.where(column == me + half, low, 0.0)
    ).astype(jnp.bfloat16)


def third_kernel(first, span, grad_gate_ref, grad_up_ref, gate_ref, up_ref, score_ref, near_ref, far_ref):
    columns = pl.ds(first, span)
    partial_value = jnp.dot(
        grad_gate_ref[...], gate_ref[:, columns], preferred_element_type=jnp.float32
    )
    partial_value = partial_value + jnp.dot(
        grad_up_ref[...], up_ref[:, columns], preferred_element_type=jnp.float32
    )
    partial_value = partial_value.astype(jnp.bfloat16)
    half = near_ref.shape[0]
    near_ref[:, :span] = partial_value[:half]
    far_ref[:, :span] = partial_value[half:]
    if near_ref.shape[1] > span:
        near_ref[:, span:] = score_ref[:half, :]
        far_ref[:, span:] = score_ref[half:, :]


def params(megabytes):
    return pltpu.CompilerParams(vmem_limit_bytes=megabytes * 1024 * 1024)


def on_device(tokens_in, out_grad, expert_ids, gate_weights, w_gate, w_up, w_down):
    inputs = tokens_in[0]
    upstream = out_grad[0]
    routes = expert_ids[0]
    gate_vals = gate_weights[0]
    tok_rows, width = inputs.shape
    hidden = w_gate.shape[1]
    devices = lax.axis_size("expert")
    group_size = devices // EXPERTS
    half = tok_rows * devices // 2
    others = list(range(2, devices, 2))
    top = routes.shape[1]

    def sent(block):
        parts = {0: block}
        for bits in others:
            parts[bits] = swapped(block, bits)
        return [parts[bits] for bits in range(0, devices, 2)]

    parts_x = sent(inputs)
    packed = pl.pallas_call(
        pack_kernel,
        out_shape=jax.ShapeDtypeStruct((tok_rows, width + LANES), jnp.bfloat16),
        in_specs=[HBM] * 6,
        out_specs=VMEM,
        scratch_shapes=[
            pltpu.VMEM((top, tok_rows), jnp.int32),
            pltpu.VMEM((top, tok_rows), jnp.bfloat16),
            pltpu.SemaphoreType.DMA((3,)),
        ],
        compiler_params=params(4),
        cost_estimate=pl.CostEstimate(
            flops=0, bytes_accessed=12 * hidden * width, transcendentals=0
        ),
    )(streamed(upstream), streamed(routes.T), streamed(gate_vals.T), streamed(w_gate[0]), streamed(w_up[0]), streamed(w_down[0]))
    parts_dy = sent(packed)
    gate_mat = resident(w_gate[0])
    up_mat = resident(w_up[0])
    down_mat = resident(w_down[0])
    flip = pl.pallas_call(
        flip_kernel,
        out_shape=jax.ShapeDtypeStruct((width, hidden), jnp.bfloat16),
        in_specs=[VMEM, VMEM],
        out_specs=VMEM,
        compiler_params=params(4),
    )
    after = resident(parts_x[1])
    gate_flipped = resident(flip(after, gate_mat))
    up_flipped = resident(flip(after, up_mat))
    down_flipped = resident(flip(after, down_mat))
    parts_x, gate_flipped, up_flipped = lax.optimization_barrier((parts_x, gate_flipped, up_flipped))
    near_x = jnp.concatenate(parts_x, axis=0)
    far_x = swapped(near_x, 1)
    pre = jax.ShapeDtypeStruct((2 * half, hidden), jnp.float32)
    gate_pre, up_pre = pl.pallas_call(
        first_kernel,
        out_shape=(pre, pre),
        in_specs=[VMEM] * 4,
        out_specs=(VMEM,) * 2,
        compiler_params=params(8),
        cost_estimate=pl.CostEstimate(
            flops=8 * half * hidden * width, bytes_accessed=0, transcendentals=0
        ),
    )(resident(near_x), resident(far_x), gate_flipped, up_flipped)
    parts_dy, down_flipped = lax.optimization_barrier((parts_dy, down_flipped))
    near_dy = jnp.concatenate(parts_dy, axis=0)
    far_dy = swapped(near_dy, 1)
    grads = jax.ShapeDtypeStruct((2 * half, hidden), jnp.bfloat16)
    grad_gate, grad_up, score_lanes = pl.pallas_call(
        functools.partial(second_kernel, group_size),
        out_shape=(grads, grads, jax.ShapeDtypeStruct((2 * half, LANES), jnp.bfloat16)),
        in_specs=[VMEM] * 5,
        out_specs=(VMEM, VMEM, VMEM),
        compiler_params=params(8),
    )(resident(near_dy), resident(far_dy), down_flipped, resident(gate_pre), resident(up_pre))
    passed = []
    score_sum = None
    span = width // CHUNKS
    for chunk in range(CHUNKS):
        extra = LANES if chunk == 0 else 0
        out = jax.ShapeDtypeStruct((half, span + extra), jnp.bfloat16)
        near, far = pl.pallas_call(
            functools.partial(third_kernel, chunk * span, span),
            out_shape=(out, out),
            in_specs=[VMEM] * 5,
            out_specs=(VMEM, VMEM),
            compiler_params=params(8),
        )(resident(grad_gate), resident(grad_up), gate_mat, up_mat, resident(score_lanes))
        merged = near.astype(jnp.float32) + swapped(far, 1).astype(jnp.float32)
        merged = merged.astype(jnp.bfloat16)
        blocks = merged.reshape(devices // 2, tok_rows, span + extra)
        total = blocks[0].astype(jnp.float32)
        for bits in others:
            total = total + swapped(blocks[bits // 2], bits).astype(jnp.float32)
        if extra:
            score_sum = total[:, span:]
        passed.append(shifted(total[:, :span].astype(jnp.bfloat16), "section", -1))
    score_sum = score_sum[:, : LANES // 2] + score_sum[:, LANES // 2 :]
    owner = jnp.arange(LANES // 2, dtype=jnp.int32) // group_size
    mine = routes[:, :, None] == owner[None, None, :]
    grads_route = jnp.sum(jnp.where(mine, score_sum[:, None, :], 0.0), axis=2)
    return (jnp.concatenate(passed, axis=1)[None], grads_route[None])


def solution(mesh):
    return jax.shard_map(
        on_device,
        mesh=mesh,
        in_specs=(P("section", "expert", None),) * 7,
        out_specs=(P("section", "expert", None), P("section", "expert", None)),
        check_vma=False,
    )
```

time: 48.8 us -> 40.7 us (0.83)
  waiting for transfers between devices: 8.41 us -> 2.34 us
  Pallas kernels: 13.7 us -> 11.2 us
  starting transfers between devices: 22.4 us -> 24.2 us
  other arithmetic: 3.11 us -> 1.67 us
    ppermute x16, waiting for transfers between devices: 7.23 us -> 1.16 us  [swapped(): return lax.ppermute(array, 'expert', [(i, i ^ bits) for i in range(peers)])]
    ppermute x16, starting transfers between devices: 15.2 us -> 17.3 us  [swapped(): return lax.ppermute(array, 'expert', [(i, i ^ bits) for i in range(peers)])]
    pallas_call x2 -> x5, Pallas kernels: 9.68 us -> 7.99 us  [the longest x1 1.87 us: on_device(): pl.pallas_call(first_kernel, out_shape=(pre, pre), in_specs=[VMEM] * 4, o...]
    pallas_call x1, Pallas kernels: 2.03 us -> 1.19 us  [on_device(): pl.pallas_call(functools.partial(second_kernel, group_size), out_shape=(g...]
    reduce_sum x1 -> x0, other arithmetic: 0.75 us -> none  [on_device(): jnp.sum(jnp.where(route_hit, gate_vals[:, :, None].astype(jnp.float32), 0...]
    convert_element_type x1 -> x0, other arithmetic: 0.66 us -> none  [on_device(): gate_vals[:, :, None].astype(jnp.float32)]
  transfers between devices with their start and end apart: 18 -> 18, of which waited for: 6 -> 4; matrix products, arithmetic and copies ran while one was open for 5% -> 3% of each run, Pallas kernels for 22% -> 22%
where the time goes in v2:
time: 40.7 us; the launch traced here: 40.5 us
  starting transfers between devices  24.2 us (59%)
  Pallas kernels  11.2 us (28%)
  waiting for transfers between devices  2.34 us (6%)
  other arithmetic  1.67 us (4%)
  between operations  0.92 us (2%)
    ppermute x16, starting transfers between devices, swapped(): return lax.ppermute(array, 'expert', [(i, i ^ bits) for i in range(peers)])  17.3 us
    ppermute x2, starting transfers between devices, shifted(): lax.ppermute(array, axis, [(i, (i + by) % peers) for i in range(peers)])  6.94 us
    pallas_call x2, Pallas kernels, on_device(): pl.pallas_call(functools.partial(third_kernel, chunk * span, span), out_s...  1.99 us
    pallas_call x1, Pallas kernels, on_device(): pl.pallas_call(first_kernel, out_shape=(pre, pre), in_specs=[VMEM] * 4, o...  1.87 us
    pallas_call x1, Pallas kernels, on_device(): down_flipped = resident(flip(after, down_mat))  1.67 us
    pallas_call x1, Pallas kernels, on_device(): up_flipped = resident(flip(after, up_mat))  1.67 us
    pallas_call x1, Pallas kernels, on_device(): gate_flipped = resident(flip(after, gate_mat))  1.67 us
    pallas_call x1, Pallas kernels, on_device(): pl.pallas_call(functools.partial(second_kernel, group_size), out_shape=(g...  1.19 us
  transfers between devices with their start and end apart: 18, of which 4 were waited for; matrix products, arithmetic and copies ran while one was open for 3% of the time, Pallas kernels for 22%

profile of v2, /device:TPU:0, one launch (start us, length us, event | category | flops | bytes accessed | tf_op | source)
XLA Modules:
  0.0 40.5 jit_solution(8873068816975837432)
XLA Ops:
  0.6 3.0 %collective-permute-start.3 = (bf16[16,4096]{1,0:T(8,128)(2,1)}, bf16[16,4096]{1,0:T(8,128)(2,1)S(1)}, u32[]{:S(2)}, u32[]{:S(2)}) collective-permute-start(bf16[16,4096]{1,0:T(8,128)(2,1)} %bitcast.29), channel_id=1, source_target_pairs={{0,2},{1,3},{2,0},{3,1},{4,6},{5,7},{6,4},{7,5},{8,10},{9,11},{10,... | collective-permute-start | bytes 393224 | tf_op jit(solution)/shard_map/ppermute | solution.py:24
  3.6 1.5 %collective-permute-start.5 = (bf16[16,4096]{1,0:T(8,128)(2,1)}, bf16[16,4096]{1,0:T(8,128)(2,1)S(1)}, u32[]{:S(2)}, u32[]{:S(2)}) collective-permute-start(bf16[16,4096]{1,0:T(8,128)(2,1)} %bitcast.30), channel_id=1, source_target_pairs={{0,4},{1,5},{2,6},{3,7},{4,0},{5,1},{6,2},{7,3},{8,12},{9,13},{10,... | collective-permute-start | bytes 393224 | tf_op jit(solution)/shard_map/ppermute | solution.py:24
  5.2 1.1 %shard_map.86 = bf16[16,4224]{1,0:T(8,128)(2,1)S(1)} custom-call(bf16[16,4096]{1,0:T(8,128)(2,1)} %bitcast.28, s32[2,16]{1,0:T(2,128)} %bitcast.33, bf16[2,16]{1,0:T(2,128)(2,1)} %bitcast.36, bf16[768,4096]{1,0:T(8,128)(2,1)} %bitcast.14, bf16[768,4096]{1,0:T(8,128)(2,1)} %bitcast.18, bf16[768,4096]{1,0:T(8,128)(2,1)} %bitcast.24), custom_call_target="tpu_custom_call" | custom-call | bytes 37748736 | tf_op jit(solution)/shard_map/pallas_call | solution.py:145
  6.3 2.0 %collective-permute-start = (bf16[16,4224]{1,0:T(8,128)(2,1)S(1)}, bf16[16,4224]{1,0:T(8,128)(2,1)S(1)}, u32[]{:S(2)}, u32[]{:S(2)}) collective-permute-start(bf16[16,4224]{1,0:T(8,128)(2,1)S(1)} %shard_map.86), channel_id=1, source_target_pairs={{0,2},{1,3},{2,0},{3,1},{4,6},{5,7},{6,4},{7,5},{8,10},{9,11},{10,... | collective-permute-start | bytes 405512 | tf_op jit(solution)/shard_map/ppermute | solution.py:24
  8.3 1.5 %collective-permute-start.1 = (bf16[16,4224]{1,0:T(8,128)(2,1)S(1)}, bf16[16,4224]{1,0:T(8,128)(2,1)S(1)}, u32[]{:S(2)}, u32[]{:S(2)}) collective-permute-start(bf16[16,4224]{1,0:T(8,128)(2,1)S(1)} %shard_map.86), channel_id=1, source_target_pairs={{0,4},{1,5},{2,6},{3,7},{4,0},{5,1},{6,2},{7,3},{8,12},{9,13},{10,... | collective-permute-start | bytes 405512 | tf_op jit(solution)/shard_map/ppermute | solution.py:24
  9.8 1.3 %collective-permute-start.2 = (bf16[16,4224]{1,0:T(8,128)(2,1)S(1)}, bf16[16,4224]{1,0:T(8,128)(2,1)S(1)}, u32[]{:S(2)}, u32[]{:S(2)}) collective-permute-start(bf16[16,4224]{1,0:T(8,128)(2,1)S(1)} %shard_map.86), channel_id=1, source_target_pairs={{0,6},{1,7},{2,4},{3,5},{4,2},{5,3},{6,0},{7,1},{8,14},{9,15},{10,... | collective-permute-start | bytes 405512 | tf_op jit(solution)/shard_map/ppermute | solution.py:24
  11.2 1.7 %shard_map.88.gate_ref = bf16[4096,768]{1,0:T(8,128)(2,1)S(1)} custom-call(bf16[16,4096]{1,0:T(8,128)(2,1)S(1)} %collective-permute-done.3.after_ref, bf16[768,4096]{1,0:T(8,128)(2,1)S(1)} %bitcast.15), custom_call_target="tpu_custom_call" | custom-call | tf_op jit(solution)/shard_map/pallas_call | solution.py:172
  12.9 1.7 %shard_map.89.up_ref = bf16[4096,768]{1,0:T(8,128)(2,1)S(1)} custom-call(bf16[16,4096]{1,0:T(8,128)(2,1)S(1)} %collective-permute-done.3.after_ref, bf16[768,4096]{1,0:T(8,128)(2,1)S(1)} %bitcast.21), custom_call_target="tpu_custom_call" | custom-call | tf_op jit(solution)/shard_map/pallas_call | solution.py:173
  14.7 0.1 collective-permute-start.7
  14.8 1.7 %shard_map.87.down_ref = bf16[4096,768]{1,0:T(8,128)(2,1)S(1)} custom-call(bf16[16,4096]{1,0:T(8,128)(2,1)S(1)} %collective-permute-done.3.after_ref, bf16[768,4096]{1,0:T(8,128)(2,1)S(1)} %bitcast.27), custom_call_target="tpu_custom_call" | custom-call | tf_op jit(solution)/shard_map/pallas_call | solution.py:174
  16.5 0.9 %collective-permute-done.1 = bf16[16,4224]{1,0:T(8,128)(2,1)S(1)} collective-permute-done((bf16[16,4224]{1,0:T(8,128)(2,1)S(1)}, bf16[16,4224]{1,0:T(8,128)(2,1)S(1)}, u32[]{:S(2)}, u32[]{:S(2)}) %collective-permute-start.1) | collective-permute-done | bytes 135200 | tf_op jit(solution)/shard_map/ppermute | solution.py:24
  17.5 0.1 collective-permute-start.4
  17.6 1.9 %shard_map.90 = (f32[128,768]{1,0:T(8,128)S(1)}, f32[128,768]{1,0:T(8,128)S(1)}) custom-call(bf16[64,4096]{1,0:T(8,128)(2,1)S(1)} %constant_dynamic-update-slice_fusion.4.near_ref, bf16[64,4096]{1,0:T(8,128)(2,1)S(1)} %collective-permute-done.7.far_ref, bf16[4096,768]{1,0:T(8,128)(2,1)S(1)} %shard_map.88.gate_ref, bf16[4096,768]{1,0:T(8,128)(2,1)S(1)} %shard_map.89.up_ref), custom_call_target="tpu_custom_call" | custom-call | flops 1610612736 | tf_op jit(solution)/shard_map/pallas_call | solution.py:179
  19.5 1.2 %shard_map.91 = (bf16[128,768]{1,0:T(8,128)(2,1)S(1)}, bf16[128,768]{1,0:T(8,128)(2,1)S(1)}, bf16[128,128]{1,0:T(8,128)(2,1)S(1)}) custom-call(bf16[64,4224]{1,0:T(8,128)(2,1)S(1)} %constant_dynamic-update-slice_fusion.near_ref, bf16[64,4224]{1,0:T(8,128)(2,1)S(1)} %collective-permute-done.4.far_ref, bf16[4096,768]{1,0:T(8,128)(2,1)S(1)} %shard_map.87.down_ref, ...), custom_call_target="tpu_custom_call" | custom-call | tf_op jit(solution)/shard_map/pallas_call | solution.py:193
  20.7 1.0 %shard_map.93 = (bf16[64,2048]{1,0:T(8,128)(2,1)S(1)}, bf16[64,2048]{1,0:T(8,128)(2,1)S(1)}) custom-call(bf16[128,768]{1,0:T(8,128)(2,1)S(1)} %get-tuple-element.35.grad_gate_ref, bf16[128,768]{1,0:T(8,128)(2,1)S(1)} %get-tuple-element.36.grad_up_ref, bf16[768,4096]{1,0:T(8,128)(2,1)S(1)} %bitcast.16, bf16[768,4096]{1,0:T(8,128)(2,1)S(1)} %bitcast.22, ...), custom_call_target="tpu_custom_call" | custom-call | tf_op jit(solution)/shard_map/pallas_call | solution.py:206
  21.7 0.5 %collective-permute-start.13 = (bf16[64,2048]{1,0:T(8,128)(2,1)S(1)}, bf16[64,2048]{1,0:T(8,128)(2,1)S(1)}, u32[]{:S(2)}, u32[]{:S(2)}) collective-permute-start(bf16[64,2048]{1,0:T(8,128)(2,1)S(1)} %get-tuple-element.41), channel_id=1, source_target_pairs={{0,1},{1,0},{2,3},{3,2},{4,5},{5,4},{6,7},{7,6},{8,9},{9,8},{10,11... | collective-permute-start | bytes 786440 | tf_op jit(solution)/shard_map/ppermute | solution.py:24
  22.2 1.0 %shard_map.92 = (bf16[64,2176]{1,0:T(8,128)(2,1)S(1)}, bf16[64,2176]{1,0:T(8,128)(2,1)S(1)}) custom-call(bf16[128,768]{1,0:T(8,128)(2,1)S(1)} %get-tuple-element.35.grad_gate_ref, bf16[128,768]{1,0:T(8,128)(2,1)S(1)} %get-tuple-element.36.grad_up_ref, bf16[768,4096]{1,0:T(8,128)(2,1)S(1)} %bitcast.17, bf16[768,4096]{1,0:T(8,128)(2,1)S(1)} %bitcast.23, ...), custom_call_target="tpu_custom_call" | custom-call | tf_op jit(solution)/shard_map/pallas_call | solution.py:206
  23.2 0.1 collective-permute-start.8
  23.5 1.3 %collective-permute-start.14 = (bf16[16,2048]{1,0:T(8,128)(2,1)S(1)}, bf16[16,2048]{1,0:T(8,128)(2,1)S(1)}, u32[]{:S(2)}, u32[]{:S(2)}) collective-permute-start(bf16[16,2048]{1,0:T(8,128)(2,1)S(1)} %get-tuple-element.45), channel_id=1, source_target_pairs={{0,2},{1,3},{2,0},{3,1},{4,6},{5,7},{6,4},{7,5},{8,10},{9,11},{10,... | collective-permute-start | bytes 196616 | tf_op jit(solution)/shard_map/ppermute | solution.py:24
  24.8 0.8 %collective-permute-start.15 = (bf16[16,2048]{1,0:T(8,128)(2,1)S(1)}, bf16[16,2048]{1,0:T(8,128)(2,1)S(1)}, u32[]{:S(2)}, u32[]{:S(2)}) collective-permute-start(bf16[16,2048]{1,0:T(8,128)(2,1)S(1)} %get-tuple-element.47), channel_id=1, source_target_pairs={{0,4},{1,5},{2,6},{3,7},{4,0},{5,1},{6,2},{7,3},{8,12},{9,13},{10,... | collective-permute-start | bytes 196616 | tf_op jit(solution)/shard_map/ppermute | solution.py:24
  25.6 1.4 %collective-permute-start.16 = (bf16[16,2048]{1,0:T(8,128)(2,1)S(1)}, bf16[16,2048]{1,0:T(8,128)(2,1)S(1)}, u32[]{:S(2)}, u32[]{:S(2)}) collective-permute-start(bf16[16,2048]{1,0:T(8,128)(2,1)S(1)} %get-tuple-element.46), channel_id=1, source_target_pairs={{0,6},{1,7},{2,4},{3,5},{4,2},{5,3},{6,0},{7,1},{8,14},{9,15},{10,... | collective-permute-start | bytes 196616 | tf_op jit(solution)/shard_map/ppermute | solution.py:24
  27.1 0.1 add_convert_fusion
  27.2 1.6 %collective-permute-start.10 = (bf16[16,2176]{1,0:T(8,128)(2,1)S(1)}, bf16[16,2176]{1,0:T(8,128)(2,1)S(1)}, u32[]{:S(2)}, u32[]{:S(2)}) collective-permute-start(bf16[16,2176]{1,0:T(8,128)(2,1)S(1)} %get-tuple-element.44), channel_id=1, source_target_pairs={{0,4},{1,5},{2,6},{3,7},{4,0},{5,1},{6,2},{7,3},{8,12},{9,13},{10,... | collective-permute-start | bytes 208904 | tf_op jit(solution)/shard_map/ppermute | solution.py:24
  28.7 1.2 %collective-permute-start.11 = (bf16[16,2176]{1,0:T(8,128)(2,1)S(1)}, bf16[16,2176]{1,0:T(8,128)(2,1)S(1)}, u32[]{:S(2)}, u32[]{:S(2)}) collective-permute-start(bf16[16,2176]{1,0:T(8,128)(2,1)S(1)} %get-tuple-element.43), channel_id=1, source_target_pairs={{0,6},{1,7},{2,4},{3,5},{4,2},{5,3},{6,0},{7,1},{8,14},{9,15},{10,... | collective-permute-start | bytes 208904 | tf_op jit(solution)/shard_map/ppermute | solution.py:24
  29.9 0.8 %collective-permute-start.9 = (bf16[16,2176]{1,0:T(8,128)(2,1)S(1)}, bf16[16,2176]{1,0:T(8,128)(2,1)S(1)}, u32[]{:S(2)}, u32[]{:S(2)}) collective-permute-start(bf16[16,2176]{1,0:T(8,128)(2,1)S(1)} %get-tuple-element.42), channel_id=1, source_target_pairs={{0,2},{1,3},{2,0},{3,1},{4,6},{5,7},{6,4},{7,5},{8,10},{9,11},{10,... | collective-permute-start | bytes 208904 | tf_op jit(solution)/shard_map/ppermute | solution.py:24
  30.7 0.1 collective-permute-done.16
  30.9 3.7 %collective-permute-start.17 = (bf16[16,2048]{1,0:T(8,128)(2,1)S(1)}, bf16[16,2048]{1,0:T(8,128)(2,1)S(1)}, u32[]{:S(2)}, u32[]{:S(2)}) collective-permute-start(bf16[16,2048]{1,0:T(8,128)(2,1)S(1)} %add_convert_fusion.2), channel_id=1, source_target_pairs={{0,24},{8,0},{16,8},{24,16},{1,25},{9,1},{17,9},{25,17},{2,26},{10... | collective-permute-start | bytes 196616 | tf_op jit(solution)/shard_map/ppermute | solution.py:19
  34.6 0.1 slice_add_fusion
  34.7 3.3 %collective-permute-start.12 = (bf16[16,2048]{1,0:T(8,128)(2,1)S(1)}, bf16[16,2048]{1,0:T(8,128)(2,1)S(1)}, u32[]{:S(2)}, u32[]{:S(2)}) collective-permute-start(bf16[16,2048]{1,0:T(8,128)(2,1)S(1)} %slice.72), channel_id=1, source_target_pairs={{0,24},{8,0},{16,8},{24,16},{1,25},{9,1},{17,9},{25,17},{2,26},{10... | collective-permute-start | bytes 196616 | tf_op jit(solution)/shard_map/ppermute | solution.py:19
  38.0 0.7 %select_reduce_fusion = f32[16,2]{0,1:T(2,128)} fusion(f32[16,64]{1,0:T(8,128)S(1)} %slice_add_fusion, s32[16,2]{0,1:T(2,128)S(1)} %bitcast.34), kind=kLoop, calls=%fused_computation.14 | loop fusion | flops 6112 | bytes 4352 | tf_op jit(solution)/shard_map/reduce_sum | solution.py:225
  38.7 1.2 %collective-permute-done.12 = bf16[16,2048]{1,0:T(8,128)(2,1)S(1)} collective-permute-done((bf16[16,2048]{1,0:T(8,128)(2,1)S(1)}, bf16[16,2048]{1,0:T(8,128)(2,1)S(1)}, u32[]{:S(2)}, u32[]{:S(2)}) %collective-permute-start.12) | collective-permute-done | bytes 65568 | tf_op jit(solution)/shard_map/ppermute | solution.py:19
  39.9 0.7 %maximum_bitcast_fusion = bf16[1,16,4096]{2,1,0:T(8,128)(2,1)} fusion(bf16[16,2048]{1,0:T(8,128)(2,1)S(1)} %collective-permute-done.17, bf16[16,2048]{1,0:T(8,128)(2,1)S(1)} %collective-permute-done.12), kind=kLoop, calls=%fused_computation.4 | loop fusion | flops 262144 | bytes 262144 | tf_op jit(solution)/shard_map/broadcast_in_dim | solution.py:226
  (46 shorter events, 0.5 us)
Async XLA Ops:
  0.6 9.2 %collective-permute-start.3 = (bf16[16,4096]{1,0:T(8,128)(2,1)}, bf16[16,4096]{1,0:T(8,128)(2,1)S(1)}, u32[]{:S(2)}, u32[]{:S(2)}) collective-permute-start(bf16[16,4096]{1,0:T(8,128)(2,1)} %bitcast.29), channel_id=1, source_target_pairs={{0,2},{1,3},{2,0},{3,1},{4,6},{5,7},{6,4},{7,5},{8,10},{9,11},{10,... | collective-permute-start | bytes 393224 | tf_op jit(solution)/shard_map/ppermute | solution.py:24
  3.6 11.0 %collective-permute-start.5 = (bf16[16,4096]{1,0:T(8,128)(2,1)}, bf16[16,4096]{1,0:T(8,128)(2,1)S(1)}, u32[]{:S(2)}, u32[]{:S(2)}) collective-permute-start(bf16[16,4096]{1,0:T(8,128)(2,1)} %bitcast.30), channel_id=1, source_target_pairs={{0,4},{1,5},{2,6},{3,7},{4,0},{5,1},{6,2},{7,3},{8,12},{9,13},{10,... | collective-permute-start | bytes 393224 | tf_op jit(solution)/shard_map/ppermute | solution.py:24
  5.2 9.5 %collective-permute-start.6 = (bf16[16,4096]{1,0:T(8,128)(2,1)}, bf16[16,4096]{1,0:T(8,128)(2,1)S(1)}, u32[]{:S(2)}, u32[]{:S(2)}) collective-permute-start(bf16[16,4096]{1,0:T(8,128)(2,1)} %bitcast.31), channel_id=1, source_target_pairs={{0,6},{1,7},{2,4},{3,5},{4,2},{5,3},{6,0},{7,1},{8,14},{9,15},{10,... | collective-permute-start | bytes 393224 | tf_op jit(solution)/shard_map/ppermute | solution.py:24
  5.2 7.7 %slice-start = ((s8[6291456]{0:T(1024)(128)(4,1)}), s8[4194304]{0:T(1024)(128)(4,1)S(1)}, s32[]{:S(2)}) async-start(s8[6291456]{0:T(1024)(128)(4,1)} %bitcast.19), calls=%async_computation | async-start | bytes 8388608
  5.2 6.0 %copy-start = (bf16[1,768,4096]{2,1,0:T(8,128)(2,1)S(1)}, bf16[1,768,4096]{2,1,0:T(8,128)(2,1)}, u32[]{:S(2)}) copy-start(bf16[1,768,4096]{2,1,0:T(8,128)(2,1)} %param.11) | copy-start | bytes 18874372
  5.2 7.7 %slice-start.1 = ((s8[6291456]{0:T(1024)(128)(4,1)}), s8[2097152]{0:T(1024)(128)(4,1)S(1)}, s32[]{:S(2)}) async-start(s8[6291456]{0:T(1024)(128)(4,1)} %bitcast.19), calls=%async_computation.1 | async-start | bytes 4194304
  6.3 10.2 %collective-permute-start = (bf16[16,4224]{1,0:T(8,128)(2,1)S(1)}, bf16[16,4224]{1,0:T(8,128)(2,1)S(1)}, u32[]{:S(2)}, u32[]{:S(2)}) collective-permute-start(bf16[16,4224]{1,0:T(8,128)(2,1)S(1)} %shard_map.86), channel_id=1, source_target_pairs={{0,2},{1,3},{2,0},{3,1},{4,6},{5,7},{6,4},{7,5},{8,10},{9,11},{10,... | collective-permute-start | bytes 405512 | tf_op jit(solution)/shard_map/ppermute | solution.py:24
  8.3 9.1 %collective-permute-start.1 = (bf16[16,4224]{1,0:T(8,128)(2,1)S(1)}, bf16[16,4224]{1,0:T(8,128)(2,1)S(1)}, u32[]{:S(2)}, u32[]{:S(2)}) collective-permute-start(bf16[16,4224]{1,0:T(8,128)(2,1)S(1)} %shard_map.86), channel_id=1, source_target_pairs={{0,4},{1,5},{2,6},{3,7},{4,0},{5,1},{6,2},{7,3},{8,12},{9,13},{10,... | collective-permute-start | bytes 405512 | tf_op jit(solution)/shard_map/ppermute | solution.py:24
  9.8 7.6 %collective-permute-start.2 = (bf16[16,4224]{1,0:T(8,128)(2,1)S(1)}, bf16[16,4224]{1,0:T(8,128)(2,1)S(1)}, u32[]{:S(2)}, u32[]{:S(2)}) collective-permute-start(bf16[16,4224]{1,0:T(8,128)(2,1)S(1)} %shard_map.86), channel_id=1, source_target_pairs={{0,6},{1,7},{2,4},{3,5},{4,2},{5,3},{6,0},{7,1},{8,14},{9,15},{10,... | collective-permute-start | bytes 405512 | tf_op jit(solution)/shard_map/ppermute | solution.py:24
  11.2 3.6 %slice-start.2 = ((s8[6291456]{0:T(1024)(128)(4,1)}), s8[4194304]{0:T(1024)(128)(4,1)S(1)}, s32[]{:S(2)}) async-start(s8[6291456]{0:T(1024)(128)(4,1)} %bitcast.25), calls=%async_computation.2 | async-start | bytes 8388608
  12.9 1.7 %copy-start.1 = (bf16[1,16,4096]{2,1,0:T(8,128)(2,1)S(1)}, bf16[1,16,4096]{2,1,0:T(8,128)(2,1)}, u32[]{:S(2)}) copy-start(bf16[1,16,4096]{2,1,0:T(8,128)(2,1)} %param.7) | copy-start | bytes 393220
  12.9 1.9 %slice-start.3 = ((s8[6291456]{0:T(1024)(128)(4,1)}), s8[2097152]{0:T(1024)(128)(4,1)S(1)}, s32[]{:S(2)}) async-start(s8[6291456]{0:T(1024)(128)(4,1)} %bitcast.25), calls=%async_computation.3 | async-start | bytes 4194304
  14.7 2.9 %collective-permute-start.7 = (bf16[64,4096]{1,0:T(8,128)(2,1)S(1)}, bf16[64,4096]{1,0:T(8,128)(2,1)S(1)}, u32[]{:S(2)}, u32[]{:S(2)}) collective-permute-start(bf16[64,4096]{1,0:T(8,128)(2,1)S(1)} %constant_dynamic-update-slice_fusion.4.near_ref), channel_id=1, source_target_pairs={{0,1},{1,0},{2,3},{3,2},{4,5},{5,4},{6,7},{7,6},{8,9},{9,8},{10,11... | collective-permute-start | bytes 1572872 | tf_op jit(solution)/shard_map/ppermute | solution.py:24
  17.5 2.0 %collective-permute-start.4 = (bf16[64,4224]{1,0:T(8,128)(2,1)S(1)}, bf16[64,4224]{1,0:T(8,128)(2,1)S(1)}, u32[]{:S(2)}, u32[]{:S(2)}) collective-permute-start(bf16[64,4224]{1,0:T(8,128)(2,1)S(1)} %constant_dynamic-update-slice_fusion.near_ref), channel_id=1, source_target_pairs={{0,1},{1,0},{2,3},{3,2},{4,5},{5,4},{6,7},{7,6},{8,9},{9,8},{10,11... | collective-permute-start | bytes 1622024 | tf_op jit(solution)/shard_map/ppermute | solution.py:24
  21.7 16.3 %copy-start.2 = (s32[1,16,2]{1,2,0:T(2,128)S(1)}, s32[1,16,2]{1,2,0:T(2,128)}, u32[]{:S(2)}) copy-start(s32[1,16,2]{1,2,0:T(2,128)} %param.9) | copy-start | bytes 388
  21.7 1.7 %collective-permute-start.13 = (bf16[64,2048]{1,0:T(8,128)(2,1)S(1)}, bf16[64,2048]{1,0:T(8,128)(2,1)S(1)}, u32[]{:S(2)}, u32[]{:S(2)}) collective-permute-start(bf16[64,2048]{1,0:T(8,128)(2,1)S(1)} %get-tuple-element.41), channel_id=1, source_target_pairs={{0,1},{1,0},{2,3},{3,2},{4,5},{5,4},{6,7},{7,6},{8,9},{9,8},{10,11... | collective-permute-start | bytes 786440 | tf_op jit(solution)/shard_map/ppermute | solution.py:24
  23.2 3.8 %collective-permute-start.8 = (bf16[64,2176]{1,0:T(8,128)(2,1)S(1)}, bf16[64,2176]{1,0:T(8,128)(2,1)S(1)}, u32[]{:S(2)}, u32[]{:S(2)}) collective-permute-start(bf16[64,2176]{1,0:T(8,128)(2,1)S(1)} %get-tuple-element.39), channel_id=1, source_target_pairs={{0,1},{1,0},{2,3},{3,2},{4,5},{5,4},{6,7},{7,6},{8,9},{9,8},{10,11... | collective-permute-start | bytes 835592 | tf_op jit(solution)/shard_map/ppermute | solution.py:24
  23.5 6.4 %collective-permute-start.14 = (bf16[16,2048]{1,0:T(8,128)(2,1)S(1)}, bf16[16,2048]{1,0:T(8,128)(2,1)S(1)}, u32[]{:S(2)}, u32[]{:S(2)}) collective-permute-start(bf16[16,2048]{1,0:T(8,128)(2,1)S(1)} %get-tuple-element.45), channel_id=1, source_target_pairs={{0,2},{1,3},{2,0},{3,1},{4,6},{5,7},{6,4},{7,5},{8,10},{9,11},{10,... | collective-permute-start | bytes 196616 | tf_op jit(solution)/shard_map/ppermute | solution.py:24
  24.8 5.9 %collective-permute-start.15 = (bf16[16,2048]{1,0:T(8,128)(2,1)S(1)}, bf16[16,2048]{1,0:T(8,128)(2,1)S(1)}, u32[]{:S(2)}, u32[]{:S(2)}) collective-permute-start(bf16[16,2048]{1,0:T(8,128)(2,1)S(1)} %get-tuple-element.47), channel_id=1, source_target_pairs={{0,4},{1,5},{2,6},{3,7},{4,0},{5,1},{6,2},{7,3},{8,12},{9,13},{10,... | collective-permute-start | bytes 196616 | tf_op jit(solution)/shard_map/ppermute | solution.py:24
  25.6 5.2 %collective-permute-start.16 = (bf16[16,2048]{1,0:T(8,128)(2,1)S(1)}, bf16[16,2048]{1,0:T(8,128)(2,1)S(1)}, u32[]{:S(2)}, u32[]{:S(2)}) collective-permute-start(bf16[16,2048]{1,0:T(8,128)(2,1)S(1)} %get-tuple-element.46), channel_id=1, source_target_pairs={{0,6},{1,7},{2,4},{3,5},{4,2},{5,3},{6,0},{7,1},{8,14},{9,15},{10,... | collective-permute-start | bytes 196616 | tf_op jit(solution)/shard_map/ppermute | solution.py:24
  27.2 7.4 %collective-permute-start.10 = (bf16[16,2176]{1,0:T(8,128)(2,1)S(1)}, bf16[16,2176]{1,0:T(8,128)(2,1)S(1)}, u32[]{:S(2)}, u32[]{:S(2)}) collective-permute-start(bf16[16,2176]{1,0:T(8,128)(2,1)S(1)} %get-tuple-element.44), channel_id=1, source_target_pairs={{0,4},{1,5},{2,6},{3,7},{4,0},{5,1},{6,2},{7,3},{8,12},{9,13},{10,... | collective-permute-start | bytes 208904 | tf_op jit(solution)/shard_map/ppermute | solution.py:24
  28.7 5.8 %collective-permute-start.11 = (bf16[16,2176]{1,0:T(8,128)(2,1)S(1)}, bf16[16,2176]{1,0:T(8,128)(2,1)S(1)}, u32[]{:S(2)}, u32[]{:S(2)}) collective-permute-start(bf16[16,2176]{1,0:T(8,128)(2,1)S(1)} %get-tuple-element.43), channel_id=1, source_target_pairs={{0,6},{1,7},{2,4},{3,5},{4,2},{5,3},{6,0},{7,1},{8,14},{9,15},{10,... | collective-permute-start | bytes 208904 | tf_op jit(solution)/shard_map/ppermute | solution.py:24
  29.9 4.6 %collective-permute-start.9 = (bf16[16,2176]{1,0:T(8,128)(2,1)S(1)}, bf16[16,2176]{1,0:T(8,128)(2,1)S(1)}, u32[]{:S(2)}, u32[]{:S(2)}) collective-permute-start(bf16[16,2176]{1,0:T(8,128)(2,1)S(1)} %get-tuple-element.42), channel_id=1, source_target_pairs={{0,2},{1,3},{2,0},{3,1},{4,6},{5,7},{6,4},{7,5},{8,10},{9,11},{10,... | collective-permute-start | bytes 208904 | tf_op jit(solution)/shard_map/ppermute | solution.py:24
  30.9 7.8 %collective-permute-start.17 = (bf16[16,2048]{1,0:T(8,128)(2,1)S(1)}, bf16[16,2048]{1,0:T(8,128)(2,1)S(1)}, u32[]{:S(2)}, u32[]{:S(2)}) collective-permute-start(bf16[16,2048]{1,0:T(8,128)(2,1)S(1)} %add_convert_fusion.2), channel_id=1, source_target_pairs={{0,24},{8,0},{16,8},{24,16},{1,25},{9,1},{17,9},{25,17},{2,26},{10... | collective-permute-start | bytes 196616 | tf_op jit(solution)/shard_map/ppermute | solution.py:19
  34.7 5.2 %collective-permute-start.12 = (bf16[16,2048]{1,0:T(8,128)(2,1)S(1)}, bf16[16,2048]{1,0:T(8,128)(2,1)S(1)}, u32[]{:S(2)}, u32[]{:S(2)}) collective-permute-start(bf16[16,2048]{1,0:T(8,128)(2,1)S(1)} %slice.72), channel_id=1, source_target_pairs={{0,24},{8,0},{16,8},{24,16},{1,25},{9,1},{17,9},{25,17},{2,26},{10... | collective-permute-start | bytes 196616 | tf_op jit(solution)/shard_map/ppermute | solution.py:19

commit v3 on v2

--- a/solution.py
+++ b/solution.py
@@ -49,17 +49,15 @@
     return jnp.dot(rows, flipped_ref[...], preferred_element_type=jnp.float32)
 
 
-def pack_kernel(upstream_hbm, routes_hbm, vals_hbm, a_hbm, b_hbm, c_hbm, packed_ref, routes_ref, vals_ref, sems):
+def pack_kernel(upstream_hbm, routes_hbm, vals_ref, a_hbm, b_hbm, c_hbm, packed_ref, routes_ref, sems):
     tok_rows, width = upstream_hbm.shape
     copies = [
         pltpu.make_async_copy(routes_hbm, routes_ref, sems.at[0]),
-        pltpu.make_async_copy(vals_hbm, vals_ref, sems.at[1]),
-        pltpu.make_async_copy(upstream_hbm, packed_ref.at[:, pl.ds(0, width)], sems.at[2]),
+        pltpu.make_async_copy(upstream_hbm, packed_ref.at[:, pl.ds(0, width)], sems.at[1]),
     ]
     for copy in copies:
         copy.start()
-    for copy in copies[:2]:
-        copy.wait()
+    copies[0].wait()
     expert = lax.broadcasted_iota(jnp.int32, (LANES, tok_rows), 0)
     table = jnp.zeros((LANES, tok_rows), jnp.float32)
     for route in range(routes_ref.shape[0]):
@@ -67,7 +65,7 @@
         value = vals_ref[route : route + 1, :].astype(jnp.float32)
         table = table + jnp.where(chosen, value, 0.0)
     packed_ref[:, width:] = jnp.transpose(table).astype(jnp.bfloat16)
-    copies[2].wait()
+    copies[1].wait()
 
 
 def first_kernel(near_ref, far_ref, gate_ref, up_ref, gate_pre_ref, up_pre_ref):
@@ -145,18 +143,17 @@
     packed = pl.pallas_call(
         pack_kernel,
         out_shape=jax.ShapeDtypeStruct((tok_rows, width + LANES), jnp.bfloat16),
-        in_specs=[HBM] * 6,
+        in_specs=[HBM, HBM, VMEM, HBM, HBM, HBM],
         out_specs=VMEM,
         scratch_shapes=[
             pltpu.VMEM((top, tok_rows), jnp.int32),
-            pltpu.VMEM((top, tok_rows), jnp.bfloat16),
-            pltpu.SemaphoreType.DMA((3,)),
+            pltpu.SemaphoreType.DMA((2,)),
         ],
         compiler_params=params(4),
         cost_estimate=pl.CostEstimate(
             flops=0, bytes_accessed=12 * hidden * width, transcendentals=0
         ),
-    )(streamed(upstream), streamed(routes.T), streamed(gate_vals.T), streamed(w_gate[0]), streamed(w_up[0]), streamed(w_down[0]))
+    )(streamed(upstream), streamed(routes.T), gate_vals.T, streamed(w_gate[0]), streamed(w_up[0]), streamed(w_down[0]))
     parts_dy = sent(packed)
     gate_mat = resident(w_gate[0])
     up_mat = resident(w_up[0])

time: 40.7 us -> 40.7 us (level)
  starting transfers between devices: 24.2 us -> 22.6 us
  local copies, waits for them, and re-layouts: 0.18 us -> 0.99 us
  waiting for transfers between devices: 2.34 us -> 2.99 us
    ppermute x16, starting transfers between devices: 17.3 us -> 16.3 us  [swapped(): return lax.ppermute(array, 'expert', [(i, i ^ bits) for i in range(peers)])]
    unnamed x20 -> x22, local copies, waits for them, and re-layouts: 0.11 us -> 0.92 us
    ppermute x2, starting transfers between devices: 6.94 us -> 6.29 us  [shifted(): lax.ppermute(array, axis, [(i, (i + by) % peers) for i in range(peers)])]
    ppermute x16, waiting for transfers between devices: 1.16 us -> 1.8 us  [swapped(): return lax.ppermute(array, 'expert', [(i, i ^ bits) for i in range(peers)])]
  transfers between devices with their start and end apart: 18 -> 18, of which waited for: 4 -> 4; matrix products, arithmetic and copies ran while one was open for 3% -> 3% of each run, Pallas kernels for 22% -> 23%
where the time goes in v3:
time: 40.7 us; the launch traced here: 40.5 us
  starting transfers between devices  22.6 us (56%)
  Pallas kernels  11.4 us (28%)
  waiting for transfers between devices  2.99 us (7%)
  other arithmetic  1.67 us (4%)
  local copies, waits for them, and re-layouts  0.99 us (2%)
  between operations  0.92 us (2%)
    ppermute x16, starting transfers between devices, swapped(): return lax.ppermute(array, 'expert', [(i, i ^ bits) for i in range(peers)])  16.3 us
    ppermute x2, starting transfers between devices, shifted(): lax.ppermute(array, axis, [(i, (i + by) % peers) for i in range(peers)])  6.29 us
    pallas_call x2, Pallas kernels, on_device(): pl.pallas_call(functools.partial(third_kernel, chunk * span, span), out_s...  1.99 us
    pallas_call x1, Pallas kernels, on_device(): pl.pallas_call(first_kernel, out_shape=(pre, pre), in_specs=[VMEM] * 4, o...  1.87 us
    ppermute x16, waiting for transfers between devices, swapped(): return lax.ppermute(array, 'expert', [(i, i ^ bits) for i in range(peers)])  1.8 us
    pallas_call x1, Pallas kernels, on_device(): up_flipped = resident(flip(after, up_mat))  1.67 us
    pallas_call x1, Pallas kernels, on_device(): down_flipped = resident(flip(after, down_mat))  1.67 us
    pallas_call x1, Pallas kernels, on_device(): gate_flipped = resident(flip(after, gate_mat))  1.67 us
  transfers between devices with their start and end apart: 18, of which 4 were waited for; matrix products, arithmetic and copies ran while one was open for 3% of the time, Pallas kernels for 23%

profile of v3, /device:TPU:0, one launch (start us, length us, event | category | flops | bytes accessed | tf_op | source)
XLA Modules:
  0.0 40.5 jit_solution(16730772301218787416)
XLA Ops:
  0.6 3.0 %collective-permute-start.3 = (bf16[16,4096]{1,0:T(8,128)(2,1)}, bf16[16,4096]{1,0:T(8,128)(2,1)S(1)}, u32[]{:S(2)}, u32[]{:S(2)}) collective-permute-start(bf16[16,4096]{1,0:T(8,128)(2,1)} %bitcast.30), channel_id=1, source_target_pairs={{0,2},{1,3},{2,0},{3,1},{4,6},{5,7},{6,4},{7,5},{8,10},{9,11},{10,... | collective-permute-start | bytes 393224 | tf_op jit(solution)/shard_map/ppermute | solution.py:24
  3.6 1.5 %collective-permute-start.5 = (bf16[16,4096]{1,0:T(8,128)(2,1)}, bf16[16,4096]{1,0:T(8,128)(2,1)S(1)}, u32[]{:S(2)}, u32[]{:S(2)}) collective-permute-start(bf16[16,4096]{1,0:T(8,128)(2,1)} %bitcast.31), channel_id=1, source_target_pairs={{0,4},{1,5},{2,6},{3,7},{4,0},{5,1},{6,2},{7,3},{8,12},{9,13},{10,... | collective-permute-start | bytes 393224 | tf_op jit(solution)/shard_map/ppermute | solution.py:24
  5.2 0.8 %copy-done.1 = bf16[1,16,2]{1,2,0:T(2,128)(2,1)S(1)} copy-done((bf16[1,16,2]{1,2,0:T(2,128)(2,1)S(1)}, bf16[1,16,2]{1,2,0:T(2,128)(2,1)}, u32[]{:S(2)}) %copy-start.1) | copy-done | bytes 88
  6.0 1.3 %shard_map.86 = bf16[16,4224]{1,0:T(8,128)(2,1)S(1)} custom-call(bf16[16,4096]{1,0:T(8,128)(2,1)} %bitcast.29, s32[2,16]{1,0:T(2,128)} %bitcast.34, bf16[2,16]{1,0:T(2,128)(2,1)S(1)} %bitcast.28, bf16[768,4096]{1,0:T(8,128)(2,1)} %bitcast.14, bf16[768,4096]{1,0:T(8,128)(2,1)} %bitcast.18, bf16[768,4096]{1,0:T(8,128)(2,1)} %bitcast.24), custom_call_target="tpu_custom_call" | custom-call | bytes 37748736 | tf_op jit(solution)/shard_map/pallas_call | solution.py:143
  7.3 2.0 %collective-permute-start = (bf16[16,4224]{1,0:T(8,128)(2,1)S(1)}, bf16[16,4224]{1,0:T(8,128)(2,1)S(1)}, u32[]{:S(2)}, u32[]{:S(2)}) collective-permute-start(bf16[16,4224]{1,0:T(8,128)(2,1)S(1)} %shard_map.86), channel_id=1, source_target_pairs={{0,2},{1,3},{2,0},{3,1},{4,6},{5,7},{6,4},{7,5},{8,10},{9,11},{10,... | collective-permute-start | bytes 405512 | tf_op jit(solution)/shard_map/ppermute | solution.py:24
  9.4 1.5 %collective-permute-start.1 = (bf16[16,4224]{1,0:T(8,128)(2,1)S(1)}, bf16[16,4224]{1,0:T(8,128)(2,1)S(1)}, u32[]{:S(2)}, u32[]{:S(2)}) collective-permute-start(bf16[16,4224]{1,0:T(8,128)(2,1)S(1)} %shard_map.86), channel_id=1, source_target_pairs={{0,4},{1,5},{2,6},{3,7},{4,0},{5,1},{6,2},{7,3},{8,12},{9,13},{10,... | collective-permute-start | bytes 405512 | tf_op jit(solution)/shard_map/ppermute | solution.py:24
  10.9 0.3 collective-permute-start.2
  11.2 1.7 %shard_map.88.gate_ref = bf16[4096,768]{1,0:T(8,128)(2,1)S(1)} custom-call(bf16[16,4096]{1,0:T(8,128)(2,1)S(1)} %collective-permute-done.3.after_ref, bf16[768,4096]{1,0:T(8,128)(2,1)S(1)} %bitcast.15), custom_call_target="tpu_custom_call" | custom-call | tf_op jit(solution)/shard_map/pallas_call | solution.py:169
  12.9 1.7 %shard_map.89.up_ref = bf16[4096,768]{1,0:T(8,128)(2,1)S(1)} custom-call(bf16[16,4096]{1,0:T(8,128)(2,1)S(1)} %collective-permute-done.3.after_ref, bf16[768,4096]{1,0:T(8,128)(2,1)S(1)} %bitcast.21), custom_call_target="tpu_custom_call" | custom-call | tf_op jit(solution)/shard_map/pallas_call | solution.py:170
  14.7 0.1 collective-permute-start.7
  14.8 1.7 %shard_map.87.down_ref = bf16[4096,768]{1,0:T(8,128)(2,1)S(1)} custom-call(bf16[16,4096]{1,0:T(8,128)(2,1)S(1)} %collective-permute-done.3.after_ref, bf16[768,4096]{1,0:T(8,128)(2,1)S(1)} %bitcast.27), custom_call_target="tpu_custom_call" | custom-call | tf_op jit(solution)/shard_map/pallas_call | solution.py:171
  16.5 0.9 %collective-permute-done.1 = bf16[16,4224]{1,0:T(8,128)(2,1)S(1)} collective-permute-done((bf16[16,4224]{1,0:T(8,128)(2,1)S(1)}, bf16[16,4224]{1,0:T(8,128)(2,1)S(1)}, u32[]{:S(2)}, u32[]{:S(2)}) %collective-permute-start.1) | collective-permute-done | bytes 135200 | tf_op jit(solution)/shard_map/ppermute | solution.py:24
  17.5 0.1 collective-permute-start.4
  17.6 1.9 %shard_map.90 = (f32[128,768]{1,0:T(8,128)S(1)}, f32[128,768]{1,0:T(8,128)S(1)}) custom-call(bf16[64,4096]{1,0:T(8,128)(2,1)S(1)} %constant_dynamic-update-slice_fusion.4.near_ref, bf16[64,4096]{1,0:T(8,128)(2,1)S(1)} %collective-permute-done.7.far_ref, bf16[4096,768]{1,0:T(8,128)(2,1)S(1)} %shard_map.88.gate_ref, bf16[4096,768]{1,0:T(8,128)(2,1)S(1)} %shard_map.89.up_ref), custom_call_target="tpu_custom_call" | custom-call | flops 1610612736 | tf_op jit(solution)/shard_map/pallas_call | solution.py:176
  19.5 1.2 %shard_map.91 = (bf16[128,768]{1,0:T(8,128)(2,1)S(1)}, bf16[128,768]{1,0:T(8,128)(2,1)S(1)}, bf16[128,128]{1,0:T(8,128)(2,1)S(1)}) custom-call(bf16[64,4224]{1,0:T(8,128)(2,1)S(1)} %constant_dynamic-update-slice_fusion.near_ref, bf16[64,4224]{1,0:T(8,128)(2,1)S(1)} %collective-permute-done.4.far_ref, bf16[4096,768]{1,0:T(8,128)(2,1)S(1)} %shard_map.87.down_ref, ...), custom_call_target="tpu_custom_call" | custom-call | tf_op jit(solution)/shard_map/pallas_call | solution.py:190
  20.7 1.0 %shard_map.93 = (bf16[64,2048]{1,0:T(8,128)(2,1)S(1)}, bf16[64,2048]{1,0:T(8,128)(2,1)S(1)}) custom-call(bf16[128,768]{1,0:T(8,128)(2,1)S(1)} %get-tuple-element.35.grad_gate_ref, bf16[128,768]{1,0:T(8,128)(2,1)S(1)} %get-tuple-element.36.grad_up_ref, bf16[768,4096]{1,0:T(8,128)(2,1)S(1)} %bitcast.16, bf16[768,4096]{1,0:T(8,128)(2,1)S(1)} %bitcast.22, ...), custom_call_target="tpu_custom_call" | custom-call | tf_op jit(solution)/shard_map/pallas_call | solution.py:203
  21.7 0.5 %collective-permute-start.13 = (bf16[64,2048]{1,0:T(8,128)(2,1)S(1)}, bf16[64,2048]{1,0:T(8,128)(2,1)S(1)}, u32[]{:S(2)}, u32[]{:S(2)}) collective-permute-start(bf16[64,2048]{1,0:T(8,128)(2,1)S(1)} %get-tuple-element.41), channel_id=1, source_target_pairs={{0,1},{1,0},{2,3},{3,2},{4,5},{5,4},{6,7},{7,6},{8,9},{9,8},{10,11... | collective-permute-start | bytes 786440 | tf_op jit(solution)/shard_map/ppermute | solution.py:24
  22.2 1.0 %shard_map.92 = (bf16[64,2176]{1,0:T(8,128)(2,1)S(1)}, bf16[64,2176]{1,0:T(8,128)(2,1)S(1)}) custom-call(bf16[128,768]{1,0:T(8,128)(2,1)S(1)} %get-tuple-element.35.grad_gate_ref, bf16[128,768]{1,0:T(8,128)(2,1)S(1)} %get-tuple-element.36.grad_up_ref, bf16[768,4096]{1,0:T(8,128)(2,1)S(1)} %bitcast.17, bf16[768,4096]{1,0:T(8,128)(2,1)S(1)} %bitcast.23, ...), custom_call_target="tpu_custom_call" | custom-call | tf_op jit(solution)/shard_map/pallas_call | solution.py:203
  23.2 0.1 collective-permute-start.8
  23.5 1.3 %collective-permute-start.14 = (bf16[16,2048]{1,0:T(8,128)(2,1)S(1)}, bf16[16,2048]{1,0:T(8,128)(2,1)S(1)}, u32[]{:S(2)}, u32[]{:S(2)}) collective-permute-start(bf16[16,2048]{1,0:T(8,128)(2,1)S(1)} %get-tuple-element.45), channel_id=1, source_target_pairs={{0,2},{1,3},{2,0},{3,1},{4,6},{5,7},{6,4},{7,5},{8,10},{9,11},{10,... | collective-permute-start | bytes 196616 | tf_op jit(solution)/shard_map/ppermute | solution.py:24
  24.8 1.4 %collective-permute-start.15 = (bf16[16,2048]{1,0:T(8,128)(2,1)S(1)}, bf16[16,2048]{1,0:T(8,128)(2,1)S(1)}, u32[]{:S(2)}, u32[]{:S(2)}) collective-permute-start(bf16[16,2048]{1,0:T(8,128)(2,1)S(1)} %get-tuple-element.47), channel_id=1, source_target_pairs={{0,4},{1,5},{2,6},{3,7},{4,0},{5,1},{6,2},{7,3},{8,12},{9,13},{10,... | collective-permute-start | bytes 196616 | tf_op jit(solution)/shard_map/ppermute | solution.py:24
  26.2 0.8 %collective-permute-start.16 = (bf16[16,2048]{1,0:T(8,128)(2,1)S(1)}, bf16[16,2048]{1,0:T(8,128)(2,1)S(1)}, u32[]{:S(2)}, u32[]{:S(2)}) collective-permute-start(bf16[16,2048]{1,0:T(8,128)(2,1)S(1)} %get-tuple-element.46), channel_id=1, source_target_pairs={{0,6},{1,7},{2,4},{3,5},{4,2},{5,3},{6,0},{7,1},{8,14},{9,15},{10,... | collective-permute-start | bytes 196616 | tf_op jit(solution)/shard_map/ppermute | solution.py:24
  27.2 1.6 %collective-permute-start.10 = (bf16[16,2176]{1,0:T(8,128)(2,1)S(1)}, bf16[16,2176]{1,0:T(8,128)(2,1)S(1)}, u32[]{:S(2)}, u32[]{:S(2)}) collective-permute-start(bf16[16,2176]{1,0:T(8,128)(2,1)S(1)} %get-tuple-element.44), channel_id=1, source_target_pairs={{0,4},{1,5},{2,6},{3,7},{4,0},{5,1},{6,2},{7,3},{8,12},{9,13},{10,... | collective-permute-start | bytes 208904 | tf_op jit(solution)/shard_map/ppermute | solution.py:24
  28.7 1.2 %collective-permute-start.11 = (bf16[16,2176]{1,0:T(8,128)(2,1)S(1)}, bf16[16,2176]{1,0:T(8,128)(2,1)S(1)}, u32[]{:S(2)}, u32[]{:S(2)}) collective-permute-start(bf16[16,2176]{1,0:T(8,128)(2,1)S(1)} %get-tuple-element.43), channel_id=1, source_target_pairs={{0,6},{1,7},{2,4},{3,5},{4,2},{5,3},{6,0},{7,1},{8,14},{9,15},{10,... | collective-permute-start | bytes 208904 | tf_op jit(solution)/shard_map/ppermute | solution.py:24
  29.9 0.8 %collective-permute-start.9 = (bf16[16,2176]{1,0:T(8,128)(2,1)S(1)}, bf16[16,2176]{1,0:T(8,128)(2,1)S(1)}, u32[]{:S(2)}, u32[]{:S(2)}) collective-permute-start(bf16[16,2176]{1,0:T(8,128)(2,1)S(1)} %get-tuple-element.42), channel_id=1, source_target_pairs={{0,2},{1,3},{2,0},{3,1},{4,6},{5,7},{6,4},{7,5},{8,10},{9,11},{10,... | collective-permute-start | bytes 208904 | tf_op jit(solution)/shard_map/ppermute | solution.py:24
  30.7 0.8 %collective-permute-done.16 = bf16[16,2048]{1,0:T(8,128)(2,1)S(1)} collective-permute-done((bf16[16,2048]{1,0:T(8,128)(2,1)S(1)}, bf16[16,2048]{1,0:T(8,128)(2,1)S(1)}, u32[]{:S(2)}, u32[]{:S(2)}) %collective-permute-start.16) | collective-permute-done | bytes 65568 | tf_op jit(solution)/shard_map/ppermute | solution.py:24
  31.5 3.7 %collective-permute-start.17 = (bf16[16,2048]{1,0:T(8,128)(2,1)S(1)}, bf16[16,2048]{1,0:T(8,128)(2,1)S(1)}, u32[]{:S(2)}, u32[]{:S(2)}) collective-permute-start(bf16[16,2048]{1,0:T(8,128)(2,1)S(1)} %add_convert_fusion.2), channel_id=1, source_target_pairs={{0,24},{8,0},{16,8},{24,16},{1,25},{9,1},{17,9},{25,17},{2,26},{10... | collective-permute-start | bytes 196616 | tf_op jit(solution)/shard_map/ppermute | solution.py:19
  35.2 0.1 slice_add_fusion
  35.3 2.6 %collective-permute-start.12 = (bf16[16,2048]{1,0:T(8,128)(2,1)S(1)}, bf16[16,2048]{1,0:T(8,128)(2,1)S(1)}, u32[]{:S(2)}, u32[]{:S(2)}) collective-permute-start(bf16[16,2048]{1,0:T(8,128)(2,1)S(1)} %slice.72), channel_id=1, source_target_pairs={{0,24},{8,0},{16,8},{24,16},{1,25},{9,1},{17,9},{25,17},{2,26},{10... | collective-permute-start | bytes 196616 | tf_op jit(solution)/shard_map/ppermute | solution.py:19
  38.0 0.7 %select_reduce_fusion = f32[16,2]{0,1:T(2,128)} fusion(f32[16,64]{1,0:T(8,128)S(1)} %slice_add_fusion, s32[16,2]{0,1:T(2,128)S(1)} %bitcast.35), kind=kLoop, calls=%fused_computation.14 | loop fusion | flops 6112 | bytes 4352 | tf_op jit(solution)/shard_map/reduce_sum | solution.py:222
  38.7 1.2 %collective-permute-done.12 = bf16[16,2048]{1,0:T(8,128)(2,1)S(1)} collective-permute-done((bf16[16,2048]{1,0:T(8,128)(2,1)S(1)}, bf16[16,2048]{1,0:T(8,128)(2,1)S(1)}, u32[]{:S(2)}, u32[]{:S(2)}) %collective-permute-start.12) | collective-permute-done | bytes 65568 | tf_op jit(solution)/shard_map/ppermute | solution.py:19
  39.9 0.7 %maximum_bitcast_fusion = bf16[1,16,4096]{2,1,0:T(8,128)(2,1)} fusion(bf16[16,2048]{1,0:T(8,128)(2,1)S(1)} %collective-permute-done.17, bf16[16,2048]{1,0:T(8,128)(2,1)S(1)} %collective-permute-done.12), kind=kLoop, calls=%fused_computation.4 | loop fusion | flops 262144 | bytes 262144 | tf_op jit(solution)/shard_map/broadcast_in_dim | solution.py:223
  (48 shorter events, 0.6 us)
Async XLA Ops:
  0.6 10.2 %collective-permute-start.3 = (bf16[16,4096]{1,0:T(8,128)(2,1)}, bf16[16,4096]{1,0:T(8,128)(2,1)S(1)}, u32[]{:S(2)}, u32[]{:S(2)}) collective-permute-start(bf16[16,4096]{1,0:T(8,128)(2,1)} %bitcast.30), channel_id=1, source_target_pairs={{0,2},{1,3},{2,0},{3,1},{4,6},{5,7},{6,4},{7,5},{8,10},{9,11},{10,... | collective-permute-start | bytes 393224 | tf_op jit(solution)/shard_map/ppermute | solution.py:24
  3.6 11.0 %collective-permute-start.5 = (bf16[16,4096]{1,0:T(8,128)(2,1)}, bf16[16,4096]{1,0:T(8,128)(2,1)S(1)}, u32[]{:S(2)}, u32[]{:S(2)}) collective-permute-start(bf16[16,4096]{1,0:T(8,128)(2,1)} %bitcast.31), channel_id=1, source_target_pairs={{0,4},{1,5},{2,6},{3,7},{4,0},{5,1},{6,2},{7,3},{8,12},{9,13},{10,... | collective-permute-start | bytes 393224 | tf_op jit(solution)/shard_map/ppermute | solution.py:24
  5.2 9.5 %collective-permute-start.6 = (bf16[16,4096]{1,0:T(8,128)(2,1)}, bf16[16,4096]{1,0:T(8,128)(2,1)S(1)}, u32[]{:S(2)}, u32[]{:S(2)}) collective-permute-start(bf16[16,4096]{1,0:T(8,128)(2,1)} %bitcast.32), channel_id=1, source_target_pairs={{0,6},{1,7},{2,4},{3,5},{4,2},{5,3},{6,0},{7,1},{8,14},{9,15},{10,... | collective-permute-start | bytes 393224 | tf_op jit(solution)/shard_map/ppermute | solution.py:24
  5.2 7.7 %slice-start = ((s8[6291456]{0:T(1024)(128)(4,1)}), s8[4194304]{0:T(1024)(128)(4,1)S(1)}, s32[]{:S(2)}) async-start(s8[6291456]{0:T(1024)(128)(4,1)} %bitcast.19), calls=%async_computation | async-start | bytes 8388608
  5.2 0.8 %copy-start.1 = (bf16[1,16,2]{1,2,0:T(2,128)(2,1)S(1)}, bf16[1,16,2]{1,2,0:T(2,128)(2,1)}, u32[]{:S(2)}) copy-start(bf16[1,16,2]{1,2,0:T(2,128)(2,1)} %param.10) | copy-start | bytes 196
  6.0 5.2 %copy-start = (bf16[1,768,4096]{2,1,0:T(8,128)(2,1)S(1)}, bf16[1,768,4096]{2,1,0:T(8,128)(2,1)}, u32[]{:S(2)}) copy-start(bf16[1,768,4096]{2,1,0:T(8,128)(2,1)} %param.11) | copy-start | bytes 18874372
  6.0 6.9 %slice-start.1 = ((s8[6291456]{0:T(1024)(128)(4,1)}), s8[2097152]{0:T(1024)(128)(4,1)S(1)}, s32[]{:S(2)}) async-start(s8[6291456]{0:T(1024)(128)(4,1)} %bitcast.19), calls=%async_computation.1 | async-start | bytes 4194304
  7.3 9.1 %collective-permute-start = (bf16[16,4224]{1,0:T(8,128)(2,1)S(1)}, bf16[16,4224]{1,0:T(8,128)(2,1)S(1)}, u32[]{:S(2)}, u32[]{:S(2)}) collective-permute-start(bf16[16,4224]{1,0:T(8,128)(2,1)S(1)} %shard_map.86), channel_id=1, source_target_pairs={{0,2},{1,3},{2,0},{3,1},{4,6},{5,7},{6,4},{7,5},{8,10},{9,11},{10,... | collective-permute-start | bytes 405512 | tf_op jit(solution)/shard_map/ppermute | solution.py:24
  9.4 8.1 %collective-permute-start.1 = (bf16[16,4224]{1,0:T(8,128)(2,1)S(1)}, bf16[16,4224]{1,0:T(8,128)(2,1)S(1)}, u32[]{:S(2)}, u32[]{:S(2)}) collective-permute-start(bf16[16,4224]{1,0:T(8,128)(2,1)S(1)} %shard_map.86), channel_id=1, source_target_pairs={{0,4},{1,5},{2,6},{3,7},{4,0},{5,1},{6,2},{7,3},{8,12},{9,13},{10,... | collective-permute-start | bytes 405512 | tf_op jit(solution)/shard_map/ppermute | solution.py:24
  10.9 6.5 %collective-permute-start.2 = (bf16[16,4224]{1,0:T(8,128)(2,1)S(1)}, bf16[16,4224]{1,0:T(8,128)(2,1)S(1)}, u32[]{:S(2)}, u32[]{:S(2)}) collective-permute-start(bf16[16,4224]{1,0:T(8,128)(2,1)S(1)} %shard_map.86), channel_id=1, source_target_pairs={{0,6},{1,7},{2,4},{3,5},{4,2},{5,3},{6,0},{7,1},{8,14},{9,15},{10,... | collective-permute-start | bytes 405512 | tf_op jit(solution)/shard_map/ppermute | solution.py:24
  11.2 3.6 %slice-start.2 = ((s8[6291456]{0:T(1024)(128)(4,1)}), s8[4194304]{0:T(1024)(128)(4,1)S(1)}, s32[]{:S(2)}) async-start(s8[6291456]{0:T(1024)(128)(4,1)} %bitcast.25), calls=%async_computation.2 | async-start | bytes 8388608
  12.9 1.7 %copy-start.2 = (bf16[1,16,4096]{2,1,0:T(8,128)(2,1)S(1)}, bf16[1,16,4096]{2,1,0:T(8,128)(2,1)}, u32[]{:S(2)}) copy-start(bf16[1,16,4096]{2,1,0:T(8,128)(2,1)} %param.7) | copy-start | bytes 393220
  12.9 1.9 %slice-start.3 = ((s8[6291456]{0:T(1024)(128)(4,1)}), s8[2097152]{0:T(1024)(128)(4,1)S(1)}, s32[]{:S(2)}) async-start(s8[6291456]{0:T(1024)(128)(4,1)} %bitcast.25), calls=%async_computation.3 | async-start | bytes 4194304
  14.7 2.9 %collective-permute-start.7 = (bf16[64,4096]{1,0:T(8,128)(2,1)S(1)}, bf16[64,4096]{1,0:T(8,128)(2,1)S(1)}, u32[]{:S(2)}, u32[]{:S(2)}) collective-permute-start(bf16[64,4096]{1,0:T(8,128)(2,1)S(1)} %constant_dynamic-update-slice_fusion.4.near_ref), channel_id=1, source_target_pairs={{0,1},{1,0},{2,3},{3,2},{4,5},{5,4},{6,7},{7,6},{8,9},{9,8},{10,11... | collective-permute-start | bytes 1572872 | tf_op jit(solution)/shard_map/ppermute | solution.py:24
  17.5 2.0 %collective-permute-start.4 = (bf16[64,4224]{1,0:T(8,128)(2,1)S(1)}, bf16[64,4224]{1,0:T(8,128)(2,1)S(1)}, u32[]{:S(2)}, u32[]{:S(2)}) collective-permute-start(bf16[64,4224]{1,0:T(8,128)(2,1)S(1)} %constant_dynamic-update-slice_fusion.near_ref), channel_id=1, source_target_pairs={{0,1},{1,0},{2,3},{3,2},{4,5},{5,4},{6,7},{7,6},{8,9},{9,8},{10,11... | collective-permute-start | bytes 1622024 | tf_op jit(solution)/shard_map/ppermute | solution.py:24
  21.7 16.3 %copy-start.3 = (s32[1,16,2]{1,2,0:T(2,128)S(1)}, s32[1,16,2]{1,2,0:T(2,128)}, u32[]{:S(2)}) copy-start(s32[1,16,2]{1,2,0:T(2,128)} %param.9) | copy-start | bytes 388
  21.7 1.7 %collective-permute-start.13 = (bf16[64,2048]{1,0:T(8,128)(2,1)S(1)}, bf16[64,2048]{1,0:T(8,128)(2,1)S(1)}, u32[]{:S(2)}, u32[]{:S(2)}) collective-permute-start(bf16[64,2048]{1,0:T(8,128)(2,1)S(1)} %get-tuple-element.41), channel_id=1, source_target_pairs={{0,1},{1,0},{2,3},{3,2},{4,5},{5,4},{6,7},{7,6},{8,9},{9,8},{10,11... | collective-permute-start | bytes 786440 | tf_op jit(solution)/shard_map/ppermute | solution.py:24
  23.2 3.8 %collective-permute-start.8 = (bf16[64,2176]{1,0:T(8,128)(2,1)S(1)}, bf16[64,2176]{1,0:T(8,128)(2,1)S(1)}, u32[]{:S(2)}, u32[]{:S(2)}) collective-permute-start(bf16[64,2176]{1,0:T(8,128)(2,1)S(1)} %get-tuple-element.39), channel_id=1, source_target_pairs={{0,1},{1,0},{2,3},{3,2},{4,5},{5,4},{6,7},{7,6},{8,9},{9,8},{10,11... | collective-permute-start | bytes 835592 | tf_op jit(solution)/shard_map/ppermute | solution.py:24
  23.5 6.4 %collective-permute-start.14 = (bf16[16,2048]{1,0:T(8,128)(2,1)S(1)}, bf16[16,2048]{1,0:T(8,128)(2,1)S(1)}, u32[]{:S(2)}, u32[]{:S(2)}) collective-permute-start(bf16[16,2048]{1,0:T(8,128)(2,1)S(1)} %get-tuple-element.45), channel_id=1, source_target_pairs={{0,2},{1,3},{2,0},{3,1},{4,6},{5,7},{6,4},{7,5},{8,10},{9,11},{10,... | collective-permute-start | bytes 196616 | tf_op jit(solution)/shard_map/ppermute | solution.py:24
  24.8 5.9 %collective-permute-start.15 = (bf16[16,2048]{1,0:T(8,128)(2,1)S(1)}, bf16[16,2048]{1,0:T(8,128)(2,1)S(1)}, u32[]{:S(2)}, u32[]{:S(2)}) collective-permute-start(bf16[16,2048]{1,0:T(8,128)(2,1)S(1)} %get-tuple-element.47), channel_id=1, source_target_pairs={{0,4},{1,5},{2,6},{3,7},{4,0},{5,1},{6,2},{7,3},{8,12},{9,13},{10,... | collective-permute-start | bytes 196616 | tf_op jit(solution)/shard_map/ppermute | solution.py:24
  26.2 5.2 %collective-permute-start.16 = (bf16[16,2048]{1,0:T(8,128)(2,1)S(1)}, bf16[16,2048]{1,0:T(8,128)(2,1)S(1)}, u32[]{:S(2)}, u32[]{:S(2)}) collective-permute-start(bf16[16,2048]{1,0:T(8,128)(2,1)S(1)} %get-tuple-element.46), channel_id=1, source_target_pairs={{0,6},{1,7},{2,4},{3,5},{4,2},{5,3},{6,0},{7,1},{8,14},{9,15},{10,... | collective-permute-start | bytes 196616 | tf_op jit(solution)/shard_map/ppermute | solution.py:24
  27.2 8.0 %collective-permute-start.10 = (bf16[16,2176]{1,0:T(8,128)(2,1)S(1)}, bf16[16,2176]{1,0:T(8,128)(2,1)S(1)}, u32[]{:S(2)}, u32[]{:S(2)}) collective-permute-start(bf16[16,2176]{1,0:T(8,128)(2,1)S(1)} %get-tuple-element.44), channel_id=1, source_target_pairs={{0,4},{1,5},{2,6},{3,7},{4,0},{5,1},{6,2},{7,3},{8,12},{9,13},{10,... | collective-permute-start | bytes 208904 | tf_op jit(solution)/shard_map/ppermute | solution.py:24
  28.7 6.4 %collective-permute-start.11 = (bf16[16,2176]{1,0:T(8,128)(2,1)S(1)}, bf16[16,2176]{1,0:T(8,128)(2,1)S(1)}, u32[]{:S(2)}, u32[]{:S(2)}) collective-permute-start(bf16[16,2176]{1,0:T(8,128)(2,1)S(1)} %get-tuple-element.43), channel_id=1, source_target_pairs={{0,6},{1,7},{2,4},{3,5},{4,2},{5,3},{6,0},{7,1},{8,14},{9,15},{10,... | collective-permute-start | bytes 208904 | tf_op jit(solution)/shard_map/ppermute | solution.py:24
  29.9 5.3 %collective-permute-start.9 = (bf16[16,2176]{1,0:T(8,128)(2,1)S(1)}, bf16[16,2176]{1,0:T(8,128)(2,1)S(1)}, u32[]{:S(2)}, u32[]{:S(2)}) collective-permute-start(bf16[16,2176]{1,0:T(8,128)(2,1)S(1)} %get-tuple-element.42), channel_id=1, source_target_pairs={{0,2},{1,3},{2,0},{3,1},{4,6},{5,7},{6,4},{7,5},{8,10},{9,11},{10,... | collective-permute-start | bytes 208904 | tf_op jit(solution)/shard_map/ppermute | solution.py:24
  31.5 7.2 %collective-permute-start.17 = (bf16[16,2048]{1,0:T(8,128)(2,1)S(1)}, bf16[16,2048]{1,0:T(8,128)(2,1)S(1)}, u32[]{:S(2)}, u32[]{:S(2)}) collective-permute-start(bf16[16,2048]{1,0:T(8,128)(2,1)S(1)} %add_convert_fusion.2), channel_id=1, source_target_pairs={{0,24},{8,0},{16,8},{24,16},{1,25},{9,1},{17,9},{25,17},{2,26},{10... | collective-permute-start | bytes 196616 | tf_op jit(solution)/shard_map/ppermute | solution.py:19
  35.3 4.5 %collective-permute-start.12 = (bf16[16,2048]{1,0:T(8,128)(2,1)S(1)}, bf16[16,2048]{1,0:T(8,128)(2,1)S(1)}, u32[]{:S(2)}, u32[]{:S(2)}) collective-permute-start(bf16[16,2048]{1,0:T(8,128)(2,1)S(1)} %slice.72), channel_id=1, source_target_pairs={{0,24},{8,0},{16,8},{24,16},{1,25},{9,1},{17,9},{25,17},{2,26},{10... | collective-permute-start | bytes 196616 | tf_op jit(solution)/shard_map/ppermute | solution.py:19

commit v4 on v3

--- a/solution.py
+++ b/solution.py
@@ -60,10 +60,10 @@
     copies[0].wait()
     expert = lax.broadcasted_iota(jnp.int32, (LANES, tok_rows), 0)
     table = jnp.zeros((LANES, tok_rows), jnp.float32)
+    vals = vals_ref[...].astype(jnp.float32)
     for route in range(routes_ref.shape[0]):
         chosen = routes_ref[route : route + 1, :] == expert
-        value = vals_ref[route : route + 1, :].astype(jnp.float32)
-        table = table + jnp.where(chosen, value, 0.0)
+        table = table + jnp.where(chosen, vals[route : route + 1, :], 0.0)
     packed_ref[:, width:] = jnp.transpose(table).astype(jnp.bfloat16)
     copies[1].wait()
 

time: 40.7 us -> 40.7 us (level)
  no operation moved by 1% of the time
where the time goes in v4:
time: 40.7 us; the launch traced here: 40.5 us
  starting transfers between devices  22.6 us (56%)
  Pallas kernels  11.4 us (28%)
  waiting for transfers between devices  2.99 us (7%)
  other arithmetic  1.67 us (4%)
  local copies, waits for them, and re-layouts  0.99 us (2%)
  between operations  0.92 us (2%)
    ppermute x16, starting transfers between devices, swapped(): return lax.ppermute(array, 'expert', [(i, i ^ bits) for i in range(peers)])  16.3 us
    ppermute x2, starting transfers between devices, shifted(): lax.ppermute(array, axis, [(i, (i + by) % peers) for i in range(peers)])  6.29 us
    pallas_call x2, Pallas kernels, on_device(): pl.pallas_call(functools.partial(third_kernel, chunk * span, span), out_s...  1.99 us
    pallas_call x1, Pallas kernels, on_device(): pl.pallas_call(first_kernel, out_shape=(pre, pre), in_specs=[VMEM] * 4, o...  1.87 us
    ppermute x16, waiting for transfers between devices, swapped(): return lax.ppermute(array, 'expert', [(i, i ^ bits) for i in range(peers)])  1.8 us
    pallas_call x1, Pallas kernels, on_device(): up_flipped = resident(flip(after, up_mat))  1.67 us
    pallas_call x1, Pallas kernels, on_device(): down_flipped = resident(flip(after, down_mat))  1.67 us
    pallas_call x1, Pallas kernels, on_device(): gate_flipped = resident(flip(after, gate_mat))  1.67 us
  transfers between devices with their start and end apart: 18, of which 4 were waited for; matrix products, arithmetic and copies ran while one was open for 3% of the time, Pallas kernels for 23%

profile of v4, /device:TPU:0, one launch (start us, length us, event | category | flops | bytes accessed | tf_op | source)
XLA Modules:
  0.0 40.5 jit_solution(17110256222526905794)
XLA Ops:
  0.6 3.0 %collective-permute-start.3 = (bf16[16,4096]{1,0:T(8,128)(2,1)}, bf16[16,4096]{1,0:T(8,128)(2,1)S(1)}, u32[]{:S(2)}, u32[]{:S(2)}) collective-permute-start(bf16[16,4096]{1,0:T(8,128)(2,1)} %bitcast.30), channel_id=1, source_target_pairs={{0,2},{1,3},{2,0},{3,1},{4,6},{5,7},{6,4},{7,5},{8,10},{9,11},{10,... | collective-permute-start | bytes 393224 | tf_op jit(solution)/shard_map/ppermute | solution.py:24
  3.6 1.5 %collective-permute-start.5 = (bf16[16,4096]{1,0:T(8,128)(2,1)}, bf16[16,4096]{1,0:T(8,128)(2,1)S(1)}, u32[]{:S(2)}, u32[]{:S(2)}) collective-permute-start(bf16[16,4096]{1,0:T(8,128)(2,1)} %bitcast.31), channel_id=1, source_target_pairs={{0,4},{1,5},{2,6},{3,7},{4,0},{5,1},{6,2},{7,3},{8,12},{9,13},{10,... | collective-permute-start | bytes 393224 | tf_op jit(solution)/shard_map/ppermute | solution.py:24
  5.2 0.8 %copy-done.1 = bf16[1,16,2]{1,2,0:T(2,128)(2,1)S(1)} copy-done((bf16[1,16,2]{1,2,0:T(2,128)(2,1)S(1)}, bf16[1,16,2]{1,2,0:T(2,128)(2,1)}, u32[]{:S(2)}) %copy-start.1) | copy-done | bytes 88
  6.0 1.3 %shard_map.86 = bf16[16,4224]{1,0:T(8,128)(2,1)S(1)} custom-call(bf16[16,4096]{1,0:T(8,128)(2,1)} %bitcast.29, s32[2,16]{1,0:T(2,128)} %bitcast.34, bf16[2,16]{1,0:T(2,128)(2,1)S(1)} %bitcast.28, bf16[768,4096]{1,0:T(8,128)(2,1)} %bitcast.14, bf16[768,4096]{1,0:T(8,128)(2,1)} %bitcast.18, bf16[768,4096]{1,0:T(8,128)(2,1)} %bitcast.24), custom_call_target="tpu_custom_call" | custom-call | bytes 37748736 | tf_op jit(solution)/shard_map/pallas_call | solution.py:143
  7.3 2.0 %collective-permute-start = (bf16[16,4224]{1,0:T(8,128)(2,1)S(1)}, bf16[16,4224]{1,0:T(8,128)(2,1)S(1)}, u32[]{:S(2)}, u32[]{:S(2)}) collective-permute-start(bf16[16,4224]{1,0:T(8,128)(2,1)S(1)} %shard_map.86), channel_id=1, source_target_pairs={{0,2},{1,3},{2,0},{3,1},{4,6},{5,7},{6,4},{7,5},{8,10},{9,11},{10,... | collective-permute-start | bytes 405512 | tf_op jit(solution)/shard_map/ppermute | solution.py:24
  9.4 1.5 %collective-permute-start.1 = (bf16[16,4224]{1,0:T(8,128)(2,1)S(1)}, bf16[16,4224]{1,0:T(8,128)(2,1)S(1)}, u32[]{:S(2)}, u32[]{:S(2)}) collective-permute-start(bf16[16,4224]{1,0:T(8,128)(2,1)S(1)} %shard_map.86), channel_id=1, source_target_pairs={{0,4},{1,5},{2,6},{3,7},{4,0},{5,1},{6,2},{7,3},{8,12},{9,13},{10,... | collective-permute-start | bytes 405512 | tf_op jit(solution)/shard_map/ppermute | solution.py:24
  10.9 0.3 collective-permute-start.2
  11.2 1.7 %shard_map.88.gate_ref = bf16[4096,768]{1,0:T(8,128)(2,1)S(1)} custom-call(bf16[16,4096]{1,0:T(8,128)(2,1)S(1)} %collective-permute-done.3.after_ref, bf16[768,4096]{1,0:T(8,128)(2,1)S(1)} %bitcast.15), custom_call_target="tpu_custom_call" | custom-call | tf_op jit(solution)/shard_map/pallas_call | solution.py:169
  12.9 1.7 %shard_map.89.up_ref = bf16[4096,768]{1,0:T(8,128)(2,1)S(1)} custom-call(bf16[16,4096]{1,0:T(8,128)(2,1)S(1)} %collective-permute-done.3.after_ref, bf16[768,4096]{1,0:T(8,128)(2,1)S(1)} %bitcast.21), custom_call_target="tpu_custom_call" | custom-call | tf_op jit(solution)/shard_map/pallas_call | solution.py:170
  14.7 0.1 collective-permute-start.7
  14.8 1.7 %shard_map.87.down_ref = bf16[4096,768]{1,0:T(8,128)(2,1)S(1)} custom-call(bf16[16,4096]{1,0:T(8,128)(2,1)S(1)} %collective-permute-done.3.after_ref, bf16[768,4096]{1,0:T(8,128)(2,1)S(1)} %bitcast.27), custom_call_target="tpu_custom_call" | custom-call | tf_op jit(solution)/shard_map/pallas_call | solution.py:171
  16.5 0.9 %collective-permute-done.1 = bf16[16,4224]{1,0:T(8,128)(2,1)S(1)} collective-permute-done((bf16[16,4224]{1,0:T(8,128)(2,1)S(1)}, bf16[16,4224]{1,0:T(8,128)(2,1)S(1)}, u32[]{:S(2)}, u32[]{:S(2)}) %collective-permute-start.1) | collective-permute-done | bytes 135200 | tf_op jit(solution)/shard_map/ppermute | solution.py:24
  17.5 0.1 collective-permute-start.4
  17.6 1.9 %shard_map.90 = (f32[128,768]{1,0:T(8,128)S(1)}, f32[128,768]{1,0:T(8,128)S(1)}) custom-call(bf16[64,4096]{1,0:T(8,128)(2,1)S(1)} %constant_dynamic-update-slice_fusion.4.near_ref, bf16[64,4096]{1,0:T(8,128)(2,1)S(1)} %collective-permute-done.7.far_ref, bf16[4096,768]{1,0:T(8,128)(2,1)S(1)} %shard_map.88.gate_ref, bf16[4096,768]{1,0:T(8,128)(2,1)S(1)} %shard_map.89.up_ref), custom_call_target="tpu_custom_call" | custom-call | flops 1610612736 | tf_op jit(solution)/shard_map/pallas_call | solution.py:176
  19.5 1.2 %shard_map.91 = (bf16[128,768]{1,0:T(8,128)(2,1)S(1)}, bf16[128,768]{1,0:T(8,128)(2,1)S(1)}, bf16[128,128]{1,0:T(8,128)(2,1)S(1)}) custom-call(bf16[64,4224]{1,0:T(8,128)(2,1)S(1)} %constant_dynamic-update-slice_fusion.near_ref, bf16[64,4224]{1,0:T(8,128)(2,1)S(1)} %collective-permute-done.4.far_ref, bf16[4096,768]{1,0:T(8,128)(2,1)S(1)} %shard_map.87.down_ref, ...), custom_call_target="tpu_custom_call" | custom-call | tf_op jit(solution)/shard_map/pallas_call | solution.py:190
  20.7 1.0 %shard_map.93 = (bf16[64,2048]{1,0:T(8,128)(2,1)S(1)}, bf16[64,2048]{1,0:T(8,128)(2,1)S(1)}) custom-call(bf16[128,768]{1,0:T(8,128)(2,1)S(1)} %get-tuple-element.35.grad_gate_ref, bf16[128,768]{1,0:T(8,128)(2,1)S(1)} %get-tuple-element.36.grad_up_ref, bf16[768,4096]{1,0:T(8,128)(2,1)S(1)} %bitcast.16, bf16[768,4096]{1,0:T(8,128)(2,1)S(1)} %bitcast.22, ...), custom_call_target="tpu_custom_call" | custom-call | tf_op jit(solution)/shard_map/pallas_call | solution.py:203
  21.7 0.5 %collective-permute-start.13 = (bf16[64,2048]{1,0:T(8,128)(2,1)S(1)}, bf16[64,2048]{1,0:T(8,128)(2,1)S(1)}, u32[]{:S(2)}, u32[]{:S(2)}) collective-permute-start(bf16[64,2048]{1,0:T(8,128)(2,1)S(1)} %get-tuple-element.41), channel_id=1, source_target_pairs={{0,1},{1,0},{2,3},{3,2},{4,5},{5,4},{6,7},{7,6},{8,9},{9,8},{10,11... | collective-permute-start | bytes 786440 | tf_op jit(solution)/shard_map/ppermute | solution.py:24
  22.2 1.0 %shard_map.92 = (bf16[64,2176]{1,0:T(8,128)(2,1)S(1)}, bf16[64,2176]{1,0:T(8,128)(2,1)S(1)}) custom-call(bf16[128,768]{1,0:T(8,128)(2,1)S(1)} %get-tuple-element.35.grad_gate_ref, bf16[128,768]{1,0:T(8,128)(2,1)S(1)} %get-tuple-element.36.grad_up_ref, bf16[768,4096]{1,0:T(8,128)(2,1)S(1)} %bitcast.17, bf16[768,4096]{1,0:T(8,128)(2,1)S(1)} %bitcast.23, ...), custom_call_target="tpu_custom_call" | custom-call | tf_op jit(solution)/shard_map/pallas_call | solution.py:203
  23.2 0.1 collective-permute-start.8
  23.5 1.3 %collective-permute-start.14 = (bf16[16,2048]{1,0:T(8,128)(2,1)S(1)}, bf16[16,2048]{1,0:T(8,128)(2,1)S(1)}, u32[]{:S(2)}, u32[]{:S(2)}) collective-permute-start(bf16[16,2048]{1,0:T(8,128)(2,1)S(1)} %get-tuple-element.45), channel_id=1, source_target_pairs={{0,2},{1,3},{2,0},{3,1},{4,6},{5,7},{6,4},{7,5},{8,10},{9,11},{10,... | collective-permute-start | bytes 196616 | tf_op jit(solution)/shard_map/ppermute | solution.py:24
  24.8 1.4 %collective-permute-start.15 = (bf16[16,2048]{1,0:T(8,128)(2,1)S(1)}, bf16[16,2048]{1,0:T(8,128)(2,1)S(1)}, u32[]{:S(2)}, u32[]{:S(2)}) collective-permute-start(bf16[16,2048]{1,0:T(8,128)(2,1)S(1)} %get-tuple-element.47), channel_id=1, source_target_pairs={{0,4},{1,5},{2,6},{3,7},{4,0},{5,1},{6,2},{7,3},{8,12},{9,13},{10,... | collective-permute-start | bytes 196616 | tf_op jit(solution)/shard_map/ppermute | solution.py:24
  26.2 0.8 %collective-permute-start.16 = (bf16[16,2048]{1,0:T(8,128)(2,1)S(1)}, bf16[16,2048]{1,0:T(8,128)(2,1)S(1)}, u32[]{:S(2)}, u32[]{:S(2)}) collective-permute-start(bf16[16,2048]{1,0:T(8,128)(2,1)S(1)} %get-tuple-element.46), channel_id=1, source_target_pairs={{0,6},{1,7},{2,4},{3,5},{4,2},{5,3},{6,0},{7,1},{8,14},{9,15},{10,... | collective-permute-start | bytes 196616 | tf_op jit(solution)/shard_map/ppermute | solution.py:24
  27.2 1.6 %collective-permute-start.10 = (bf16[16,2176]{1,0:T(8,128)(2,1)S(1)}, bf16[16,2176]{1,0:T(8,128)(2,1)S(1)}, u32[]{:S(2)}, u32[]{:S(2)}) collective-permute-start(bf16[16,2176]{1,0:T(8,128)(2,1)S(1)} %get-tuple-element.44), channel_id=1, source_target_pairs={{0,4},{1,5},{2,6},{3,7},{4,0},{5,1},{6,2},{7,3},{8,12},{9,13},{10,... | collective-permute-start | bytes 208904 | tf_op jit(solution)/shard_map/ppermute | solution.py:24
  28.7 1.2 %collective-permute-start.11 = (bf16[16,2176]{1,0:T(8,128)(2,1)S(1)}, bf16[16,2176]{1,0:T(8,128)(2,1)S(1)}, u32[]{:S(2)}, u32[]{:S(2)}) collective-permute-start(bf16[16,2176]{1,0:T(8,128)(2,1)S(1)} %get-tuple-element.43), channel_id=1, source_target_pairs={{0,6},{1,7},{2,4},{3,5},{4,2},{5,3},{6,0},{7,1},{8,14},{9,15},{10,... | collective-permute-start | bytes 208904 | tf_op jit(solution)/shard_map/ppermute | solution.py:24
  29.9 0.8 %collective-permute-start.9 = (bf16[16,2176]{1,0:T(8,128)(2,1)S(1)}, bf16[16,2176]{1,0:T(8,128)(2,1)S(1)}, u32[]{:S(2)}, u32[]{:S(2)}) collective-permute-start(bf16[16,2176]{1,0:T(8,128)(2,1)S(1)} %get-tuple-element.42), channel_id=1, source_target_pairs={{0,2},{1,3},{2,0},{3,1},{4,6},{5,7},{6,4},{7,5},{8,10},{9,11},{10,... | collective-permute-start | bytes 208904 | tf_op jit(solution)/shard_map/ppermute | solution.py:24
  30.7 0.8 %collective-permute-done.16 = bf16[16,2048]{1,0:T(8,128)(2,1)S(1)} collective-permute-done((bf16[16,2048]{1,0:T(8,128)(2,1)S(1)}, bf16[16,2048]{1,0:T(8,128)(2,1)S(1)}, u32[]{:S(2)}, u32[]{:S(2)}) %collective-permute-start.16) | collective-permute-done | bytes 65568 | tf_op jit(solution)/shard_map/ppermute | solution.py:24
  31.5 3.7 %collective-permute-start.17 = (bf16[16,2048]{1,0:T(8,128)(2,1)S(1)}, bf16[16,2048]{1,0:T(8,128)(2,1)S(1)}, u32[]{:S(2)}, u32[]{:S(2)}) collective-permute-start(bf16[16,2048]{1,0:T(8,128)(2,1)S(1)} %add_convert_fusion.2), channel_id=1, source_target_pairs={{0,24},{8,0},{16,8},{24,16},{1,25},{9,1},{17,9},{25,17},{2,26},{10... | collective-permute-start | bytes 196616 | tf_op jit(solution)/shard_map/ppermute | solution.py:19
  35.2 0.1 slice_add_fusion
  35.3 2.6 %collective-permute-start.12 = (bf16[16,2048]{1,0:T(8,128)(2,1)S(1)}, bf16[16,2048]{1,0:T(8,128)(2,1)S(1)}, u32[]{:S(2)}, u32[]{:S(2)}) collective-permute-start(bf16[16,2048]{1,0:T(8,128)(2,1)S(1)} %slice.72), channel_id=1, source_target_pairs={{0,24},{8,0},{16,8},{24,16},{1,25},{9,1},{17,9},{25,17},{2,26},{10... | collective-permute-start | bytes 196616 | tf_op jit(solution)/shard_map/ppermute | solution.py:19
  38.0 0.7 %select_reduce_fusion = f32[16,2]{0,1:T(2,128)} fusion(f32[16,64]{1,0:T(8,128)S(1)} %slice_add_fusion, s32[16,2]{0,1:T(2,128)S(1)} %bitcast.35), kind=kLoop, calls=%fused_computation.14 | loop fusion | flops 6112 | bytes 4352 | tf_op jit(solution)/shard_map/reduce_sum | solution.py:222
  38.7 1.2 %collective-permute-done.12 = bf16[16,2048]{1,0:T(8,128)(2,1)S(1)} collective-permute-done((bf16[16,2048]{1,0:T(8,128)(2,1)S(1)}, bf16[16,2048]{1,0:T(8,128)(2,1)S(1)}, u32[]{:S(2)}, u32[]{:S(2)}) %collective-permute-start.12) | collective-permute-done | bytes 65568 | tf_op jit(solution)/shard_map/ppermute | solution.py:19
  39.9 0.7 %maximum_bitcast_fusion = bf16[1,16,4096]{2,1,0:T(8,128)(2,1)} fusion(bf16[16,2048]{1,0:T(8,128)(2,1)S(1)} %collective-permute-done.17, bf16[16,2048]{1,0:T(8,128)(2,1)S(1)} %collective-permute-done.12), kind=kLoop, calls=%fused_computation.4 | loop fusion | flops 262144 | bytes 262144 | tf_op jit(solution)/shard_map/broadcast_in_dim | solution.py:223
  (48 shorter events, 0.6 us)
Async XLA Ops:
  0.6 10.2 %collective-permute-start.3 = (bf16[16,4096]{1,0:T(8,128)(2,1)}, bf16[16,4096]{1,0:T(8,128)(2,1)S(1)}, u32[]{:S(2)}, u32[]{:S(2)}) collective-permute-start(bf16[16,4096]{1,0:T(8,128)(2,1)} %bitcast.30), channel_id=1, source_target_pairs={{0,2},{1,3},{2,0},{3,1},{4,6},{5,7},{6,4},{7,5},{8,10},{9,11},{10,... | collective-permute-start | bytes 393224 | tf_op jit(solution)/shard_map/ppermute | solution.py:24
  3.6 11.0 %collective-permute-start.5 = (bf16[16,4096]{1,0:T(8,128)(2,1)}, bf16[16,4096]{1,0:T(8,128)(2,1)S(1)}, u32[]{:S(2)}, u32[]{:S(2)}) collective-permute-start(bf16[16,4096]{1,0:T(8,128)(2,1)} %bitcast.31), channel_id=1, source_target_pairs={{0,4},{1,5},{2,6},{3,7},{4,0},{5,1},{6,2},{7,3},{8,12},{9,13},{10,... | collective-permute-start | bytes 393224 | tf_op jit(solution)/shard_map/ppermute | solution.py:24
  5.2 9.5 %collective-permute-start.6 = (bf16[16,4096]{1,0:T(8,128)(2,1)}, bf16[16,4096]{1,0:T(8,128)(2,1)S(1)}, u32[]{:S(2)}, u32[]{:S(2)}) collective-permute-start(bf16[16,4096]{1,0:T(8,128)(2,1)} %bitcast.32), channel_id=1, source_target_pairs={{0,6},{1,7},{2,4},{3,5},{4,2},{5,3},{6,0},{7,1},{8,14},{9,15},{10,... | collective-permute-start | bytes 393224 | tf_op jit(solution)/shard_map/ppermute | solution.py:24
  5.2 7.7 %slice-start = ((s8[6291456]{0:T(1024)(128)(4,1)}), s8[4194304]{0:T(1024)(128)(4,1)S(1)}, s32[]{:S(2)}) async-start(s8[6291456]{0:T(1024)(128)(4,1)} %bitcast.19), calls=%async_computation | async-start | bytes 8388608
  5.2 0.8 %copy-start.1 = (bf16[1,16,2]{1,2,0:T(2,128)(2,1)S(1)}, bf16[1,16,2]{1,2,0:T(2,128)(2,1)}, u32[]{:S(2)}) copy-start(bf16[1,16,2]{1,2,0:T(2,128)(2,1)} %param.10) | copy-start | bytes 196
  6.0 5.2 %copy-start = (bf16[1,768,4096]{2,1,0:T(8,128)(2,1)S(1)}, bf16[1,768,4096]{2,1,0:T(8,128)(2,1)}, u32[]{:S(2)}) copy-start(bf16[1,768,4096]{2,1,0:T(8,128)(2,1)} %param.11) | copy-start | bytes 18874372
  6.0 6.9 %slice-start.1 = ((s8[6291456]{0:T(1024)(128)(4,1)}), s8[2097152]{0:T(1024)(128)(4,1)S(1)}, s32[]{:S(2)}) async-start(s8[6291456]{0:T(1024)(128)(4,1)} %bitcast.19), calls=%async_computation.1 | async-start | bytes 4194304
  7.3 9.1 %collective-permute-start = (bf16[16,4224]{1,0:T(8,128)(2,1)S(1)}, bf16[16,4224]{1,0:T(8,128)(2,1)S(1)}, u32[]{:S(2)}, u32[]{:S(2)}) collective-permute-start(bf16[16,4224]{1,0:T(8,128)(2,1)S(1)} %shard_map.86), channel_id=1, source_target_pairs={{0,2},{1,3},{2,0},{3,1},{4,6},{5,7},{6,4},{7,5},{8,10},{9,11},{10,... | collective-permute-start | bytes 405512 | tf_op jit(solution)/shard_map/ppermute | solution.py:24
  9.4 8.1 %collective-permute-start.1 = (bf16[16,4224]{1,0:T(8,128)(2,1)S(1)}, bf16[16,4224]{1,0:T(8,128)(2,1)S(1)}, u32[]{:S(2)}, u32[]{:S(2)}) collective-permute-start(bf16[16,4224]{1,0:T(8,128)(2,1)S(1)} %shard_map.86), channel_id=1, source_target_pairs={{0,4},{1,5},{2,6},{3,7},{4,0},{5,1},{6,2},{7,3},{8,12},{9,13},{10,... | collective-permute-start | bytes 405512 | tf_op jit(solution)/shard_map/ppermute | solution.py:24
  10.9 6.5 %collective-permute-start.2 = (bf16[16,4224]{1,0:T(8,128)(2,1)S(1)}, bf16[16,4224]{1,0:T(8,128)(2,1)S(1)}, u32[]{:S(2)}, u32[]{:S(2)}) collective-permute-start(bf16[16,4224]{1,0:T(8,128)(2,1)S(1)} %shard_map.86), channel_id=1, source_target_pairs={{0,6},{1,7},{2,4},{3,5},{4,2},{5,3},{6,0},{7,1},{8,14},{9,15},{10,... | collective-permute-start | bytes 405512 | tf_op jit(solution)/shard_map/ppermute | solution.py:24
  11.2 3.6 %slice-start.2 = ((s8[6291456]{0:T(1024)(128)(4,1)}), s8[4194304]{0:T(1024)(128)(4,1)S(1)}, s32[]{:S(2)}) async-start(s8[6291456]{0:T(1024)(128)(4,1)} %bitcast.25), calls=%async_computation.2 | async-start | bytes 8388608
  12.9 1.7 %copy-start.2 = (bf16[1,16,4096]{2,1,0:T(8,128)(2,1)S(1)}, bf16[1,16,4096]{2,1,0:T(8,128)(2,1)}, u32[]{:S(2)}) copy-start(bf16[1,16,4096]{2,1,0:T(8,128)(2,1)} %param.7) | copy-start | bytes 393220
  12.9 1.9 %slice-start.3 = ((s8[6291456]{0:T(1024)(128)(4,1)}), s8[2097152]{0:T(1024)(128)(4,1)S(1)}, s32[]{:S(2)}) async-start(s8[6291456]{0:T(1024)(128)(4,1)} %bitcast.25), calls=%async_computation.3 | async-start | bytes 4194304
  14.7 2.9 %collective-permute-start.7 = (bf16[64,4096]{1,0:T(8,128)(2,1)S(1)}, bf16[64,4096]{1,0:T(8,128)(2,1)S(1)}, u32[]{:S(2)}, u32[]{:S(2)}) collective-permute-start(bf16[64,4096]{1,0:T(8,128)(2,1)S(1)} %constant_dynamic-update-slice_fusion.4.near_ref), channel_id=1, source_target_pairs={{0,1},{1,0},{2,3},{3,2},{4,5},{5,4},{6,7},{7,6},{8,9},{9,8},{10,11... | collective-permute-start | bytes 1572872 | tf_op jit(solution)/shard_map/ppermute | solution.py:24
  17.5 2.0 %collective-permute-start.4 = (bf16[64,4224]{1,0:T(8,128)(2,1)S(1)}, bf16[64,4224]{1,0:T(8,128)(2,1)S(1)}, u32[]{:S(2)}, u32[]{:S(2)}) collective-permute-start(bf16[64,4224]{1,0:T(8,128)(2,1)S(1)} %constant_dynamic-update-slice_fusion.near_ref), channel_id=1, source_target_pairs={{0,1},{1,0},{2,3},{3,2},{4,5},{5,4},{6,7},{7,6},{8,9},{9,8},{10,11... | collective-permute-start | bytes 1622024 | tf_op jit(solution)/shard_map/ppermute | solution.py:24
  21.7 16.3 %copy-start.3 = (s32[1,16,2]{1,2,0:T(2,128)S(1)}, s32[1,16,2]{1,2,0:T(2,128)}, u32[]{:S(2)}) copy-start(s32[1,16,2]{1,2,0:T(2,128)} %param.9) | copy-start | bytes 388
  21.7 1.7 %collective-permute-start.13 = (bf16[64,2048]{1,0:T(8,128)(2,1)S(1)}, bf16[64,2048]{1,0:T(8,128)(2,1)S(1)}, u32[]{:S(2)}, u32[]{:S(2)}) collective-permute-start(bf16[64,2048]{1,0:T(8,128)(2,1)S(1)} %get-tuple-element.41), channel_id=1, source_target_pairs={{0,1},{1,0},{2,3},{3,2},{4,5},{5,4},{6,7},{7,6},{8,9},{9,8},{10,11... | collective-permute-start | bytes 786440 | tf_op jit(solution)/shard_map/ppermute | solution.py:24
  23.2 3.8 %collective-permute-start.8 = (bf16[64,2176]{1,0:T(8,128)(2,1)S(1)}, bf16[64,2176]{1,0:T(8,128)(2,1)S(1)}, u32[]{:S(2)}, u32[]{:S(2)}) collective-permute-start(bf16[64,2176]{1,0:T(8,128)(2,1)S(1)} %get-tuple-element.39), channel_id=1, source_target_pairs={{0,1},{1,0},{2,3},{3,2},{4,5},{5,4},{6,7},{7,6},{8,9},{9,8},{10,11... | collective-permute-start | bytes 835592 | tf_op jit(solution)/shard_map/ppermute | solution.py:24
  23.5 6.4 %collective-permute-start.14 = (bf16[16,2048]{1,0:T(8,128)(2,1)S(1)}, bf16[16,2048]{1,0:T(8,128)(2,1)S(1)}, u32[]{:S(2)}, u32[]{:S(2)}) collective-permute-start(bf16[16,2048]{1,0:T(8,128)(2,1)S(1)} %get-tuple-element.45), channel_id=1, source_target_pairs={{0,2},{1,3},{2,0},{3,1},{4,6},{5,7},{6,4},{7,5},{8,10},{9,11},{10,... | collective-permute-start | bytes 196616 | tf_op jit(solution)/shard_map/ppermute | solution.py:24
  24.8 5.9 %collective-permute-start.15 = (bf16[16,2048]{1,0:T(8,128)(2,1)S(1)}, bf16[16,2048]{1,0:T(8,128)(2,1)S(1)}, u32[]{:S(2)}, u32[]{:S(2)}) collective-permute-start(bf16[16,2048]{1,0:T(8,128)(2,1)S(1)} %get-tuple-element.47), channel_id=1, source_target_pairs={{0,4},{1,5},{2,6},{3,7},{4,0},{5,1},{6,2},{7,3},{8,12},{9,13},{10,... | collective-permute-start | bytes 196616 | tf_op jit(solution)/shard_map/ppermute | solution.py:24
  26.2 5.2 %collective-permute-start.16 = (bf16[16,2048]{1,0:T(8,128)(2,1)S(1)}, bf16[16,2048]{1,0:T(8,128)(2,1)S(1)}, u32[]{:S(2)}, u32[]{:S(2)}) collective-permute-start(bf16[16,2048]{1,0:T(8,128)(2,1)S(1)} %get-tuple-element.46), channel_id=1, source_target_pairs={{0,6},{1,7},{2,4},{3,5},{4,2},{5,3},{6,0},{7,1},{8,14},{9,15},{10,... | collective-permute-start | bytes 196616 | tf_op jit(solution)/shard_map/ppermute | solution.py:24
  27.2 8.0 %collective-permute-start.10 = (bf16[16,2176]{1,0:T(8,128)(2,1)S(1)}, bf16[16,2176]{1,0:T(8,128)(2,1)S(1)}, u32[]{:S(2)}, u32[]{:S(2)}) collective-permute-start(bf16[16,2176]{1,0:T(8,128)(2,1)S(1)} %get-tuple-element.44), channel_id=1, source_target_pairs={{0,4},{1,5},{2,6},{3,7},{4,0},{5,1},{6,2},{7,3},{8,12},{9,13},{10,... | collective-permute-start | bytes 208904 | tf_op jit(solution)/shard_map/ppermute | solution.py:24
  28.7 6.4 %collective-permute-start.11 = (bf16[16,2176]{1,0:T(8,128)(2,1)S(1)}, bf16[16,2176]{1,0:T(8,128)(2,1)S(1)}, u32[]{:S(2)}, u32[]{:S(2)}) collective-permute-start(bf16[16,2176]{1,0:T(8,128)(2,1)S(1)} %get-tuple-element.43), channel_id=1, source_target_pairs={{0,6},{1,7},{2,4},{3,5},{4,2},{5,3},{6,0},{7,1},{8,14},{9,15},{10,... | collective-permute-start | bytes 208904 | tf_op jit(solution)/shard_map/ppermute | solution.py:24
  29.9 5.3 %collective-permute-start.9 = (bf16[16,2176]{1,0:T(8,128)(2,1)S(1)}, bf16[16,2176]{1,0:T(8,128)(2,1)S(1)}, u32[]{:S(2)}, u32[]{:S(2)}) collective-permute-start(bf16[16,2176]{1,0:T(8,128)(2,1)S(1)} %get-tuple-element.42), channel_id=1, source_target_pairs={{0,2},{1,3},{2,0},{3,1},{4,6},{5,7},{6,4},{7,5},{8,10},{9,11},{10,... | collective-permute-start | bytes 208904 | tf_op jit(solution)/shard_map/ppermute | solution.py:24
  31.5 7.2 %collective-permute-start.17 = (bf16[16,2048]{1,0:T(8,128)(2,1)S(1)}, bf16[16,2048]{1,0:T(8,128)(2,1)S(1)}, u32[]{:S(2)}, u32[]{:S(2)}) collective-permute-start(bf16[16,2048]{1,0:T(8,128)(2,1)S(1)} %add_convert_fusion.2), channel_id=1, source_target_pairs={{0,24},{8,0},{16,8},{24,16},{1,25},{9,1},{17,9},{25,17},{2,26},{10... | collective-permute-start | bytes 196616 | tf_op jit(solution)/shard_map/ppermute | solution.py:19
  35.3 4.5 %collective-permute-start.12 = (bf16[16,2048]{1,0:T(8,128)(2,1)S(1)}, bf16[16,2048]{1,0:T(8,128)(2,1)S(1)}, u32[]{:S(2)}, u32[]{:S(2)}) collective-permute-start(bf16[16,2048]{1,0:T(8,128)(2,1)S(1)} %slice.72), channel_id=1, source_target_pairs={{0,24},{8,0},{16,8},{24,16},{1,25},{9,1},{17,9},{25,17},{2,26},{10... | collective-permute-start | bytes 196616 | tf_op jit(solution)/shard_map/ppermute | solution.py:19

commit v5 on v4

--- a/solution.py
+++ b/solution.py
@@ -34,6 +34,15 @@
 
 def rows_of(near_ref, far_ref, columns):
     return jnp.concatenate([near_ref[:, columns], far_ref[:, columns]], axis=0)
+
+
+def flip_pair_kernel(after_ref, gate_ref, up_ref, out_ref):
+    step = 512
+    hidden, width = gate_ref.shape
+    for start in range(0, width, step):
+        columns = pl.ds(start, min(step, width - start))
+        out_ref[columns, :hidden] = gate_ref[:, columns].T
+        out_ref[columns, hidden:] = up_ref[:, columns].T
 
 
 def flip_kernel(after_ref, mat_ref, out_ref):
@@ -68,9 +77,11 @@
     copies[1].wait()
 
 
-def first_kernel(near_ref, far_ref, gate_ref, up_ref, gate_pre_ref, up_pre_ref):
-    gate_pre_ref[...] = products(near_ref, far_ref, gate_ref)
-    up_pre_ref[...] = products(near_ref, far_ref, up_ref)
+def first_kernel(near_ref, far_ref, pair_ref, gate_pre_ref, up_pre_ref):
+    both = products(near_ref, far_ref, pair_ref)
+    hidden = gate_pre_ref.shape[1]
+    gate_pre_ref[...] = both[:, :hidden]
+    up_pre_ref[...] = both[:, hidden:]
 
 
 def second_kernel(
@@ -166,23 +177,30 @@
         compiler_params=params(4),
     )
     after = resident(parts_x[1])
-    gate_flipped = resident(flip(after, gate_mat))
-    up_flipped = resident(flip(after, up_mat))
+    pair = resident(
+        pl.pallas_call(
+            flip_pair_kernel,
+            out_shape=jax.ShapeDtypeStruct((width, 2 * hidden), jnp.bfloat16),
+            in_specs=[VMEM] * 3,
+            out_specs=VMEM,
+            compiler_params=params(4),
+        )(after, gate_mat, up_mat)
+    )
     down_flipped = resident(flip(after, down_mat))
-    parts_x, gate_flipped, up_flipped = lax.optimization_barrier((parts_x, gate_flipped, up_flipped))
+    parts_x, pair = lax.optimization_barrier((parts_x, pair))
     near_x = jnp.concatenate(parts_x, axis=0)
     far_x = swapped(near_x, 1)
     pre = jax.ShapeDtypeStruct((2 * half, hidden), jnp.float32)
     gate_pre, up_pre = pl.pallas_call(
         first_kernel,
         out_shape=(pre, pre),
-        in_specs=[VMEM] * 4,
+        in_specs=[VMEM] * 3,
         out_specs=(VMEM,) * 2,
         compiler_params=params(8),
         cost_estimate=pl.CostEstimate(
             flops=8 * half * hidden * width, bytes_accessed=0, transcendentals=0
         ),
-    )(resident(near_x), resident(far_x), gate_flipped, up_flipped)
+    )(resident(near_x), resident(far_x), pair)
     parts_dy, down_flipped = lax.optimization_barrier((parts_dy, down_flipped))
     near_dy = jnp.concatenate(parts_dy, axis=0)
     far_dy = swapped(near_dy, 1)

time: 40.7 us -> 40.6 us (level)
  starting transfers between devices: 22.6 us -> 23.4 us
    ppermute x2, starting transfers between devices: 6.29 us -> 6.75 us  [shifted(): lax.ppermute(array, axis, [(i, (i + by) % peers) for i in range(peers)])]
    ppermute x16, starting transfers between devices: 16.3 us -> 16.7 us  [swapped(): return lax.ppermute(array, 'expert', [(i, i ^ bits) for i in range(peers)])]
    unnamed x22 -> x20, local copies, waits for them, and re-layouts: 0.92 us -> 0.76 us
    pallas_call x3 -> x2, Pallas kernels: 5.21 us -> 5.09 us  [the longest x1 3.29 us: on_device(): pl.pallas_call(flip_pair_kernel, out_shape=jax.ShapeDtypeStruct((width, 2...]
  transfers between devices with their start and end apart: 18 -> 18, of which waited for: 4 -> 4; matrix products, arithmetic and copies ran while one was open for 3% -> 3% of each run, Pallas kernels for 23% -> 22%
where the time goes in v5:
time: 40.6 us; the launch traced here: 40.5 us
  starting transfers between devices  23.4 us (58%)
  Pallas kernels  11 us (27%)
  waiting for transfers between devices  2.65 us (7%)
  other arithmetic  1.66 us (4%)
  between operations  0.89 us (2%)
  local copies, waits for them, and re-layouts  0.83 us (2%)
    ppermute x16, starting transfers between devices, swapped(): return lax.ppermute(array, 'expert', [(i, i ^ bits) for i in range(peers)])  16.7 us
    ppermute x2, starting transfers between devices, shifted(): lax.ppermute(array, axis, [(i, (i + by) % peers) for i in range(peers)])  6.75 us
    pallas_call x1, Pallas kernels, on_device(): pl.pallas_call(flip_pair_kernel, out_shape=jax.ShapeDtypeStruct((width, 2...  3.29 us
    pallas_call x2, Pallas kernels, on_device(): pl.pallas_call(functools.partial(third_kernel, chunk * span, span), out_s...  1.98 us
    pallas_call x1, Pallas kernels, on_device(): pl.pallas_call(first_kernel, out_shape=(pre, pre), in_specs=[VMEM] * 3, o...  1.8 us
    pallas_call x1, Pallas kernels, on_device(): down_flipped = resident(flip(after, down_mat))  1.67 us
    ppermute x16, waiting for transfers between devices, swapped(): return lax.ppermute(array, 'expert', [(i, i ^ bits) for i in range(peers)])  1.47 us
    ppermute x2, waiting for transfers between devices, shifted(): lax.ppermute(array, axis, [(i, (i + by) % peers) for i in range(peers)])  1.18 us
  transfers between devices with their start and end apart: 18, of which 4 were waited for; matrix products, arithmetic and copies ran while one was open for 3% of the time, Pallas kernels for 22%

profile of v5, /device:TPU:0, one launch (start us, length us, event | category | flops | bytes accessed | tf_op | source)
XLA Modules:
  0.0 40.5 jit_solution(17601184977555090267)
XLA Ops:
  0.6 3.0 %collective-permute-start.3 = (bf16[16,4096]{1,0:T(8,128)(2,1)}, bf16[16,4096]{1,0:T(8,128)(2,1)S(1)}, u32[]{:S(2)}, u32[]{:S(2)}) collective-permute-start(bf16[16,4096]{1,0:T(8,128)(2,1)} %bitcast.28), channel_id=1, source_target_pairs={{0,2},{1,3},{2,0},{3,1},{4,6},{5,7},{6,4},{7,5},{8,10},{9,11},{10,... | collective-permute-start | bytes 393224 | tf_op jit(solution)/shard_map/ppermute | solution.py:24
  3.6 1.5 %collective-permute-start.5 = (bf16[16,4096]{1,0:T(8,128)(2,1)}, bf16[16,4096]{1,0:T(8,128)(2,1)S(1)}, u32[]{:S(2)}, u32[]{:S(2)}) collective-permute-start(bf16[16,4096]{1,0:T(8,128)(2,1)} %bitcast.29), channel_id=1, source_target_pairs={{0,4},{1,5},{2,6},{3,7},{4,0},{5,1},{6,2},{7,3},{8,12},{9,13},{10,... | collective-permute-start | bytes 393224 | tf_op jit(solution)/shard_map/ppermute | solution.py:24
  5.2 0.7 %copy-done.2 = bf16[1,16,2]{1,2,0:T(2,128)(2,1)S(1)} copy-done((bf16[1,16,2]{1,2,0:T(2,128)(2,1)S(1)}, bf16[1,16,2]{1,2,0:T(2,128)(2,1)}, u32[]{:S(2)}) %copy-start.2) | copy-done | bytes 88
  5.8 1.1 %shard_map.86 = bf16[16,4224]{1,0:T(8,128)(2,1)S(1)} custom-call(bf16[16,4096]{1,0:T(8,128)(2,1)} %bitcast.27, s32[2,16]{1,0:T(2,128)} %bitcast.32, bf16[2,16]{1,0:T(2,128)(2,1)S(1)} %bitcast.26, bf16[768,4096]{1,0:T(8,128)(2,1)} %bitcast.14, bf16[768,4096]{1,0:T(8,128)(2,1)} %bitcast.18, bf16[768,4096]{1,0:T(8,128)(2,1)} %bitcast.22), custom_call_target="tpu_custom_call" | custom-call | bytes 37748736 | tf_op jit(solution)/shard_map/pallas_call | solution.py:154
  7.0 2.0 %collective-permute-start = (bf16[16,4224]{1,0:T(8,128)(2,1)S(1)}, bf16[16,4224]{1,0:T(8,128)(2,1)S(1)}, u32[]{:S(2)}, u32[]{:S(2)}) collective-permute-start(bf16[16,4224]{1,0:T(8,128)(2,1)S(1)} %shard_map.86), channel_id=1, source_target_pairs={{0,2},{1,3},{2,0},{3,1},{4,6},{5,7},{6,4},{7,5},{8,10},{9,11},{10,... | collective-permute-start | bytes 405512 | tf_op jit(solution)/shard_map/ppermute | solution.py:24
  9.0 1.5 %collective-permute-start.1 = (bf16[16,4224]{1,0:T(8,128)(2,1)S(1)}, bf16[16,4224]{1,0:T(8,128)(2,1)S(1)}, u32[]{:S(2)}, u32[]{:S(2)}) collective-permute-start(bf16[16,4224]{1,0:T(8,128)(2,1)S(1)} %shard_map.86), channel_id=1, source_target_pairs={{0,4},{1,5},{2,6},{3,7},{4,0},{5,1},{6,2},{7,3},{8,12},{9,13},{10,... | collective-permute-start | bytes 405512 | tf_op jit(solution)/shard_map/ppermute | solution.py:24
  10.5 0.7 %collective-permute-start.2 = (bf16[16,4224]{1,0:T(8,128)(2,1)S(1)}, bf16[16,4224]{1,0:T(8,128)(2,1)S(1)}, u32[]{:S(2)}, u32[]{:S(2)}) collective-permute-start(bf16[16,4224]{1,0:T(8,128)(2,1)S(1)} %shard_map.86), channel_id=1, source_target_pairs={{0,6},{1,7},{2,4},{3,5},{4,2},{5,3},{6,0},{7,1},{8,14},{9,15},{10,... | collective-permute-start | bytes 405512 | tf_op jit(solution)/shard_map/ppermute | solution.py:24
  11.2 3.3 %shard_map.88.pair_ref = bf16[4096,1536]{1,0:T(8,128)(2,1)S(1)} custom-call(bf16[16,4096]{1,0:T(8,128)(2,1)S(1)} %collective-permute-done.3.after_ref, bf16[768,4096]{1,0:T(8,128)(2,1)S(1)} %bitcast.15, bf16[768,4096]{1,0:T(8,128)(2,1)S(1)} %bitcast.19), custom_call_target="tpu_custom_call" | custom-call | tf_op jit(solution)/shard_map/pallas_call | solution.py:181
  14.6 0.1 collective-permute-start.7
  14.7 1.7 %shard_map.87.down_ref = bf16[4096,768]{1,0:T(8,128)(2,1)S(1)} custom-call(bf16[16,4096]{1,0:T(8,128)(2,1)S(1)} %collective-permute-done.3.after_ref, bf16[768,4096]{1,0:T(8,128)(2,1)S(1)} %bitcast.25), custom_call_target="tpu_custom_call" | custom-call | tf_op jit(solution)/shard_map/pallas_call | solution.py:189
  16.4 1.0 %collective-permute-done.1 = bf16[16,4224]{1,0:T(8,128)(2,1)S(1)} collective-permute-done((bf16[16,4224]{1,0:T(8,128)(2,1)S(1)}, bf16[16,4224]{1,0:T(8,128)(2,1)S(1)}, u32[]{:S(2)}, u32[]{:S(2)}) %collective-permute-start.1) | collective-permute-done | bytes 135200 | tf_op jit(solution)/shard_map/ppermute | solution.py:24
  17.5 0.1 collective-permute-start.4
  17.6 1.8 %shard_map.89 = (f32[128,768]{1,0:T(8,128)S(1)}, f32[128,768]{1,0:T(8,128)S(1)}) custom-call(bf16[64,4096]{1,0:T(8,128)(2,1)S(1)} %constant_dynamic-update-slice_fusion.4.near_ref, bf16[64,4096]{1,0:T(8,128)(2,1)S(1)} %collective-permute-done.7.far_ref, bf16[4096,1536]{1,0:T(8,128)(2,1)S(1)} %shard_map.88.pair_ref), custom_call_target="tpu_custom_call" | custom-call | flops 1610612736 | tf_op jit(solution)/shard_map/pallas_call | solution.py:194
  19.4 0.1 collective-permute-done.4.far_ref
  19.5 1.2 %shard_map.90 = (bf16[128,768]{1,0:T(8,128)(2,1)S(1)}, bf16[128,768]{1,0:T(8,128)(2,1)S(1)}, bf16[128,128]{1,0:T(8,128)(2,1)S(1)}) custom-call(bf16[64,4224]{1,0:T(8,128)(2,1)S(1)} %constant_dynamic-update-slice_fusion.near_ref, bf16[64,4224]{1,0:T(8,128)(2,1)S(1)} %collective-permute-done.4.far_ref, bf16[4096,768]{1,0:T(8,128)(2,1)S(1)} %shard_map.87.down_ref, ...), custom_call_target="tpu_custom_call" | custom-call | tf_op jit(solution)/shard_map/pallas_call | solution.py:208
  20.7 1.0 %shard_map.92 = (bf16[64,2048]{1,0:T(8,128)(2,1)S(1)}, bf16[64,2048]{1,0:T(8,128)(2,1)S(1)}) custom-call(bf16[128,768]{1,0:T(8,128)(2,1)S(1)} %get-tuple-element.33.grad_gate_ref, bf16[128,768]{1,0:T(8,128)(2,1)S(1)} %get-tuple-element.34.grad_up_ref, bf16[768,4096]{1,0:T(8,128)(2,1)S(1)} %bitcast.16, bf16[768,4096]{1,0:T(8,128)(2,1)S(1)} %bitcast.20, ...), custom_call_target="tpu_custom_call" | custom-call | tf_op jit(solution)/shard_map/pallas_call | solution.py:221
  21.7 0.5 %collective-permute-start.13 = (bf16[64,2048]{1,0:T(8,128)(2,1)S(1)}, bf16[64,2048]{1,0:T(8,128)(2,1)S(1)}, u32[]{:S(2)}, u32[]{:S(2)}) collective-permute-start(bf16[64,2048]{1,0:T(8,128)(2,1)S(1)} %get-tuple-element.39), channel_id=1, source_target_pairs={{0,1},{1,0},{2,3},{3,2},{4,5},{5,4},{6,7},{7,6},{8,9},{9,8},{10,11... | collective-permute-start | bytes 786440 | tf_op jit(solution)/shard_map/ppermute | solution.py:24
  22.1 1.0 %shard_map.91 = (bf16[64,2176]{1,0:T(8,128)(2,1)S(1)}, bf16[64,2176]{1,0:T(8,128)(2,1)S(1)}) custom-call(bf16[128,768]{1,0:T(8,128)(2,1)S(1)} %get-tuple-element.33.grad_gate_ref, bf16[128,768]{1,0:T(8,128)(2,1)S(1)} %get-tuple-element.34.grad_up_ref, bf16[768,4096]{1,0:T(8,128)(2,1)S(1)} %bitcast.17, bf16[768,4096]{1,0:T(8,128)(2,1)S(1)} %bitcast.21, ...), custom_call_target="tpu_custom_call" | custom-call | tf_op jit(solution)/shard_map/pallas_call | solution.py:221
  23.1 0.2 collective-permute-start.8
  23.4 1.3 %collective-permute-start.14 = (bf16[16,2048]{1,0:T(8,128)(2,1)S(1)}, bf16[16,2048]{1,0:T(8,128)(2,1)S(1)}, u32[]{:S(2)}, u32[]{:S(2)}) collective-permute-start(bf16[16,2048]{1,0:T(8,128)(2,1)S(1)} %get-tuple-element.43), channel_id=1, source_target_pairs={{0,2},{1,3},{2,0},{3,1},{4,6},{5,7},{6,4},{7,5},{8,10},{9,11},{10,... | collective-permute-start | bytes 196616 | tf_op jit(solution)/shard_map/ppermute | solution.py:24
  24.7 1.0 %collective-permute-start.15 = (bf16[16,2048]{1,0:T(8,128)(2,1)S(1)}, bf16[16,2048]{1,0:T(8,128)(2,1)S(1)}, u32[]{:S(2)}, u32[]{:S(2)}) collective-permute-start(bf16[16,2048]{1,0:T(8,128)(2,1)S(1)} %get-tuple-element.45), channel_id=1, source_target_pairs={{0,4},{1,5},{2,6},{3,7},{4,0},{5,1},{6,2},{7,3},{8,12},{9,13},{10,... | collective-permute-start | bytes 196616 | tf_op jit(solution)/shard_map/ppermute | solution.py:24
  25.7 1.3 %collective-permute-start.16 = (bf16[16,2048]{1,0:T(8,128)(2,1)S(1)}, bf16[16,2048]{1,0:T(8,128)(2,1)S(1)}, u32[]{:S(2)}, u32[]{:S(2)}) collective-permute-start(bf16[16,2048]{1,0:T(8,128)(2,1)S(1)} %get-tuple-element.44), channel_id=1, source_target_pairs={{0,6},{1,7},{2,4},{3,5},{4,2},{5,3},{6,0},{7,1},{8,14},{9,15},{10,... | collective-permute-start | bytes 196616 | tf_op jit(solution)/shard_map/ppermute | solution.py:24
  27.1 1.6 %collective-permute-start.10 = (bf16[16,2176]{1,0:T(8,128)(2,1)S(1)}, bf16[16,2176]{1,0:T(8,128)(2,1)S(1)}, u32[]{:S(2)}, u32[]{:S(2)}) collective-permute-start(bf16[16,2176]{1,0:T(8,128)(2,1)S(1)} %get-tuple-element.42), channel_id=1, source_target_pairs={{0,4},{1,5},{2,6},{3,7},{4,0},{5,1},{6,2},{7,3},{8,12},{9,13},{10,... | collective-permute-start | bytes 208904 | tf_op jit(solution)/shard_map/ppermute | solution.py:24
  28.7 1.1 %collective-permute-start.11 = (bf16[16,2176]{1,0:T(8,128)(2,1)S(1)}, bf16[16,2176]{1,0:T(8,128)(2,1)S(1)}, u32[]{:S(2)}, u32[]{:S(2)}) collective-permute-start(bf16[16,2176]{1,0:T(8,128)(2,1)S(1)} %get-tuple-element.41), channel_id=1, source_target_pairs={{0,6},{1,7},{2,4},{3,5},{4,2},{5,3},{6,0},{7,1},{8,14},{9,15},{10,... | collective-permute-start | bytes 208904 | tf_op jit(solution)/shard_map/ppermute | solution.py:24
  29.8 0.8 %collective-permute-start.9 = (bf16[16,2176]{1,0:T(8,128)(2,1)S(1)}, bf16[16,2176]{1,0:T(8,128)(2,1)S(1)}, u32[]{:S(2)}, u32[]{:S(2)}) collective-permute-start(bf16[16,2176]{1,0:T(8,128)(2,1)S(1)} %get-tuple-element.40), channel_id=1, source_target_pairs={{0,2},{1,3},{2,0},{3,1},{4,6},{5,7},{6,4},{7,5},{8,10},{9,11},{10,... | collective-permute-start | bytes 208904 | tf_op jit(solution)/shard_map/ppermute | solution.py:24
  30.7 0.3 collective-permute-done.16
  31.0 3.7 %collective-permute-start.17 = (bf16[16,2048]{1,0:T(8,128)(2,1)S(1)}, bf16[16,2048]{1,0:T(8,128)(2,1)S(1)}, u32[]{:S(2)}, u32[]{:S(2)}) collective-permute-start(bf16[16,2048]{1,0:T(8,128)(2,1)S(1)} %add_convert_fusion.2), channel_id=1, source_target_pairs={{0,24},{8,0},{16,8},{24,16},{1,25},{9,1},{17,9},{25,17},{2,26},{10... | collective-permute-start | bytes 196616 | tf_op jit(solution)/shard_map/ppermute | solution.py:19
  34.7 0.1 slice_add_fusion
  34.8 3.1 %collective-permute-start.12 = (bf16[16,2048]{1,0:T(8,128)(2,1)S(1)}, bf16[16,2048]{1,0:T(8,128)(2,1)S(1)}, u32[]{:S(2)}, u32[]{:S(2)}) collective-permute-start(bf16[16,2048]{1,0:T(8,128)(2,1)S(1)} %slice.72), channel_id=1, source_target_pairs={{0,24},{8,0},{16,8},{24,16},{1,25},{9,1},{17,9},{25,17},{2,26},{10... | collective-permute-start | bytes 196616 | tf_op jit(solution)/shard_map/ppermute | solution.py:19
  37.9 0.7 %select_reduce_fusion = f32[16,2]{0,1:T(2,128)} fusion(f32[16,64]{1,0:T(8,128)S(1)} %slice_add_fusion, s32[16,2]{0,1:T(2,128)S(1)} %bitcast.33), kind=kLoop, calls=%fused_computation.14 | loop fusion | flops 6112 | bytes 4352 | tf_op jit(solution)/shard_map/reduce_sum | solution.py:240
  38.6 1.2 %collective-permute-done.12 = bf16[16,2048]{1,0:T(8,128)(2,1)S(1)} collective-permute-done((bf16[16,2048]{1,0:T(8,128)(2,1)S(1)}, bf16[16,2048]{1,0:T(8,128)(2,1)S(1)}, u32[]{:S(2)}, u32[]{:S(2)}) %collective-permute-start.12) | collective-permute-done | bytes 65568 | tf_op jit(solution)/shard_map/ppermute | solution.py:19
  39.8 0.7 %maximum_bitcast_fusion = bf16[1,16,4096]{2,1,0:T(8,128)(2,1)} fusion(bf16[16,2048]{1,0:T(8,128)(2,1)S(1)} %collective-permute-done.17, bf16[16,2048]{1,0:T(8,128)(2,1)S(1)} %collective-permute-done.12), kind=kLoop, calls=%fused_computation.4 | loop fusion | flops 262144 | bytes 262144 | tf_op jit(solution)/shard_map/broadcast_in_dim | solution.py:241
  (44 shorter events, 0.4 us)
Async XLA Ops:
  0.6 9.9 %collective-permute-start.3 = (bf16[16,4096]{1,0:T(8,128)(2,1)}, bf16[16,4096]{1,0:T(8,128)(2,1)S(1)}, u32[]{:S(2)}, u32[]{:S(2)}) collective-permute-start(bf16[16,4096]{1,0:T(8,128)(2,1)} %bitcast.28), channel_id=1, source_target_pairs={{0,2},{1,3},{2,0},{3,1},{4,6},{5,7},{6,4},{7,5},{8,10},{9,11},{10,... | collective-permute-start | bytes 393224 | tf_op jit(solution)/shard_map/ppermute | solution.py:24
  3.6 10.9 %collective-permute-start.5 = (bf16[16,4096]{1,0:T(8,128)(2,1)}, bf16[16,4096]{1,0:T(8,128)(2,1)S(1)}, u32[]{:S(2)}, u32[]{:S(2)}) collective-permute-start(bf16[16,4096]{1,0:T(8,128)(2,1)} %bitcast.29), channel_id=1, source_target_pairs={{0,4},{1,5},{2,6},{3,7},{4,0},{5,1},{6,2},{7,3},{8,12},{9,13},{10,... | collective-permute-start | bytes 393224 | tf_op jit(solution)/shard_map/ppermute | solution.py:24
  5.2 9.3 %collective-permute-start.6 = (bf16[16,4096]{1,0:T(8,128)(2,1)}, bf16[16,4096]{1,0:T(8,128)(2,1)S(1)}, u32[]{:S(2)}, u32[]{:S(2)}) collective-permute-start(bf16[16,4096]{1,0:T(8,128)(2,1)} %bitcast.30), channel_id=1, source_target_pairs={{0,6},{1,7},{2,4},{3,5},{4,2},{5,3},{6,0},{7,1},{8,14},{9,15},{10,... | collective-permute-start | bytes 393224 | tf_op jit(solution)/shard_map/ppermute | solution.py:24
  5.2 0.7 %copy-start.2 = (bf16[1,16,2]{1,2,0:T(2,128)(2,1)S(1)}, bf16[1,16,2]{1,2,0:T(2,128)(2,1)}, u32[]{:S(2)}) copy-start(bf16[1,16,2]{1,2,0:T(2,128)(2,1)} %param.10) | copy-start | bytes 196
  5.8 5.4 %copy-start = (bf16[1,768,4096]{2,1,0:T(8,128)(2,1)S(1)}, bf16[1,768,4096]{2,1,0:T(8,128)(2,1)}, u32[]{:S(2)}) copy-start(bf16[1,768,4096]{2,1,0:T(8,128)(2,1)} %param.11) | copy-start | bytes 18874372
  5.8 5.4 %copy-start.1 = (bf16[1,768,4096]{2,1,0:T(8,128)(2,1)S(1)}, bf16[1,768,4096]{2,1,0:T(8,128)(2,1)}, u32[]{:S(2)}) copy-start(bf16[1,768,4096]{2,1,0:T(8,128)(2,1)} %param.12) | copy-start | bytes 18874372
  5.8 8.8 %slice-start = ((s8[6291456]{0:T(1024)(128)(4,1)}), s8[4194304]{0:T(1024)(128)(4,1)S(1)}, s32[]{:S(2)}) async-start(s8[6291456]{0:T(1024)(128)(4,1)} %bitcast.23), calls=%async_computation | async-start | bytes 8388608
  6.9 7.6 %copy-start.3 = (bf16[1,16,4096]{2,1,0:T(8,128)(2,1)S(1)}, bf16[1,16,4096]{2,1,0:T(8,128)(2,1)}, u32[]{:S(2)}) copy-start(bf16[1,16,4096]{2,1,0:T(8,128)(2,1)} %param.7) | copy-start | bytes 393220
  6.9 7.7 %slice-start.1 = ((s8[6291456]{0:T(1024)(128)(4,1)}), s8[2097152]{0:T(1024)(128)(4,1)S(1)}, s32[]{:S(2)}) async-start(s8[6291456]{0:T(1024)(128)(4,1)} %bitcast.23), calls=%async_computation.1 | async-start | bytes 4194304
  7.0 9.4 %collective-permute-start = (bf16[16,4224]{1,0:T(8,128)(2,1)S(1)}, bf16[16,4224]{1,0:T(8,128)(2,1)S(1)}, u32[]{:S(2)}, u32[]{:S(2)}) collective-permute-start(bf16[16,4224]{1,0:T(8,128)(2,1)S(1)} %shard_map.86), channel_id=1, source_target_pairs={{0,2},{1,3},{2,0},{3,1},{4,6},{5,7},{6,4},{7,5},{8,10},{9,11},{10,... | collective-permute-start | bytes 405512 | tf_op jit(solution)/shard_map/ppermute | solution.py:24
  9.0 8.4 %collective-permute-start.1 = (bf16[16,4224]{1,0:T(8,128)(2,1)S(1)}, bf16[16,4224]{1,0:T(8,128)(2,1)S(1)}, u32[]{:S(2)}, u32[]{:S(2)}) collective-permute-start(bf16[16,4224]{1,0:T(8,128)(2,1)S(1)} %shard_map.86), channel_id=1, source_target_pairs={{0,4},{1,5},{2,6},{3,7},{4,0},{5,1},{6,2},{7,3},{8,12},{9,13},{10,... | collective-permute-start | bytes 405512 | tf_op jit(solution)/shard_map/ppermute | solution.py:24
  10.5 6.9 %collective-permute-start.2 = (bf16[16,4224]{1,0:T(8,128)(2,1)S(1)}, bf16[16,4224]{1,0:T(8,128)(2,1)S(1)}, u32[]{:S(2)}, u32[]{:S(2)}) collective-permute-start(bf16[16,4224]{1,0:T(8,128)(2,1)S(1)} %shard_map.86), channel_id=1, source_target_pairs={{0,6},{1,7},{2,4},{3,5},{4,2},{5,3},{6,0},{7,1},{8,14},{9,15},{10,... | collective-permute-start | bytes 405512 | tf_op jit(solution)/shard_map/ppermute | solution.py:24
  14.6 3.0 %collective-permute-start.7 = (bf16[64,4096]{1,0:T(8,128)(2,1)S(1)}, bf16[64,4096]{1,0:T(8,128)(2,1)S(1)}, u32[]{:S(2)}, u32[]{:S(2)}) collective-permute-start(bf16[64,4096]{1,0:T(8,128)(2,1)S(1)} %constant_dynamic-update-slice_fusion.4.near_ref), channel_id=1, source_target_pairs={{0,1},{1,0},{2,3},{3,2},{4,5},{5,4},{6,7},{7,6},{8,9},{9,8},{10,11... | collective-permute-start | bytes 1572872 | tf_op jit(solution)/shard_map/ppermute | solution.py:24
  17.5 2.0 %collective-permute-start.4 = (bf16[64,4224]{1,0:T(8,128)(2,1)S(1)}, bf16[64,4224]{1,0:T(8,128)(2,1)S(1)}, u32[]{:S(2)}, u32[]{:S(2)}) collective-permute-start(bf16[64,4224]{1,0:T(8,128)(2,1)S(1)} %constant_dynamic-update-slice_fusion.near_ref), channel_id=1, source_target_pairs={{0,1},{1,0},{2,3},{3,2},{4,5},{5,4},{6,7},{7,6},{8,9},{9,8},{10,11... | collective-permute-start | bytes 1622024 | tf_op jit(solution)/shard_map/ppermute | solution.py:24
  21.7 16.2 %copy-start.4 = (s32[1,16,2]{1,2,0:T(2,128)S(1)}, s32[1,16,2]{1,2,0:T(2,128)}, u32[]{:S(2)}) copy-start(s32[1,16,2]{1,2,0:T(2,128)} %param.9) | copy-start | bytes 388
  21.7 1.6 %collective-permute-start.13 = (bf16[64,2048]{1,0:T(8,128)(2,1)S(1)}, bf16[64,2048]{1,0:T(8,128)(2,1)S(1)}, u32[]{:S(2)}, u32[]{:S(2)}) collective-permute-start(bf16[64,2048]{1,0:T(8,128)(2,1)S(1)} %get-tuple-element.39), channel_id=1, source_target_pairs={{0,1},{1,0},{2,3},{3,2},{4,5},{5,4},{6,7},{7,6},{8,9},{9,8},{10,11... | collective-permute-start | bytes 786440 | tf_op jit(solution)/shard_map/ppermute | solution.py:24
  23.1 3.9 %collective-permute-start.8 = (bf16[64,2176]{1,0:T(8,128)(2,1)S(1)}, bf16[64,2176]{1,0:T(8,128)(2,1)S(1)}, u32[]{:S(2)}, u32[]{:S(2)}) collective-permute-start(bf16[64,2176]{1,0:T(8,128)(2,1)S(1)} %get-tuple-element.37), channel_id=1, source_target_pairs={{0,1},{1,0},{2,3},{3,2},{4,5},{5,4},{6,7},{7,6},{8,9},{9,8},{10,11... | collective-permute-start | bytes 835592 | tf_op jit(solution)/shard_map/ppermute | solution.py:24
  23.4 6.4 %collective-permute-start.14 = (bf16[16,2048]{1,0:T(8,128)(2,1)S(1)}, bf16[16,2048]{1,0:T(8,128)(2,1)S(1)}, u32[]{:S(2)}, u32[]{:S(2)}) collective-permute-start(bf16[16,2048]{1,0:T(8,128)(2,1)S(1)} %get-tuple-element.43), channel_id=1, source_target_pairs={{0,2},{1,3},{2,0},{3,1},{4,6},{5,7},{6,4},{7,5},{8,10},{9,11},{10,... | collective-permute-start | bytes 196616 | tf_op jit(solution)/shard_map/ppermute | solution.py:24
  24.7 6.0 %collective-permute-start.15 = (bf16[16,2048]{1,0:T(8,128)(2,1)S(1)}, bf16[16,2048]{1,0:T(8,128)(2,1)S(1)}, u32[]{:S(2)}, u32[]{:S(2)}) collective-permute-start(bf16[16,2048]{1,0:T(8,128)(2,1)S(1)} %get-tuple-element.45), channel_id=1, source_target_pairs={{0,4},{1,5},{2,6},{3,7},{4,0},{5,1},{6,2},{7,3},{8,12},{9,13},{10,... | collective-permute-start | bytes 196616 | tf_op jit(solution)/shard_map/ppermute | solution.py:24
  25.7 5.3 %collective-permute-start.16 = (bf16[16,2048]{1,0:T(8,128)(2,1)S(1)}, bf16[16,2048]{1,0:T(8,128)(2,1)S(1)}, u32[]{:S(2)}, u32[]{:S(2)}) collective-permute-start(bf16[16,2048]{1,0:T(8,128)(2,1)S(1)} %get-tuple-element.44), channel_id=1, source_target_pairs={{0,6},{1,7},{2,4},{3,5},{4,2},{5,3},{6,0},{7,1},{8,14},{9,15},{10,... | collective-permute-start | bytes 196616 | tf_op jit(solution)/shard_map/ppermute | solution.py:24
  27.1 7.6 %collective-permute-start.10 = (bf16[16,2176]{1,0:T(8,128)(2,1)S(1)}, bf16[16,2176]{1,0:T(8,128)(2,1)S(1)}, u32[]{:S(2)}, u32[]{:S(2)}) collective-permute-start(bf16[16,2176]{1,0:T(8,128)(2,1)S(1)} %get-tuple-element.42), channel_id=1, source_target_pairs={{0,4},{1,5},{2,6},{3,7},{4,0},{5,1},{6,2},{7,3},{8,12},{9,13},{10,... | collective-permute-start | bytes 208904 | tf_op jit(solution)/shard_map/ppermute | solution.py:24
  28.7 6.0 %collective-permute-start.11 = (bf16[16,2176]{1,0:T(8,128)(2,1)S(1)}, bf16[16,2176]{1,0:T(8,128)(2,1)S(1)}, u32[]{:S(2)}, u32[]{:S(2)}) collective-permute-start(bf16[16,2176]{1,0:T(8,128)(2,1)S(1)} %get-tuple-element.41), channel_id=1, source_target_pairs={{0,6},{1,7},{2,4},{3,5},{4,2},{5,3},{6,0},{7,1},{8,14},{9,15},{10,... | collective-permute-start | bytes 208904 | tf_op jit(solution)/shard_map/ppermute | solution.py:24
  29.8 4.8 %collective-permute-start.9 = (bf16[16,2176]{1,0:T(8,128)(2,1)S(1)}, bf16[16,2176]{1,0:T(8,128)(2,1)S(1)}, u32[]{:S(2)}, u32[]{:S(2)}) collective-permute-start(bf16[16,2176]{1,0:T(8,128)(2,1)S(1)} %get-tuple-element.40), channel_id=1, source_target_pairs={{0,2},{1,3},{2,0},{3,1},{4,6},{5,7},{6,4},{7,5},{8,10},{9,11},{10,... | collective-permute-start | bytes 208904 | tf_op jit(solution)/shard_map/ppermute | solution.py:24
  31.0 7.6 %collective-permute-start.17 = (bf16[16,2048]{1,0:T(8,128)(2,1)S(1)}, bf16[16,2048]{1,0:T(8,128)(2,1)S(1)}, u32[]{:S(2)}, u32[]{:S(2)}) collective-permute-start(bf16[16,2048]{1,0:T(8,128)(2,1)S(1)} %add_convert_fusion.2), channel_id=1, source_target_pairs={{0,24},{8,0},{16,8},{24,16},{1,25},{9,1},{17,9},{25,17},{2,26},{10... | collective-permute-start | bytes 196616 | tf_op jit(solution)/shard_map/ppermute | solution.py:19
  34.8 5.0 %collective-permute-start.12 = (bf16[16,2048]{1,0:T(8,128)(2,1)S(1)}, bf16[16,2048]{1,0:T(8,128)(2,1)S(1)}, u32[]{:S(2)}, u32[]{:S(2)}) collective-permute-start(bf16[16,2048]{1,0:T(8,128)(2,1)S(1)} %slice.72), channel_id=1, source_target_pairs={{0,24},{8,0},{16,8},{24,16},{1,25},{9,1},{17,9},{25,17},{2,26},{10... | collective-permute-start | bytes 196616 | tf_op jit(solution)/shard_map/ppermute | solution.py:19

commit v6 on v5

--- a/solution.py
+++ b/solution.py
@@ -186,7 +186,7 @@
             compiler_params=params(4),
         )(after, gate_mat, up_mat)
     )
-    down_flipped = resident(flip(after, down_mat))
+    down_flipped = resident(flip(resident(parts_dy[1]), down_mat))
     parts_x, pair = lax.optimization_barrier((parts_x, pair))
     near_x = jnp.concatenate(parts_x, axis=0)
     far_x = swapped(near_x, 1)

time: 40.6 us -> 40.6 us (level)
  no operation moved by 1% of the time
where the time goes in v6:
time: 40.6 us; the launch traced here: 40.5 us
  starting transfers between devices  23.4 us (58%)
  Pallas kernels  11 us (27%)
  waiting for transfers between devices  2.66 us (7%)
  other arithmetic  1.66 us (4%)
  between operations  0.89 us (2%)
  local copies, waits for them, and re-layouts  0.83 us (2%)
    ppermute x16, starting transfers between devices, swapped(): return lax.ppermute(array, 'expert', [(i, i ^ bits) for i in range(peers)])  16.7 us
    ppermute x2, starting transfers between devices, shifted(): lax.ppermute(array, axis, [(i, (i + by) % peers) for i in range(peers)])  6.74 us
    pallas_call x1, Pallas kernels, on_device(): pl.pallas_call(flip_pair_kernel, out_shape=jax.ShapeDtypeStruct((width, 2...  3.29 us
    pallas_call x2, Pallas kernels, on_device(): pl.pallas_call(functools.partial(third_kernel, chunk * span, span), out_s...  1.98 us
    pallas_call x1, Pallas kernels, on_device(): pl.pallas_call(first_kernel, out_shape=(pre, pre), in_specs=[VMEM] * 3, o...  1.8 us
    pallas_call x1, Pallas kernels, on_device(): down_flipped = resident(flip(resident(parts_dy[1]), down_mat))  1.67 us
    ppermute x16, waiting for transfers between devices, swapped(): return lax.ppermute(array, 'expert', [(i, i ^ bits) for i in range(peers)])  1.47 us
    ppermute x2, waiting for transfers between devices, shifted(): lax.ppermute(array, axis, [(i, (i + by) % peers) for i in range(peers)])  1.18 us
  transfers between devices with their start and end apart: 18, of which 4 were waited for; matrix products, arithmetic and copies ran while one was open for 3% of the time, Pallas kernels for 22%

profile of v6, /device:TPU:0, one launch (start us, length us, event | category | flops | bytes accessed | tf_op | source)
XLA Modules:
  0.0 40.5 jit_solution(13735937475954069826)
XLA Ops:
  0.6 3.0 %collective-permute-start.4 = (bf16[16,4096]{1,0:T(8,128)(2,1)}, bf16[16,4096]{1,0:T(8,128)(2,1)S(1)}, u32[]{:S(2)}, u32[]{:S(2)}) collective-permute-start(bf16[16,4096]{1,0:T(8,128)(2,1)} %bitcast.28), channel_id=1, source_target_pairs={{0,2},{1,3},{2,0},{3,1},{4,6},{5,7},{6,4},{7,5},{8,10},{9,11},{10,... | collective-permute-start | bytes 393224 | tf_op jit(solution)/shard_map/ppermute | solution.py:24
  3.6 1.5 %collective-permute-start.5 = (bf16[16,4096]{1,0:T(8,128)(2,1)}, bf16[16,4096]{1,0:T(8,128)(2,1)S(1)}, u32[]{:S(2)}, u32[]{:S(2)}) collective-permute-start(bf16[16,4096]{1,0:T(8,128)(2,1)} %bitcast.29), channel_id=1, source_target_pairs={{0,4},{1,5},{2,6},{3,7},{4,0},{5,1},{6,2},{7,3},{8,12},{9,13},{10,... | collective-permute-start | bytes 393224 | tf_op jit(solution)/shard_map/ppermute | solution.py:24
  5.2 0.7 %copy-done.2 = bf16[1,16,2]{1,2,0:T(2,128)(2,1)S(1)} copy-done((bf16[1,16,2]{1,2,0:T(2,128)(2,1)S(1)}, bf16[1,16,2]{1,2,0:T(2,128)(2,1)}, u32[]{:S(2)}) %copy-start.2) | copy-done | bytes 88
  5.8 1.1 %shard_map.86 = bf16[16,4224]{1,0:T(8,128)(2,1)S(1)} custom-call(bf16[16,4096]{1,0:T(8,128)(2,1)} %bitcast.27, s32[2,16]{1,0:T(2,128)} %bitcast.32, bf16[2,16]{1,0:T(2,128)(2,1)S(1)} %bitcast.26, bf16[768,4096]{1,0:T(8,128)(2,1)} %bitcast.14, bf16[768,4096]{1,0:T(8,128)(2,1)} %bitcast.18, bf16[768,4096]{1,0:T(8,128)(2,1)} %bitcast.22), custom_call_target="tpu_custom_call" | custom-call | bytes 37748736 | tf_op jit(solution)/shard_map/pallas_call | solution.py:154
  7.0 2.0 %collective-permute-start = (bf16[16,4224]{1,0:T(8,128)(2,1)S(1)}, bf16[16,4224]{1,0:T(8,128)(2,1)S(1)}, u32[]{:S(2)}, u32[]{:S(2)}) collective-permute-start(bf16[16,4224]{1,0:T(8,128)(2,1)S(1)} %shard_map.86), channel_id=1, source_target_pairs={{0,2},{1,3},{2,0},{3,1},{4,6},{5,7},{6,4},{7,5},{8,10},{9,11},{10,... | collective-permute-start | bytes 405512 | tf_op jit(solution)/shard_map/ppermute | solution.py:24
  9.0 1.5 %collective-permute-start.1 = (bf16[16,4224]{1,0:T(8,128)(2,1)S(1)}, bf16[16,4224]{1,0:T(8,128)(2,1)S(1)}, u32[]{:S(2)}, u32[]{:S(2)}) collective-permute-start(bf16[16,4224]{1,0:T(8,128)(2,1)S(1)} %shard_map.86), channel_id=1, source_target_pairs={{0,4},{1,5},{2,6},{3,7},{4,0},{5,1},{6,2},{7,3},{8,12},{9,13},{10,... | collective-permute-start | bytes 405512 | tf_op jit(solution)/shard_map/ppermute | solution.py:24
  10.5 0.7 %collective-permute-start.2 = (bf16[16,4224]{1,0:T(8,128)(2,1)S(1)}, bf16[16,4224]{1,0:T(8,128)(2,1)S(1)}, u32[]{:S(2)}, u32[]{:S(2)}) collective-permute-start(bf16[16,4224]{1,0:T(8,128)(2,1)S(1)} %shard_map.86), channel_id=1, source_target_pairs={{0,6},{1,7},{2,4},{3,5},{4,2},{5,3},{6,0},{7,1},{8,14},{9,15},{10,... | collective-permute-start | bytes 405512 | tf_op jit(solution)/shard_map/ppermute | solution.py:24
  11.2 3.3 %shard_map.88.pair_ref = bf16[4096,1536]{1,0:T(8,128)(2,1)S(1)} custom-call(bf16[16,4096]{1,0:T(8,128)(2,1)S(1)} %collective-permute-done.4.after_ref, bf16[768,4096]{1,0:T(8,128)(2,1)S(1)} %bitcast.15, bf16[768,4096]{1,0:T(8,128)(2,1)S(1)} %bitcast.19), custom_call_target="tpu_custom_call" | custom-call | tf_op jit(solution)/shard_map/pallas_call | solution.py:181
  14.6 0.1 collective-permute-start.7
  14.7 1.7 %shard_map.87.down_ref = bf16[4096,768]{1,0:T(8,128)(2,1)S(1)} custom-call(bf16[16,4224]{1,0:T(8,128)(2,1)S(1)} %collective-permute-done.after_ref, bf16[768,4096]{1,0:T(8,128)(2,1)S(1)} %bitcast.25), custom_call_target="tpu_custom_call" | custom-call | tf_op jit(solution)/shard_map/pallas_call | solution.py:189
  16.4 1.0 %collective-permute-done.1 = bf16[16,4224]{1,0:T(8,128)(2,1)S(1)} collective-permute-done((bf16[16,4224]{1,0:T(8,128)(2,1)S(1)}, bf16[16,4224]{1,0:T(8,128)(2,1)S(1)}, u32[]{:S(2)}, u32[]{:S(2)}) %collective-permute-start.1) | collective-permute-done | bytes 135200 | tf_op jit(solution)/shard_map/ppermute | solution.py:24
  17.5 0.1 collective-permute-start.3
  17.6 1.8 %shard_map.89 = (f32[128,768]{1,0:T(8,128)S(1)}, f32[128,768]{1,0:T(8,128)S(1)}) custom-call(bf16[64,4096]{1,0:T(8,128)(2,1)S(1)} %constant_dynamic-update-slice_fusion.4.near_ref, bf16[64,4096]{1,0:T(8,128)(2,1)S(1)} %collective-permute-done.7.far_ref, bf16[4096,1536]{1,0:T(8,128)(2,1)S(1)} %shard_map.88.pair_ref), custom_call_target="tpu_custom_call" | custom-call | flops 1610612736 | tf_op jit(solution)/shard_map/pallas_call | solution.py:194
  19.4 0.1 collective-permute-done.3.far_ref
  19.5 1.2 %shard_map.90 = (bf16[128,768]{1,0:T(8,128)(2,1)S(1)}, bf16[128,768]{1,0:T(8,128)(2,1)S(1)}, bf16[128,128]{1,0:T(8,128)(2,1)S(1)}) custom-call(bf16[64,4224]{1,0:T(8,128)(2,1)S(1)} %constant_dynamic-update-slice_fusion.near_ref, bf16[64,4224]{1,0:T(8,128)(2,1)S(1)} %collective-permute-done.3.far_ref, bf16[4096,768]{1,0:T(8,128)(2,1)S(1)} %shard_map.87.down_ref, ...), custom_call_target="tpu_custom_call" | custom-call | tf_op jit(solution)/shard_map/pallas_call | solution.py:208
  20.7 1.0 %shard_map.92 = (bf16[64,2048]{1,0:T(8,128)(2,1)S(1)}, bf16[64,2048]{1,0:T(8,128)(2,1)S(1)}) custom-call(bf16[128,768]{1,0:T(8,128)(2,1)S(1)} %get-tuple-element.33.grad_gate_ref, bf16[128,768]{1,0:T(8,128)(2,1)S(1)} %get-tuple-element.34.grad_up_ref, bf16[768,4096]{1,0:T(8,128)(2,1)S(1)} %bitcast.16, bf16[768,4096]{1,0:T(8,128)(2,1)S(1)} %bitcast.20, ...), custom_call_target="tpu_custom_call" | custom-call | tf_op jit(solution)/shard_map/pallas_call | solution.py:221
  21.7 0.5 %collective-permute-start.13 = (bf16[64,2048]{1,0:T(8,128)(2,1)S(1)}, bf16[64,2048]{1,0:T(8,128)(2,1)S(1)}, u32[]{:S(2)}, u32[]{:S(2)}) collective-permute-start(bf16[64,2048]{1,0:T(8,128)(2,1)S(1)} %get-tuple-element.39), channel_id=1, source_target_pairs={{0,1},{1,0},{2,3},{3,2},{4,5},{5,4},{6,7},{7,6},{8,9},{9,8},{10,11... | collective-permute-start | bytes 786440 | tf_op jit(solution)/shard_map/ppermute | solution.py:24
  22.1 1.0 %shard_map.91 = (bf16[64,2176]{1,0:T(8,128)(2,1)S(1)}, bf16[64,2176]{1,0:T(8,128)(2,1)S(1)}) custom-call(bf16[128,768]{1,0:T(8,128)(2,1)S(1)} %get-tuple-element.33.grad_gate_ref, bf16[128,768]{1,0:T(8,128)(2,1)S(1)} %get-tuple-element.34.grad_up_ref, bf16[768,4096]{1,0:T(8,128)(2,1)S(1)} %bitcast.17, bf16[768,4096]{1,0:T(8,128)(2,1)S(1)} %bitcast.21, ...), custom_call_target="tpu_custom_call" | custom-call | tf_op jit(solution)/shard_map/pallas_call | solution.py:221
  23.1 0.2 collective-permute-start.8
  23.4 1.3 %collective-permute-start.14 = (bf16[16,2048]{1,0:T(8,128)(2,1)S(1)}, bf16[16,2048]{1,0:T(8,128)(2,1)S(1)}, u32[]{:S(2)}, u32[]{:S(2)}) collective-permute-start(bf16[16,2048]{1,0:T(8,128)(2,1)S(1)} %get-tuple-element.43), channel_id=1, source_target_pairs={{0,2},{1,3},{2,0},{3,1},{4,6},{5,7},{6,4},{7,5},{8,10},{9,11},{10,... | collective-permute-start | bytes 196616 | tf_op jit(solution)/shard_map/ppermute | solution.py:24
  24.7 1.0 %collective-permute-start.15 = (bf16[16,2048]{1,0:T(8,128)(2,1)S(1)}, bf16[16,2048]{1,0:T(8,128)(2,1)S(1)}, u32[]{:S(2)}, u32[]{:S(2)}) collective-permute-start(bf16[16,2048]{1,0:T(8,128)(2,1)S(1)} %get-tuple-element.45), channel_id=1, source_target_pairs={{0,4},{1,5},{2,6},{3,7},{4,0},{5,1},{6,2},{7,3},{8,12},{9,13},{10,... | collective-permute-start | bytes 196616 | tf_op jit(solution)/shard_map/ppermute | solution.py:24
  25.7 1.3 %collective-permute-start.16 = (bf16[16,2048]{1,0:T(8,128)(2,1)S(1)}, bf16[16,2048]{1,0:T(8,128)(2,1)S(1)}, u32[]{:S(2)}, u32[]{:S(2)}) collective-permute-start(bf16[16,2048]{1,0:T(8,128)(2,1)S(1)} %get-tuple-element.44), channel_id=1, source_target_pairs={{0,6},{1,7},{2,4},{3,5},{4,2},{5,3},{6,0},{7,1},{8,14},{9,15},{10,... | collective-permute-start | bytes 196616 | tf_op jit(solution)/shard_map/ppermute | solution.py:24
  27.1 1.6 %collective-permute-start.10 = (bf16[16,2176]{1,0:T(8,128)(2,1)S(1)}, bf16[16,2176]{1,0:T(8,128)(2,1)S(1)}, u32[]{:S(2)}, u32[]{:S(2)}) collective-permute-start(bf16[16,2176]{1,0:T(8,128)(2,1)S(1)} %get-tuple-element.42), channel_id=1, source_target_pairs={{0,4},{1,5},{2,6},{3,7},{4,0},{5,1},{6,2},{7,3},{8,12},{9,13},{10,... | collective-permute-start | bytes 208904 | tf_op jit(solution)/shard_map/ppermute | solution.py:24
  28.7 1.1 %collective-permute-start.11 = (bf16[16,2176]{1,0:T(8,128)(2,1)S(1)}, bf16[16,2176]{1,0:T(8,128)(2,1)S(1)}, u32[]{:S(2)}, u32[]{:S(2)}) collective-permute-start(bf16[16,2176]{1,0:T(8,128)(2,1)S(1)} %get-tuple-element.41), channel_id=1, source_target_pairs={{0,6},{1,7},{2,4},{3,5},{4,2},{5,3},{6,0},{7,1},{8,14},{9,15},{10,... | collective-permute-start | bytes 208904 | tf_op jit(solution)/shard_map/ppermute | solution.py:24
  29.8 0.8 %collective-permute-start.9 = (bf16[16,2176]{1,0:T(8,128)(2,1)S(1)}, bf16[16,2176]{1,0:T(8,128)(2,1)S(1)}, u32[]{:S(2)}, u32[]{:S(2)}) collective-permute-start(bf16[16,2176]{1,0:T(8,128)(2,1)S(1)} %get-tuple-element.40), channel_id=1, source_target_pairs={{0,2},{1,3},{2,0},{3,1},{4,6},{5,7},{6,4},{7,5},{8,10},{9,11},{10,... | collective-permute-start | bytes 208904 | tf_op jit(solution)/shard_map/ppermute | solution.py:24
  30.7 0.3 collective-permute-done.16
  31.0 3.7 %collective-permute-start.17 = (bf16[16,2048]{1,0:T(8,128)(2,1)S(1)}, bf16[16,2048]{1,0:T(8,128)(2,1)S(1)}, u32[]{:S(2)}, u32[]{:S(2)}) collective-permute-start(bf16[16,2048]{1,0:T(8,128)(2,1)S(1)} %add_convert_fusion.2), channel_id=1, source_target_pairs={{0,24},{8,0},{16,8},{24,16},{1,25},{9,1},{17,9},{25,17},{2,26},{10... | collective-permute-start | bytes 196616 | tf_op jit(solution)/shard_map/ppermute | solution.py:19
  34.7 0.1 slice_add_fusion
  34.8 3.1 %collective-permute-start.12 = (bf16[16,2048]{1,0:T(8,128)(2,1)S(1)}, bf16[16,2048]{1,0:T(8,128)(2,1)S(1)}, u32[]{:S(2)}, u32[]{:S(2)}) collective-permute-start(bf16[16,2048]{1,0:T(8,128)(2,1)S(1)} %slice.72), channel_id=1, source_target_pairs={{0,24},{8,0},{16,8},{24,16},{1,25},{9,1},{17,9},{25,17},{2,26},{10... | collective-permute-start | bytes 196616 | tf_op jit(solution)/shard_map/ppermute | solution.py:19
  37.9 0.7 %select_reduce_fusion = f32[16,2]{0,1:T(2,128)} fusion(f32[16,64]{1,0:T(8,128)S(1)} %slice_add_fusion, s32[16,2]{0,1:T(2,128)S(1)} %bitcast.33), kind=kLoop, calls=%fused_computation.14 | loop fusion | flops 6112 | bytes 4352 | tf_op jit(solution)/shard_map/reduce_sum | solution.py:240
  38.6 1.2 %collective-permute-done.12 = bf16[16,2048]{1,0:T(8,128)(2,1)S(1)} collective-permute-done((bf16[16,2048]{1,0:T(8,128)(2,1)S(1)}, bf16[16,2048]{1,0:T(8,128)(2,1)S(1)}, u32[]{:S(2)}, u32[]{:S(2)}) %collective-permute-start.12) | collective-permute-done | bytes 65568 | tf_op jit(solution)/shard_map/ppermute | solution.py:19
  39.8 0.7 %maximum_bitcast_fusion = bf16[1,16,4096]{2,1,0:T(8,128)(2,1)} fusion(bf16[16,2048]{1,0:T(8,128)(2,1)S(1)} %collective-permute-done.17, bf16[16,2048]{1,0:T(8,128)(2,1)S(1)} %collective-permute-done.12), kind=kLoop, calls=%fused_computation.4 | loop fusion | flops 262144 | bytes 262144 | tf_op jit(solution)/shard_map/broadcast_in_dim | solution.py:241
  (44 shorter events, 0.4 us)
Async XLA Ops:
  0.6 9.9 %collective-permute-start.4 = (bf16[16,4096]{1,0:T(8,128)(2,1)}, bf16[16,4096]{1,0:T(8,128)(2,1)S(1)}, u32[]{:S(2)}, u32[]{:S(2)}) collective-permute-start(bf16[16,4096]{1,0:T(8,128)(2,1)} %bitcast.28), channel_id=1, source_target_pairs={{0,2},{1,3},{2,0},{3,1},{4,6},{5,7},{6,4},{7,5},{8,10},{9,11},{10,... | collective-permute-start | bytes 393224 | tf_op jit(solution)/shard_map/ppermute | solution.py:24
  3.6 10.9 %collective-permute-start.5 = (bf16[16,4096]{1,0:T(8,128)(2,1)}, bf16[16,4096]{1,0:T(8,128)(2,1)S(1)}, u32[]{:S(2)}, u32[]{:S(2)}) collective-permute-start(bf16[16,4096]{1,0:T(8,128)(2,1)} %bitcast.29), channel_id=1, source_target_pairs={{0,4},{1,5},{2,6},{3,7},{4,0},{5,1},{6,2},{7,3},{8,12},{9,13},{10,... | collective-permute-start | bytes 393224 | tf_op jit(solution)/shard_map/ppermute | solution.py:24
  5.2 9.3 %collective-permute-start.6 = (bf16[16,4096]{1,0:T(8,128)(2,1)}, bf16[16,4096]{1,0:T(8,128)(2,1)S(1)}, u32[]{:S(2)}, u32[]{:S(2)}) collective-permute-start(bf16[16,4096]{1,0:T(8,128)(2,1)} %bitcast.30), channel_id=1, source_target_pairs={{0,6},{1,7},{2,4},{3,5},{4,2},{5,3},{6,0},{7,1},{8,14},{9,15},{10,... | collective-permute-start | bytes 393224 | tf_op jit(solution)/shard_map/ppermute | solution.py:24
  5.2 0.7 %copy-start.2 = (bf16[1,16,2]{1,2,0:T(2,128)(2,1)S(1)}, bf16[1,16,2]{1,2,0:T(2,128)(2,1)}, u32[]{:S(2)}) copy-start(bf16[1,16,2]{1,2,0:T(2,128)(2,1)} %param.10) | copy-start | bytes 196
  5.8 5.4 %copy-start = (bf16[1,768,4096]{2,1,0:T(8,128)(2,1)S(1)}, bf16[1,768,4096]{2,1,0:T(8,128)(2,1)}, u32[]{:S(2)}) copy-start(bf16[1,768,4096]{2,1,0:T(8,128)(2,1)} %param.11) | copy-start | bytes 18874372
  5.8 5.4 %copy-start.1 = (bf16[1,768,4096]{2,1,0:T(8,128)(2,1)S(1)}, bf16[1,768,4096]{2,1,0:T(8,128)(2,1)}, u32[]{:S(2)}) copy-start(bf16[1,768,4096]{2,1,0:T(8,128)(2,1)} %param.12) | copy-start | bytes 18874372
  5.8 8.8 %slice-start = ((s8[6291456]{0:T(1024)(128)(4,1)}), s8[4194304]{0:T(1024)(128)(4,1)S(1)}, s32[]{:S(2)}) async-start(s8[6291456]{0:T(1024)(128)(4,1)} %bitcast.23), calls=%async_computation | async-start | bytes 8388608
  6.9 7.6 %copy-start.3 = (bf16[1,16,4096]{2,1,0:T(8,128)(2,1)S(1)}, bf16[1,16,4096]{2,1,0:T(8,128)(2,1)}, u32[]{:S(2)}) copy-start(bf16[1,16,4096]{2,1,0:T(8,128)(2,1)} %param.7) | copy-start | bytes 393220
  6.9 7.7 %slice-start.1 = ((s8[6291456]{0:T(1024)(128)(4,1)}), s8[2097152]{0:T(1024)(128)(4,1)S(1)}, s32[]{:S(2)}) async-start(s8[6291456]{0:T(1024)(128)(4,1)} %bitcast.23), calls=%async_computation.1 | async-start | bytes 4194304
  7.0 7.7 %collective-permute-start = (bf16[16,4224]{1,0:T(8,128)(2,1)S(1)}, bf16[16,4224]{1,0:T(8,128)(2,1)S(1)}, u32[]{:S(2)}, u32[]{:S(2)}) collective-permute-start(bf16[16,4224]{1,0:T(8,128)(2,1)S(1)} %shard_map.86), channel_id=1, source_target_pairs={{0,2},{1,3},{2,0},{3,1},{4,6},{5,7},{6,4},{7,5},{8,10},{9,11},{10,... | collective-permute-start | bytes 405512 | tf_op jit(solution)/shard_map/ppermute | solution.py:24
  9.0 8.4 %collective-permute-start.1 = (bf16[16,4224]{1,0:T(8,128)(2,1)S(1)}, bf16[16,4224]{1,0:T(8,128)(2,1)S(1)}, u32[]{:S(2)}, u32[]{:S(2)}) collective-permute-start(bf16[16,4224]{1,0:T(8,128)(2,1)S(1)} %shard_map.86), channel_id=1, source_target_pairs={{0,4},{1,5},{2,6},{3,7},{4,0},{5,1},{6,2},{7,3},{8,12},{9,13},{10,... | collective-permute-start | bytes 405512 | tf_op jit(solution)/shard_map/ppermute | solution.py:24
  10.5 6.9 %collective-permute-start.2 = (bf16[16,4224]{1,0:T(8,128)(2,1)S(1)}, bf16[16,4224]{1,0:T(8,128)(2,1)S(1)}, u32[]{:S(2)}, u32[]{:S(2)}) collective-permute-start(bf16[16,4224]{1,0:T(8,128)(2,1)S(1)} %shard_map.86), channel_id=1, source_target_pairs={{0,6},{1,7},{2,4},{3,5},{4,2},{5,3},{6,0},{7,1},{8,14},{9,15},{10,... | collective-permute-start | bytes 405512 | tf_op jit(solution)/shard_map/ppermute | solution.py:24
  14.6 3.0 %collective-permute-start.7 = (bf16[64,4096]{1,0:T(8,128)(2,1)S(1)}, bf16[64,4096]{1,0:T(8,128)(2,1)S(1)}, u32[]{:S(2)}, u32[]{:S(2)}) collective-permute-start(bf16[64,4096]{1,0:T(8,128)(2,1)S(1)} %constant_dynamic-update-slice_fusion.4.near_ref), channel_id=1, source_target_pairs={{0,1},{1,0},{2,3},{3,2},{4,5},{5,4},{6,7},{7,6},{8,9},{9,8},{10,11... | collective-permute-start | bytes 1572872 | tf_op jit(solution)/shard_map/ppermute | solution.py:24
  17.5 2.0 %collective-permute-start.3 = (bf16[64,4224]{1,0:T(8,128)(2,1)S(1)}, bf16[64,4224]{1,0:T(8,128)(2,1)S(1)}, u32[]{:S(2)}, u32[]{:S(2)}) collective-permute-start(bf16[64,4224]{1,0:T(8,128)(2,1)S(1)} %constant_dynamic-update-slice_fusion.near_ref), channel_id=1, source_target_pairs={{0,1},{1,0},{2,3},{3,2},{4,5},{5,4},{6,7},{7,6},{8,9},{9,8},{10,11... | collective-permute-start | bytes 1622024 | tf_op jit(solution)/shard_map/ppermute | solution.py:24
  21.7 16.2 %copy-start.4 = (s32[1,16,2]{1,2,0:T(2,128)S(1)}, s32[1,16,2]{1,2,0:T(2,128)}, u32[]{:S(2)}) copy-start(s32[1,16,2]{1,2,0:T(2,128)} %param.9) | copy-start | bytes 388
  21.7 1.6 %collective-permute-start.13 = (bf16[64,2048]{1,0:T(8,128)(2,1)S(1)}, bf16[64,2048]{1,0:T(8,128)(2,1)S(1)}, u32[]{:S(2)}, u32[]{:S(2)}) collective-permute-start(bf16[64,2048]{1,0:T(8,128)(2,1)S(1)} %get-tuple-element.39), channel_id=1, source_target_pairs={{0,1},{1,0},{2,3},{3,2},{4,5},{5,4},{6,7},{7,6},{8,9},{9,8},{10,11... | collective-permute-start | bytes 786440 | tf_op jit(solution)/shard_map/ppermute | solution.py:24
  23.1 3.9 %collective-permute-start.8 = (bf16[64,2176]{1,0:T(8,128)(2,1)S(1)}, bf16[64,2176]{1,0:T(8,128)(2,1)S(1)}, u32[]{:S(2)}, u32[]{:S(2)}) collective-permute-start(bf16[64,2176]{1,0:T(8,128)(2,1)S(1)} %get-tuple-element.37), channel_id=1, source_target_pairs={{0,1},{1,0},{2,3},{3,2},{4,5},{5,4},{6,7},{7,6},{8,9},{9,8},{10,11... | collective-permute-start | bytes 835592 | tf_op jit(solution)/shard_map/ppermute | solution.py:24
  23.4 6.4 %collective-permute-start.14 = (bf16[16,2048]{1,0:T(8,128)(2,1)S(1)}, bf16[16,2048]{1,0:T(8,128)(2,1)S(1)}, u32[]{:S(2)}, u32[]{:S(2)}) collective-permute-start(bf16[16,2048]{1,0:T(8,128)(2,1)S(1)} %get-tuple-element.43), channel_id=1, source_target_pairs={{0,2},{1,3},{2,0},{3,1},{4,6},{5,7},{6,4},{7,5},{8,10},{9,11},{10,... | collective-permute-start | bytes 196616 | tf_op jit(solution)/shard_map/ppermute | solution.py:24
  24.7 6.0 %collective-permute-start.15 = (bf16[16,2048]{1,0:T(8,128)(2,1)S(1)}, bf16[16,2048]{1,0:T(8,128)(2,1)S(1)}, u32[]{:S(2)}, u32[]{:S(2)}) collective-permute-start(bf16[16,2048]{1,0:T(8,128)(2,1)S(1)} %get-tuple-element.45), channel_id=1, source_target_pairs={{0,4},{1,5},{2,6},{3,7},{4,0},{5,1},{6,2},{7,3},{8,12},{9,13},{10,... | collective-permute-start | bytes 196616 | tf_op jit(solution)/shard_map/ppermute | solution.py:24
  25.7 5.3 %collective-permute-start.16 = (bf16[16,2048]{1,0:T(8,128)(2,1)S(1)}, bf16[16,2048]{1,0:T(8,128)(2,1)S(1)}, u32[]{:S(2)}, u32[]{:S(2)}) collective-permute-start(bf16[16,2048]{1,0:T(8,128)(2,1)S(1)} %get-tuple-element.44), channel_id=1, source_target_pairs={{0,6},{1,7},{2,4},{3,5},{4,2},{5,3},{6,0},{7,1},{8,14},{9,15},{10,... | collective-permute-start | bytes 196616 | tf_op jit(solution)/shard_map/ppermute | solution.py:24
  27.1 7.6 %collective-permute-start.10 = (bf16[16,2176]{1,0:T(8,128)(2,1)S(1)}, bf16[16,2176]{1,0:T(8,128)(2,1)S(1)}, u32[]{:S(2)}, u32[]{:S(2)}) collective-permute-start(bf16[16,2176]{1,0:T(8,128)(2,1)S(1)} %get-tuple-element.42), channel_id=1, source_target_pairs={{0,4},{1,5},{2,6},{3,7},{4,0},{5,1},{6,2},{7,3},{8,12},{9,13},{10,... | collective-permute-start | bytes 208904 | tf_op jit(solution)/shard_map/ppermute | solution.py:24
  28.7 6.0 %collective-permute-start.11 = (bf16[16,2176]{1,0:T(8,128)(2,1)S(1)}, bf16[16,2176]{1,0:T(8,128)(2,1)S(1)}, u32[]{:S(2)}, u32[]{:S(2)}) collective-permute-start(bf16[16,2176]{1,0:T(8,128)(2,1)S(1)} %get-tuple-element.41), channel_id=1, source_target_pairs={{0,6},{1,7},{2,4},{3,5},{4,2},{5,3},{6,0},{7,1},{8,14},{9,15},{10,... | collective-permute-start | bytes 208904 | tf_op jit(solution)/shard_map/ppermute | solution.py:24
  29.8 4.8 %collective-permute-start.9 = (bf16[16,2176]{1,0:T(8,128)(2,1)S(1)}, bf16[16,2176]{1,0:T(8,128)(2,1)S(1)}, u32[]{:S(2)}, u32[]{:S(2)}) collective-permute-start(bf16[16,2176]{1,0:T(8,128)(2,1)S(1)} %get-tuple-element.40), channel_id=1, source_target_pairs={{0,2},{1,3},{2,0},{3,1},{4,6},{5,7},{6,4},{7,5},{8,10},{9,11},{10,... | collective-permute-start | bytes 208904 | tf_op jit(solution)/shard_map/ppermute | solution.py:24
  31.0 7.6 %collective-permute-start.17 = (bf16[16,2048]{1,0:T(8,128)(2,1)S(1)}, bf16[16,2048]{1,0:T(8,128)(2,1)S(1)}, u32[]{:S(2)}, u32[]{:S(2)}) collective-permute-start(bf16[16,2048]{1,0:T(8,128)(2,1)S(1)} %add_convert_fusion.2), channel_id=1, source_target_pairs={{0,24},{8,0},{16,8},{24,16},{1,25},{9,1},{17,9},{25,17},{2,26},{10... | collective-permute-start | bytes 196616 | tf_op jit(solution)/shard_map/ppermute | solution.py:19
  34.8 5.0 %collective-permute-start.12 = (bf16[16,2048]{1,0:T(8,128)(2,1)S(1)}, bf16[16,2048]{1,0:T(8,128)(2,1)S(1)}, u32[]{:S(2)}, u32[]{:S(2)}) collective-permute-start(bf16[16,2048]{1,0:T(8,128)(2,1)S(1)} %slice.72), channel_id=1, source_target_pairs={{0,24},{8,0},{16,8},{24,16},{1,25},{9,1},{17,9},{25,17},{2,26},{10... | collective-permute-start | bytes 196616 | tf_op jit(solution)/shard_map/ppermute | solution.py:19
